TPU v7x, 32 devices: a whole 2x2x4 slice. The times are simulated.
32 devices in a mesh: row: 8 (over z, x), col: 4 (over y, core).
Axes of the slice: x: 2, y: 2, z: 4, core: 2. Of those that a mesh axis runs over, the one named last changes fastest.
Arguments:
- tokens: float32 [16384, 1024], P(('row', 'col')), may hold values from -6 to 6
- teacher: float32 [16384, 1024], P(('row', 'col')), may hold values from -6 to 6
- segments: int32 [16384], P('row'), may hold values from -1 to 2, as said below
- live_mask: int32 [16384], P('row'), may hold values from 0 to 1, as said below
- weight_qkv: float32 [3, 1024, 1024], P(None, 'row', 'col'), may hold values from -0.1875 to 0.1875
- weight_proj: float32 [1024, 1024], P('col', 'row'), may hold values from -0.5 to 0.5
- weight_up: float32 [1024, 4096], P('row', 'col'), may hold values from -0.1875 to 0.1875
- weight_down: float32 [4096, 1024], P('col', 'row'), may hold values from -0.09375 to 0.09375
- norm_params: float32 [4, 1024], replicated, may hold values from -1 to 2, as said below
- first_qkv: float32 [3, 1024, 1024], P(None, 'row', 'col')
- first_proj: float32 [1024, 1024], P('col', 'row')
- first_up: float32 [1024, 4096], P('row', 'col')
- first_down: float32 [4096, 1024], P('col', 'row')
- first_norms: float32 [4, 1024], replicated
- second_qkv: float32 [3, 1024, 1024], P(None, 'row', 'col'), as said below
- second_proj: float32 [1024, 1024], P('col', 'row'), as said below
- second_up: float32 [1024, 4096], P('row', 'col'), as said below
- second_down: float32 [4096, 1024], P('col', 'row'), as said below
- second_norms: float32 [4, 1024], replicated, as said below
Outputs:
- loss_value: float32 [], replicated
- token_grad: float32 [16384, 1024], P(('row', 'col'))
- updated_qkv: float32 [3, 1024, 1024], P(None, 'row', 'col')
- updated_proj: float32 [1024, 1024], P('col', 'row')
- updated_up: float32 [1024, 4096], P('row', 'col')
- updated_down: float32 [4096, 1024], P('col', 'row')
- updated_norms: float32 [4, 1024], replicated
- momentum_qkv: float32 [3, 1024, 1024], P(None, 'row', 'col')
- momentum_proj: float32 [1024, 1024], P('col', 'row')
- momentum_up: float32 [1024, 4096], P('row', 'col')
- momentum_down: float32 [4096, 1024], P('col', 'row')
- momentum_norms: float32 [4, 1024], replicated
- variance_qkv: float32 [3, 1024, 1024], P(None, 'row', 'col')
- variance_proj: float32 [1024, 1024], P('col', 'row')
- variance_up: float32 [1024, 4096], P('row', 'col')
- variance_down: float32 [4096, 1024], P('col', 'row')
- variance_norms: float32 [4, 1024], replicated
Inputs may be any that keep to these rules, and one draw needn't show every extreme that they name: `segments`: within each group of 2048 slots, image i (0 to 2) is one run of 577 slots numbered i, the runs in order of i with padding slots, numbered -1, between or around them. `live_mask`: 1 on the first slot of every image, 0 on every padding slot. `norm_params`: rows 0 and 2 are positive. `second_qkv`: Positive. `second_proj`: Positive. `second_up`: Positive. `second_down`: Positive. `second_norms`: Positive.
All inputs are finite; a program needn't handle non-finite values.
Results may differ from a plain program's by a relative error of at most 0.012.
The roundings to bfloat16 on the way count: a program that leaves them out, or rounds other values in their place, can miss the bound.
Values may be sent and summed in bfloat16 or wider, within the bound.
No kernel may reach another device: no remote copies, remote signals or barrier semaphores. Data moves between devices by JAX's collectives and lax.ppermute only.
A program may use at most 192 MiB of HBM per device.

v0:
```python
import functools

import jax
import jax.numpy as jnp
from jax import lax
from jax.experimental import pallas as pl
from jax.experimental.pallas import tpu as pltpu
from jax.sharding import PartitionSpec as P

HEAD_DIM = 64
PATCHES = 577
STEP = 10
WINDOW = 640
QROWS = 320
TILE = 256
DIGITS = 16
SMALL = pl.CostEstimate(flops=1024, bytes_accessed=1024, transcendentals=0)
N_Z = 4
N_CORE = 2

layer_eps = 1e-06
adam_eps = 1e-08
learn_rate = 0.03
norm_rate = 0.25
moment_decay = 0.5
weight_decay = 0.05

bf16 = jnp.bfloat16
f32 = jnp.float32


def norm_forward(values, gain_row, bias_row):
    average = jnp.mean(values, axis=-1, keepdims=True)
    centred = values - average
    variance = jnp.mean(centred * centred, axis=-1, keepdims=True)
    inverse = lax.rsqrt(variance + layer_eps)
    scaled = centred * inverse
    return (scaled * gain_row + bias_row, scaled, inverse)


def norm_backward(upstream, scaled, inverse, gain_row):
    weighted = upstream * gain_row
    return inverse * (
        weighted
        - jnp.mean(weighted, axis=-1, keepdims=True)
        - scaled * jnp.mean(weighted * scaled, axis=-1, keepdims=True)
    )


def gelu_slope(hidden):
    return (
        0.5 * (1.0 + lax.erf(hidden * 0.7071067811865476))
        + hidden * jnp.exp(-0.5 * hidden * hidden) * 0.3989422804014327
    )


def adam_step(weight, gradient, momentum, variance, decay_rate, rate):
    momentum = moment_decay * momentum + (1.0 - moment_decay) * gradient
    variance = moment_decay * variance + (1.0 - moment_decay) * gradient * gradient
    correction = 1.0 - moment_decay**STEP
    direction = momentum / correction / (jnp.sqrt(variance / correction) + adam_eps)
    return (weight - rate * (direction + decay_rate * weight), momentum, variance)


def dot(left, right, left_dim, right_dim):
    return lax.dot_general(
        left, right, (((left_dim,), (right_dim,)), ((), ())), preferred_element_type=f32
    )


def head_lanes(width, head):
    lanes = lax.broadcasted_iota(jnp.int32, (1, width), 1)
    return (lanes >= head * HEAD_DIM) & (lanes < (head + 1) * HEAD_DIM)


def attend_scores(q_part, k_all, mask):
    scores = dot(q_part, k_all, 1, 1) + mask
    weights = jnp.exp(scores - jnp.max(scores, axis=-1, keepdims=True))
    return weights, jnp.sum(weights, axis=-1, keepdims=True)


def image_window(begin, group_rows):
    image = pl.program_id(0)
    start = jnp.minimum(begin[image] // 16 * 16, group_rows - WINDOW)
    first = begin[image] - start
    return image, pl.multiple_of(start, 16), first


def fill_mask(bias, mask_ref):
    for row in range(0, WINDOW, 128):
        rows = row + lax.broadcasted_iota(jnp.int32, (128, WINDOW), 0)
        cols = lax.broadcasted_iota(jnp.int32, (128, WINDOW), 1)
        mask_ref[row : row + 128, :] = jnp.where(rows == cols, 0.0, bias)


def rows_inside(rows, row_start, first):
    ids = row_start + lax.broadcasted_iota(jnp.int32, (rows, 1), 0)
    return (ids >= first) & (ids < first + PATCHES)


def attend_forward_kernel(blocks, begin, spots, code_ref, *refs):
    bias_out, out_ref, mask_ref = refs[-3:]
    image, start, first = image_window(begin, refs[0].shape[0])
    code = code_ref[pl.ds(start, WINDOW), :]
    bias = jnp.where(code == image, 0.0, -1e30).astype(f32).T
    bias_out[0] = bias[0:8, :]
    fill_mask(bias[0:1, :], mask_ref)
    lanes = refs[0].shape[1]

    for tile in range((len(refs) - 3 - blocks) // 3):
        q_ref, k_ref, v_ref = refs[3 * tile : 3 * tile + 3]
        cols = slice(tile * lanes, (tile + 1) * lanes)

        @pl.when(image == 0)
        def _():
            out_ref[:, cols] = v_ref[...]

        k_all = k_ref[pl.ds(start, WINDOW), :]
        v_all = v_ref[pl.ds(start, WINDOW), :]
        for row in range(0, WINDOW, QROWS):
            at = pl.ds(pl.multiple_of(start + row, 16), QROWS)
            q_part = q_ref[at, :] * jnp.asarray(HEAD_DIM ** (-0.5), bf16)
            inside = rows_inside(QROWS, row, first)
            mixed = None
            for head in range(lanes // HEAD_DIM):
                mine = head_lanes(lanes, head)
                q_head = jnp.where(mine, q_part, jnp.zeros_like(q_part))
                weights, totals = attend_scores(q_head, k_all, mask_ref[row : row + QROWS, :])
                part = dot(weights.astype(bf16), v_all, 1, 0) * (1.0 / totals)
                mixed = part if mixed is None else jnp.where(mine, part, mixed)
            out_ref[at, cols] = jnp.where(inside, mixed.astype(bf16), out_ref[at, cols])

    @pl.when(image == pl.num_programs(0) - 1)
    def _():
        for n, block in enumerate(refs[-3 - blocks : -3]):
            rows = block.shape[0]
            block[...] = out_ref[pl.ds(pl.multiple_of(spots[n], rows), rows), :]


def attend_backward_kernel(blocks, begin, spots, bias_ref, *refs):
    out_ref, p_ref, s_ref, go_ref, mask_ref = refs[-5:]
    go_blocks, refs = refs[3 : 3 + blocks], refs[:3]
    image, start, first = image_window(begin, refs[0].shape[0])
    fill_mask(bias_ref[0, 0:1, :], mask_ref)
    lanes = refs[0].shape[1]
    rows = go_blocks[0].shape[0]
    whole = pl.ds(start, WINDOW)
    inside_all = rows_inside(WINDOW, 0, first)

    @pl.when(image == 0)
    def _():
        for n, block_ref in enumerate(go_blocks):
            go_ref[pl.ds(pl.multiple_of(spots[n], rows), rows), :] = block_ref[...]

    for tile in range(len(refs) // 3):
        q_ref, k_ref, v_ref = refs[3 * tile : 3 * tile + 3]
        cols = slice(tile * lanes, (tile + 1) * lanes)
        base = 3 * tile * lanes
        q_cols, k_cols, v_cols = [
            slice(base + n * lanes, base + (n + 1) * lanes) for n in range(3)
        ]

        @pl.when(image == 0)
        def _():
            out_ref[:, base : base + 2 * lanes] = jnp.zeros((out_ref.shape[0], 2 * lanes), bf16)
            out_ref[:, v_cols] = go_ref[:, cols]

        k_all = k_ref[whole, :]
        v_all = v_ref[whole, :]
        q_all = q_ref[whole, :] * jnp.asarray(HEAD_DIM ** (-0.5), bf16)
        go_all = go_ref[whole, cols]
        key_grad = None
        value_grad = None
        for head in range(lanes // HEAD_DIM):
            mine = head_lanes(lanes, head)
            q_mine = jnp.where(mine, q_all, jnp.zeros_like(q_all))
            go_mine = jnp.where(mine, go_all, jnp.zeros_like(go_all))
            for row in range(0, WINDOW, QROWS):
                part = slice(row, row + QROWS)
                at = pl.ds(pl.multiple_of(start + row, 16), QROWS)
                inside = rows_inside(QROWS, row, first)
                weights, totals = attend_scores(q_mine[part], k_all, mask_ref[part, :])
                weights = weights * jnp.where(inside, 1.0 / totals, 0.0)
                weight_grad = dot(go_mine[part], v_all, 1, 1)
                product = weights * weight_grad
                score_grad = (
                    product - weights * jnp.sum(product, axis=-1, keepdims=True)
                ).astype(bf16)
                p_ref[part, :] = weights.astype(bf16)
                s_ref[part, :] = score_grad
                query_grad = (dot(score_grad, k_all, 1, 0) * HEAD_DIM ** (-0.5)).astype(bf16)
                out_ref[at, q_cols] = jnp.where(inside & mine, query_grad, out_ref[at, q_cols])
            key_part = dot(q_mine, s_ref[...], 0, 0)
            value_part = dot(go_mine, p_ref[...], 0, 0)
            key_grad = key_part if key_grad is None else key_grad + key_part
            value_grad = value_part if value_grad is None else value_grad + value_part
        key_rows = key_grad.T.astype(bf16)
        value_rows = value_grad.T.astype(bf16)
        out_ref[whole, k_cols] = jnp.where(inside_all, key_rows, out_ref[whole, k_cols])
        out_ref[whole, v_cols] = jnp.where(inside_all, value_rows, out_ref[whole, v_cols])


def qkv_operands(projected, tile):
    group_rows, total = projected.shape
    lanes = min(128, total // 3)
    if lanes % 128 == 0:
        specs = [
            pl.BlockSpec((group_rows, lanes), functools.partial(lambda n, i, *_: (0, n), 3 * tile + n))
            for n in range(3)
        ]
        return [projected] * 3, specs
    parts = [projected[:, n * lanes : (n + 1) * lanes] for n in range(3)]
    return parts, [fixed((group_rows, lanes))] * 3


def all_operands(projected):
    width = projected.shape[1] // 3
    operands, specs = [], []
    for tile in range(width // min(128, width)):
        more, places = qkv_operands(projected, tile)
        operands += more
        specs += places
    return operands, specs


def attend_forward(projected, geometry, spots, rows):
    begin, code = geometry
    group_rows, total = projected.shape
    width = total // 3
    blocks = group_rows // rows
    images = begin.shape[0]
    operands, specs = all_operands(projected)
    out = plain_call(
        functools.partial(attend_forward_kernel, blocks),
        (shaped((rows, width), bf16),) * blocks + (shaped((images, 8, WINDOW), f32),),
        code,
        *operands,
        grid=begin.shape,
        in_specs=[fixed(code.shape)] + specs,
        out_specs=(fixed((rows, width)),) * blocks
        + (pl.BlockSpec((1, 8, WINDOW), lambda i, *_: (i, 0, 0)),),
        scratch=[pltpu.VMEM((group_rows, width), bf16), pltpu.VMEM((WINDOW, WINDOW), f32)],
        scalars=(begin, spots),
        mebibytes=20,
        name="attention_forward",
    )
    return out[:blocks], out[blocks]


def attend_backward(projected, go_blocks, spots, begin, bias, tile, into):
    group_rows, total = projected.shape
    lanes = min(128, total // 3)
    operands, specs = qkv_operands(projected, tile)
    return plain_call(
        functools.partial(attend_backward_kernel, len(go_blocks)),
        shaped((group_rows, total), bf16),
        bias,
        *operands,
        *go_blocks,
        grid=begin.shape,
        in_specs=[pl.BlockSpec((1, 8, WINDOW), lambda i, *_: (i, 0, 0))]
        + specs
        + [fixed(block.shape) for block in go_blocks],
        out_specs=pl.BlockSpec((group_rows, 3 * lanes), lambda i, *_: (0, tile)),
        scratch=[pltpu.VMEM((WINDOW, WINDOW), bf16)] * 2
        + [pltpu.VMEM((group_rows, lanes), bf16), pltpu.VMEM((WINDOW, WINDOW), f32)],
        scalars=(begin, spots),
        into=into,
        mebibytes=56 if into else 16,
        name="attention_backward",
    )


def attend_geometry(segments, live_mask):
    group_rows = segments.shape[0]
    numbers = jnp.arange(group_rows // PATCHES, dtype=jnp.int32)
    positions = jnp.arange(group_rows, dtype=jnp.int32)
    begin = jnp.min(
        jnp.where(segments[None, :] == numbers[:, None], positions[None, :], group_rows - PATCHES),
        axis=1,
    )
    code = jnp.where(live_mask == 1, segments, -1)
    return begin, jnp.broadcast_to(code[:, None], (group_rows, 128))


def plain_call(kernel, out_shape, *operands, grid=(), in_specs=None, out_specs=None, scratch=(), scalars=(), into=(), mebibytes=16, name=None):
    params = pltpu.CompilerParams(vmem_limit_bytes=mebibytes * 1024 * 1024)
    if in_specs is None:
        in_specs = [pl.BlockSpec(a.shape, functools.partial(lambda n, *_: (0,) * n, a.ndim)) for a in operands]
    in_specs = list(in_specs) + [pl.BlockSpec(memory_space=pl.ANY)] * len(into)
    if out_specs is None:
        out_specs = jax.tree.map(
            lambda s: pl.BlockSpec(s.shape, functools.partial(lambda n, *_: (0,) * n, len(s.shape))), out_shape
        )
    return pl.pallas_call(
        kernel,
        grid_spec=pltpu.PrefetchScalarGridSpec(
            num_scalar_prefetch=len(scalars),
            grid=grid,
            in_specs=in_specs,
            out_specs=out_specs,
            scratch_shapes=list(scratch),
        ),
        out_shape=out_shape,
        input_output_aliases={len(scalars) + len(operands) + n: n for n in range(len(into))},
        compiler_params=params,
        cost_estimate=SMALL,
        name=name,
    )(*scalars, *operands, *into)


def shaped(shape, dtype):
    return jax.ShapeDtypeStruct(tuple(shape), dtype)


def row_blocks(rows, *widths):
    return [pl.BlockSpec((rows, w), lambda i, *_: (i, 0)) for w in widths]


def fixed(shape):
    return pl.BlockSpec(tuple(shape), functools.partial(lambda n, *_: (0,) * n, len(shape)))


def pack_kernel(live_ref, qkv_ref, proj_ref, up_ref, down_ref, qkv_out, up_out, down_out):
    count, slab, width = qkv_ref.shape
    lanes = min(128, width)
    for n in range(count):
        for t in range(width // lanes):
            at = (count * t + n) * lanes
            qkv_out[:, at : at + lanes] = qkv_ref[n][:, t * lanes : (t + 1) * lanes].astype(bf16)
    qkv_out[:, count * width :] = proj_ref[...].T.astype(bf16)
    up_out[:slab, :] = up_ref[...].astype(bf16)
    live = jnp.sum(jnp.sum(live_ref[...].astype(f32), axis=0, keepdims=True), axis=1, keepdims=True)
    high = jnp.floor(live * (1.0 / 256.0))
    middle = jnp.floor(live * (1.0 / 16.0)) - 16.0 * high
    low = live - 256.0 * high - 16.0 * middle
    row = lax.broadcasted_iota(jnp.int32, (DIGITS, up_out.shape[1]), 0)
    digits = jnp.where(row == 0, high, jnp.where(row == 1, middle, jnp.where(row == 2, low, 0.0)))
    up_out[slab:, :] = digits.astype(bf16)
    down_out[...] = down_ref[...].T.astype(bf16)


def first_kernel(tok_ref, par_ref, low_out):
    normed, _, _ = norm_forward(tok_ref[...], par_ref[0:1, :], par_ref[1:2, :])
    low_out[...] = normed.astype(bf16)


def place_blocks(blocks, spots):
    rows, width = blocks[0].shape

    def kernel(spot_ref, *refs):
        for n, ref in enumerate(refs[:-1]):
            refs[-1][pl.ds(pl.multiple_of(spot_ref[n], rows), rows), :] = ref[...]

    return plain_call(
        kernel,
        shaped((rows * len(blocks), width), bf16),
        *blocks,
        scalars=(spots,),
        mebibytes=20,
        name="place_blocks",
    )


def block_rows(block, slab):
    return pl.ds(pl.multiple_of(block * slab, slab), slab)


def stack_z(pieces, slab, places, count=1):
    height, width = pieces[0].shape
    extra = height - slab
    shapes = (shaped((N_Z * slab // count + extra, width), bf16),) * count

    def kernel(at_ref, *refs):
        held = refs[-1]
        for k, ref in enumerate(refs[:N_Z]):
            held[block_rows(lax.rem(at_ref[0] + N_Z - k, N_Z), slab), :] = ref[:slab, :]
        for n, out in enumerate(refs[N_Z:-1]):
            rows = N_Z * slab // count
            out[:rows, :] = held[n * rows : (n + 1) * rows, :]
            if extra:
                digits = refs[0][slab:, :].astype(f32)
                for ref in refs[1:N_Z]:
                    digits = digits + ref[slab:, :].astype(f32)
                out[rows:, :] = digits.astype(bf16)

    out = plain_call(
        kernel,
        shapes,
        *pieces,
        scalars=(places,),
        scratch=[pltpu.VMEM((N_Z * slab, width), bf16)],
        mebibytes=8,
        name="stack_z",
    )
    return out if count > 1 else out[0]


def weave(columns, cuts, slab, places):
    n_x = len(columns[0])
    width = columns[0][0][0].shape[1]
    flat = [piece for column in columns for half in column for piece in half]
    edges = [0, *cuts, width]
    sizes = [stop - start for start, stop in zip(edges[:-1], edges[1:])]

    def kernel(at_ref, *refs):
        outs = refs[len(flat) :]
        used = 0
        for y, column in enumerate(columns):
            for dx, half in enumerate(column):
                x = lax.rem(at_ref[1] + dx, n_x)
                share = N_Z // len(half)
                for z in range(N_Z):
                    piece = refs[used + z // share]
                    at = block_rows(z * n_x + x, slab)
                    row = z % share * slab
                    for out, start, size in zip(outs, edges, sizes):
                        out[at, y * size : (y + 1) * size] = piece[
                            row : row + slab, start : start + size
                        ]
                used += len(half)

    out = plain_call(
        kernel,
        tuple(shaped((N_Z * n_x * slab, size * len(columns)), bf16) for size in sizes),
        *flat,
        scalars=(places,),
        mebibytes=12,
        name="weave",
    )
    return out if cuts else out[0]


def proj_kernel(count, each, *refs):
    blocks, parts = refs[:count], refs[count : count + count // each]
    tok_ref, par_ref, res_out, low_out = refs[count + count // each :]
    total = tok_ref[...]
    for n, block in enumerate(blocks):
        size = block.shape[1]
        part = parts[n // each][:, n % each * size : (n % each + 1) * size]
        total = total + dot(block[...], part, 1, 1)
    res_out[...] = total
    normed, _, _ = norm_forward(total, par_ref[2:3, :], par_ref[3:4, :])
    low_out[...] = normed.astype(bf16)


ERF_TOP = (
    -2.72614225801306e-10,
    2.77068142495902e-08,
    -2.10102402082508e-06,
    -5.69250639462346e-05,
    -7.34990630326855e-04,
    -2.95459980854025e-03,
    -1.60960333262415e-02,
)
ERF_LOW = (
    -1.45660718464996e-05,
    -2.13374055278905e-04,
    -1.68282697438203e-03,
    -7.37332916720468e-03,
    -1.42647390514189e-02,
)


def erf(value):
    value = jnp.clip(value, -4.0, 4.0)
    square = value * value
    top = jnp.full_like(square, ERF_TOP[0])
    for number in ERF_TOP[1:]:
        top = top * square + number
    low = jnp.full_like(square, ERF_LOW[0])
    for number in ERF_LOW[1:]:
        low = low * square + number
    inverse = pl.reciprocal(low, approx=True)
    inverse = inverse * (2.0 - low * inverse)
    return value * top * inverse


def up_kernel(count, low_ref, *refs):
    outs = refs[-2 * count :]
    for n, part in enumerate(refs[:count]):
        hidden = dot(low_ref[...], part[...], 1, 0)
        share = 0.5 * (1.0 + erf(hidden * 0.7071067811865476))
        outs[2 * n][...] = (hidden * share).astype(bf16)
        slope = share + hidden * jnp.exp(-0.5 * hidden * hidden) * 0.3989422804014327
        outs[2 * n + 1][...] = slope.astype(bf16)


def up_call(low, parts, rows_all, spot, into):
    rows, model = low.shape
    width = parts[0].shape[1]
    cols = pl.BlockSpec((rows, TILE), lambda i, *_: (spot, i))
    return plain_call(
        functools.partial(up_kernel, len(parts)),
        (shaped((rows_all, width), bf16),) * (2 * len(parts)),
        low,
        *parts,
        grid=(width // TILE,),
        in_specs=[fixed(low.shape)] + [pl.BlockSpec((model, TILE), lambda i, *_: (0, i))] * len(parts),
        out_specs=(cols,) * (2 * len(parts)),
        into=into,
        mebibytes=14,
        name="up",
    )


def hidden_kernel(count, low_ref, *refs):
    outs = refs[-count:]
    for n in range(count):
        slope, part = refs[n], refs[count + n]
        outs[n][...] = (dot(low_ref[...], part[...], 1, 0) * slope[...].astype(f32)).astype(bf16)


def hidden_call(low, slopes, parts, spot, into):
    rows, model = low.shape
    width = parts[0].shape[1]
    cols = pl.BlockSpec((rows, TILE), lambda i, *_: (spot, i))
    return plain_call(
        functools.partial(hidden_kernel, len(parts)),
        tuple(shaped(slope.shape, bf16) for slope in slopes),
        low,
        *slopes,
        *parts,
        grid=(width // TILE,),
        in_specs=[fixed(low.shape)]
        + [cols] * len(parts)
        + [pl.BlockSpec((model, TILE), lambda i, *_: (0, i))] * len(parts),
        out_specs=(cols,) * len(parts),
        into=into,
        mebibytes=14,
        name="hidden",
    )


def wide_kernel(count, *refs):
    total = dot(refs[0][...], refs[count][...], 1, 1)
    for n in range(1, count):
        total = total + dot(refs[n][...], refs[count + n][...], 1, 1)
    refs[-1][...] = total.astype(refs[-1].dtype)


def wide_call(values, parts, rows, spot, kind):
    model, width = parts[0].shape
    return plain_call(
        functools.partial(wide_kernel, len(values)),
        shaped((rows, model), kind),
        *values,
        *parts,
        grid=(model // TILE,),
        in_specs=[pl.BlockSpec((rows, width), lambda i, *_: (spot, 0))] * len(values)
        + [pl.BlockSpec((TILE, width), lambda i, *_: (i, 0))] * len(parts),
        out_specs=pl.BlockSpec((rows, TILE), lambda i, *_: (0, i)),
        mebibytes=14,
        name="wide",
    )


def loss_kernel(chunks, each, *refs):
    res_ref, tea_ref, own_ref = refs[:3]
    received = refs[3 : 3 + chunks * each]
    live_ref, count_ref, grad_out, low_out, loss_out, far_ref = refs[3 + chunks * each :]
    add_received(received, each, far_ref)
    error = res_ref[...] - tea_ref[...] + own_ref[...] + far_ref[...]
    weighted = live_ref[...] * error
    grad = 2.0 * weighted / count_ref[...]
    grad_out[...] = grad
    low_out[...] = grad.astype(bf16)
    sums = jnp.sum(weighted * error, axis=0, keepdims=True)
    sums = jnp.concatenate([sums, jnp.zeros((7, sums.shape[1]), f32)], axis=0)
    loss_out[...] = jnp.where(pl.program_id(0) == 0, sums, loss_out[...] + sums)


def add_received(received, each, far_ref):
    for n in range(len(received) // each):

        @pl.when(pl.program_id(0) == n)
        def _():
            total = received[n * each][...].astype(f32)
            for ref in received[n * each + 1 : (n + 1) * each]:
                total = total + ref[...].astype(f32)
            far_ref[...] = total


def beside_call(parts):
    rows, width = parts[0].shape

    def kernel(*refs):
        for n, ref in enumerate(refs[:-1]):
            refs[-1][:, n * width : (n + 1) * width] = ref[...]

    return plain_call(
        kernel, shaped((rows, width * len(parts)), bf16), *parts, mebibytes=8, name="beside"
    )


def spread_kernel(each, tiles, low_ref, *refs):
    count = len(refs) // (1 + each * tiles)
    outs = refs[count:]
    for n in range(count * each):
        size = refs[0].shape[1] // each
        part = refs[n // each][:, n % each * size : (n % each + 1) * size]
        piece = dot(low_ref[...], part, 1, 0).astype(bf16)
        lanes = size // tiles
        for tile in range(tiles):
            outs[tile * count * each + n][...] = piece[:, tile * lanes : (tile + 1) * lanes]


def spread_call(low, parts, each):
    width = parts[0].shape[1] // each
    lanes = min(128, width)
    count = len(parts) * each
    out = plain_call(
        functools.partial(spread_kernel, each, width // lanes),
        tuple(shaped((low.shape[0], lanes), bf16) for _ in range(count * (width // lanes))),
        low,
        *parts,
        mebibytes=12,
        name="spread",
    )
    return [out[n : n + count] for n in range(0, len(out), count)]


def unproject_kernel(half, spots, grad_ref, part_ref, far_out, near_out):
    piece = dot(grad_ref[...], part_ref[...], 1, 1)

    @pl.when(pl.program_id(0) < half)
    def _():
        far_out[...] = piece.astype(bf16)

    @pl.when(pl.program_id(0) >= half)
    def _():
        near_out[...] = piece


def unproject_call(grads, part, blocks, rows):
    half = len(blocks) // 2
    model, width = part.shape
    return plain_call(
        functools.partial(unproject_kernel, half),
        (shaped((half * rows, model), bf16), shaped((half * rows, model), f32)),
        grads,
        part,
        grid=(len(blocks),),
        in_specs=[
            pl.BlockSpec((rows, width), lambda i, spots: (spots[i], 0)),
            fixed(part.shape),
        ],
        out_specs=(
            pl.BlockSpec((rows, model), lambda i, spots: (jnp.minimum(i, half - 1), 0)),
            pl.BlockSpec((rows, model), lambda i, spots: (jnp.maximum(i - half, 0), 0)),
        ),
        scalars=(jnp.stack(blocks).astype(jnp.int32),),
        mebibytes=48,
        name="unproject",
    )


def outer_proj_kernel(half, low_ref, *refs):
    blocks, (far_out, *near) = refs[: 2 * half], refs[2 * half :]
    turned = low_ref[...].astype(f32).T.astype(bf16)
    width = blocks[0].shape[1]
    for n in range(half):
        far_out[:, n * width : (n + 1) * width] = dot(turned, blocks[half + n][...], 1, 0).astype(bf16)
        near[n][...] = dot(turned, blocks[n][...], 1, 0).astype(bf16)


def outer_proj_call(low, blocks):
    model = low.shape[1]
    width = blocks[0].shape[1]
    half = len(blocks) // 2
    out = plain_call(
        functools.partial(outer_proj_kernel, half),
        (shaped((model, half * width), bf16),) + (shaped((model, width), bf16),) * half,
        low,
        *blocks,
        mebibytes=14,
        name="outer_proj",
    )
    return out[0], out[1:]


def add_lanes(own, received):
    width = own[0].shape[1]

    def kernel(*refs):
        got = refs[len(own)]
        for n, ref in enumerate(refs[: len(own)]):
            other = got[:, n * width : (n + 1) * width].astype(f32)
            refs[len(own) + 1 + n][...] = (ref[...].astype(f32) + other).astype(bf16)

    return plain_call(
        kernel,
        tuple(shaped(part.shape, bf16) for part in own),
        *own,
        received,
        mebibytes=8,
        name="add_lanes",
    )


def norm_sums(grad, scaled, out_ref, first):
    sums = jnp.concatenate(
        [
            jnp.sum(grad * scaled, axis=0, keepdims=True),
            jnp.sum(grad, axis=0, keepdims=True),
            jnp.zeros((6, grad.shape[1]), f32),
        ],
        axis=0,
    )
    out_ref[...] = jnp.where(first, sums, out_ref[...] + sums)


def middle_kernel(chunks, each, *refs):
    grad_ref, received = refs[0], refs[1 : 1 + chunks * each]
    res_ref, gout_ref, par_ref, full_out, low_out, sum_out, far_ref = refs[1 + chunks * each :]
    add_received(received, each, far_ref)
    _, scaled, inverse = norm_forward(res_ref[...], par_ref[2:3, :], par_ref[3:4, :])
    grad = grad_ref[...] + far_ref[...]
    full = gout_ref[...] + norm_backward(grad, scaled, inverse, par_ref[2:3, :])
    full_out[...] = full
    low_out[...] = full.astype(bf16)
    norm_sums(grad, scaled, sum_out, pl.program_id(0) == 0)


def leave_kernel(count, *refs):
    own_ref, received = refs[0], refs[1 : 1 + count]
    tok_ref, res_ref, par_ref, two_ref, loss_ref, out_ref, sum_out, sum_ref = refs[1 + count :]
    _, scaled, inverse = norm_forward(tok_ref[...], par_ref[0:1, :], par_ref[1:2, :])
    grad = own_ref[...]
    for ref in received:
        grad = grad + ref[...].astype(f32)
    out_ref[...] = res_ref[...] + norm_backward(grad, scaled, inverse, par_ref[0:1, :])
    norm_sums(grad, scaled, sum_ref, pl.program_id(0) == 0)
    sum_out[...] = jnp.concatenate(
        [sum_ref[0:2, :], two_ref[0:2, :], loss_ref[0:1, :], jnp.zeros((3, grad.shape[1]), f32)],
        axis=0,
    )


def split_x(parts, n_x, places):
    model = parts[0][0].shape[0]
    slab = model // (N_Z * n_x)
    total = sum(part[0].shape[1] for part in parts)
    flat = [piece for part in parts for piece in part]

    def kernel(at_ref, *refs):
        outs = refs[len(flat) :]
        for dx in range(n_x):
            x = lax.rem(at_ref[1] + dx, n_x)
            for z in range(N_Z):
                at = block_rows(z * n_x + x, slab)
                lane = 0
                used = 0
                for part in parts:
                    value = refs[used][at, :]
                    size = value.shape[1]
                    if len(part) > 1:
                        value = value.astype(f32)
                        for ref in refs[used + 1 : used + len(part)]:
                            value = value + ref[at, :].astype(f32)
                        value = value.astype(bf16)
                    outs[dx][z * slab : (z + 1) * slab, lane : lane + size] = value
                    lane += size
                    used += len(part)

    return plain_call(
        kernel,
        tuple(shaped((model // n_x, total), bf16) for _ in range(n_x)),
        *flat,
        scalars=(places,),
        mebibytes=12,
        name="split_x",
    )


def split_z(parts, places):
    rows, width = parts[0].shape
    slab = rows // N_Z

    def kernel(at_ref, *refs):
        for k, out in enumerate(refs[len(parts) :]):
            at = block_rows(lax.rem(at_ref[0] + k, N_Z), slab)
            total = refs[0][at, :].astype(f32)
            for ref in refs[1 : len(parts)]:
                total = total + ref[at, :].astype(f32)
            out[...] = total.astype(out.dtype)

    shapes = (shaped((slab, width), f32),) + (shaped((slab, width), bf16),) * (N_Z - 1)
    return plain_call(kernel, shapes, *parts, scalars=(places,), mebibytes=8, name="split_z")


def adam_kernel(layout, counts, *refs):
    grads = []
    for count in counts:
        grad = refs[0][...].astype(f32)
        for ref in refs[1:count]:
            grad = grad + ref[...].astype(f32)
        grads.append(grad)
        refs = refs[count:]
    count = len(layout)
    states, outs = refs[: 3 * count], refs[3 * count :]
    for n, (source, start, size, turned) in enumerate(layout):
        weight, first, second = states[3 * n : 3 * n + 3]
        if len(weight.shape) == 3:
            matrices = weight.shape[0]
            lanes = size // matrices
            for k in range(matrices):
                own = [
                    grads[at][:, lane + k * lanes : lane + (k + 1) * lanes] for at, lane in start
                ]
                own = own[0] if len(own) == 1 else jnp.concatenate(own, axis=1)
                new = adam_step(weight[k], own, first[k], second[k], weight_decay, learn_rate)
                for out, value in zip(outs[3 * n : 3 * n + 3], new):
                    out[k] = value
        else:
            part = grads[source][:, start : start + size]
            if turned:
                part = part.T
            new = adam_step(weight[...], part, first[...], second[...], weight_decay, learn_rate)
            for out, value in zip(outs[3 * n : 3 * n + 3], new):
                out[...] = value


def adam_call(groups, layout, *states):
    shapes = tuple(shaped(s.shape, f32) for s in states)
    out = plain_call(
        functools.partial(adam_kernel, layout, [len(group) for group in groups]),
        shapes,
        *[piece for group in groups for piece in group],
        *states,
        mebibytes=16,
        name="adam",
    )
    return [out[3 * n : 3 * n + 3] for n in range(len(layout))]


def tie(*values):
    return lax.optimization_barrier(values)


def local(
    n_x,
    n_y,
    tokens,
    teacher,
    segments,
    live_mask,
    weight_qkv,
    weight_proj,
    weight_up,
    weight_down,
    norm_params,
    first_qkv,
    first_proj,
    first_up,
    first_down,
    first_norms,
    second_qkv,
    second_proj,
    second_up,
    second_down,
    second_norms,
):
    z_at, x_at = lax.axis_index("z"), lax.axis_index("x")
    y_at, core_at = lax.axis_index("y"), lax.axis_index("core")
    rows, model = tokens.shape
    group_rows = segments.shape[0]
    slab = weight_qkv.shape[1]
    width = weight_qkv.shape[2]
    unit = weight_up.shape[1]
    part_rows = min(128, rows)
    wide_rows = min(256, rows)
    depth = N_Z * slab
    sizes = {"z": N_Z, "x": n_x, "y": n_y, "core": N_CORE}
    places = jnp.stack([z_at, x_at]).astype(jnp.int32)
    offsets = [(dc, dy) for dc in range(N_CORE) for dy in range(n_y)]
    other = N_CORE - 1

    def send(value, axis, step):
        size = sizes[axis]
        return lax.ppermute(value, axis, [(i, (i + step) % size) for i in range(size)])

    def send_col(value, dy, dc):
        perm = [
            (y * N_CORE + c, (y + dy) % n_y * N_CORE + (c + dc) % N_CORE)
            for y in range(n_y)
            for c in range(N_CORE)
        ]
        return lax.ppermute(value, ("y", "core"), perm)

    def fetch(value, axis):
        return [value] + [send(value, axis, -k) for k in range(1, sizes[axis])]

    def fetch_z(value):
        return [value] + [send(value, "z", k) for k in range(1, N_Z)]

    def place(dy, dc):
        return ((y_at + dy) % n_y * N_CORE + (core_at + dc) % N_CORE) * rows

    shard_qkv, shard_up, shard_down = plain_call(
        pack_kernel,
        (
            shaped((slab, 4 * width), bf16),
            shaped((slab + DIGITS, unit), bf16),
            shaped((slab, unit), bf16),
        ),
        live_mask.reshape(-1, 128),
        weight_qkv,
        weight_proj,
        weight_up,
        weight_down,
        mebibytes=8,
        name="pack",
    )
    near_qkv = fetch_z(shard_qkv)
    block_qkv = stack_z(near_qkv, slab, places)
    geometry = attend_geometry(segments, live_mask)
    own_live = lax.dynamic_slice_in_dim(
        live_mask, (y_at * N_CORE + core_at) * rows, rows, 0
    ).astype(f32)[:, None]
    spots_here = jnp.stack([place(dy, dc) for dc, dy in offsets]).astype(jnp.int32)
    spots = jnp.stack([place(-dy, -dc) for dc, dy in offsets]).astype(jnp.int32)
    block_qkv, shard_down, shard_up, tokens, geometry, own_live, spots_here, spots = tie(
        block_qkv, shard_down, shard_up, tokens, geometry, own_live, spots_here, spots
    )

    beside_qkv = fetch(block_qkv, "x")
    near_up = fetch_z(shard_up)
    low_one = plain_call(
        first_kernel,
        shaped(tokens.shape, bf16),
        tokens,
        norm_params,
        grid=(rows // part_rows,),
        in_specs=row_blocks(part_rows, model) + [fixed(norm_params.shape)],
        out_specs=row_blocks(part_rows, model)[0],
        mebibytes=8,
        name="first",
    )
    blocks_one = fetch(low_one, "y")
    beside_qkv, near_up, blocks_one, shard_down = tie(beside_qkv, near_up, blocks_one, shard_down)

    block_up = stack_z(near_up, slab, places)
    full_qkv, part_proj = weave([[[part] for part in beside_qkv]], [3 * width], slab, places)
    block_up, part_proj, blocks_one = tie(block_up, part_proj, blocks_one)
    blocks_one = blocks_one + [send(block, "core", -1) for block in blocks_one]
    group_one = place_blocks(blocks_one, spots_here)
    beside_up = fetch(block_up, "x")
    near_down = fetch_z(shard_down)
    full_proj = fetch(part_proj, "y")
    projected = dot(group_one, full_qkv, 1, 0).astype(bf16)
    mixed, bias = attend_forward(projected, geometry, spots, rows)
    mixed, beside_up, near_down, full_proj = tie(mixed, beside_up, near_down, full_proj)

    blocks_mixed = [
        piece if key == (0, 0) else send_col(piece, -key[1], -key[0])
        for key, piece in zip(offsets, mixed)
    ]
    full_proj = [beside_call(full_proj)]
    full_proj.append(send(full_proj[0], "core", -1))
    blocks_down = stack_z(near_down, slab, places, 2)
    beside_down = [fetch(blocks_down[0], "x")]
    full_up = [weave([[[part] for part in beside_up]], [], slab, places)]
    live_count = sum(
        256.0 * part[depth, 0].astype(f32) + 16.0 * part[depth + 1, 0].astype(f32)
        + part[depth + 2, 0].astype(f32)
        for part in beside_up
    ).reshape(1, 1)
    blocks_mixed, full_proj, full_up, live_count, beside_down, blocks_down = tie(
        blocks_mixed, full_proj, full_up, live_count, beside_down, blocks_down
    )
    beside_down.append(fetch(blocks_down[1], "x"))
    full_up.append(send(full_up[0], "core", -1))
    count = len(offsets)
    residual, low_two = plain_call(
        functools.partial(proj_kernel, count, n_y),
        (shaped(tokens.shape, f32), shaped(tokens.shape, bf16)),
        *blocks_mixed,
        *full_proj,
        tokens,
        norm_params,
        grid=(rows // wide_rows,),
        in_specs=row_blocks(wide_rows, *([width] * count))
        + [fixed(part.shape) for part in full_proj]
        + row_blocks(wide_rows, model)
        + [fixed(norm_params.shape)],
        out_specs=tuple(row_blocks(wide_rows, model, model)),
        mebibytes=18,
        name="proj",
    )
    low_two, full_up = tie(low_two, full_up)

    chunk = min(256, rows)
    chunks = range(rows // chunk)
    neighbours = range(1, n_y)
    rows_all = n_y * rows

    def cross(value, n):
        piece = value[n * chunk : (n + 1) * chunk]
        return {dy: send(piece, "y", -dy) for dy in neighbours}

    def spot_of(dy, n):
        return (dy * rows) // chunk + n

    low_far = {0: cross(low_two, 0)}
    hidden = up_call(low_two, full_up, rows_all, 0, ())
    low_far[0], hidden, low_two, beside_down = tie(low_far[0], hidden, low_two, beside_down)
    full_down = [weave([list(zip(*beside_down))], [], slab, places)]
    full_down.append(send(full_down[0], "core", -1))
    far_out = {}
    for n in chunks:
        if n + 1 in chunks:
            low_far[n + 1] = cross(low_two, n + 1)
        for dy in neighbours:
            hidden = up_call(low_far[n][dy], full_up, rows_all, spot_of(dy, n), hidden)
        outs = {
            dy: wide_call(hidden[::2], full_down, chunk, spot_of(dy, n), bf16) for dy in neighbours
        }
        if n + 1 in chunks:
            outs, hidden, low_far[n + 1] = tie(outs, hidden, low_far[n + 1])
        else:
            outs, hidden = tie(outs, hidden)
        if n:
            far_out[n - 1] = tie(far_out[n - 1], outs)[0]
        far_out[n] = {dy: send(outs[dy], "y", dy) for dy in neighbours}
    own_out = wide_call(hidden[::2], full_down, rows, 0, f32)
    own_out, far_out = tie(own_out, far_out)
    far_out = [far_out[n][dy] for n in chunks for dy in neighbours]
    each = len(neighbours)
    grad_output, grad_branch, loss_rows = plain_call(
        functools.partial(loss_kernel, len(chunks), each),
        (shaped(tokens.shape, f32), shaped(tokens.shape, bf16), shaped((8, model), f32)),
        residual,
        teacher,
        own_out,
        *far_out,
        own_live,
        live_count,
        grid=(len(chunks),),
        in_specs=row_blocks(chunk, model, model, model)
        + [fixed((chunk, model))] * len(far_out)
        + row_blocks(chunk, 1)
        + [fixed((1, 1))],
        out_specs=tuple(row_blocks(chunk, model, model) + [fixed((8, model))]),
        scratch=[pltpu.VMEM((chunk, model), f32)],
        mebibytes=20,
        name="loss",
    )
    active, slope = hidden[::2], hidden[1::2]

    grad_far = {0: cross(grad_branch, 0)}
    grad_hidden = hidden_call(grad_branch, slope, full_down, 0, ())
    own_two = wide_call(grad_hidden, full_up, rows, 0, f32)
    grad_far[0], grad_hidden, own_two, grad_branch = tie(
        grad_far[0], grad_hidden, own_two, grad_branch
    )
    def gather_rows(own, far):
        return jnp.concatenate([own] + [far[n][dy] for dy in neighbours for n in chunks], axis=0)

    far_two = {}
    for n in chunks:
        if n + 1 in chunks:
            grad_far[n + 1] = cross(grad_branch, n + 1)
        for dy in neighbours:
            grad_hidden = hidden_call(
                grad_far[n][dy], slope, full_down, spot_of(dy, n), grad_hidden
            )
        outs = {
            dy: wide_call(grad_hidden, full_up, chunk, spot_of(dy, n), bf16) for dy in neighbours
        }
        if n + 1 in chunks:
            outs, grad_hidden, grad_far[n + 1] = tie(outs, grad_hidden, grad_far[n + 1])
        else:
            grad_all = gather_rows(grad_branch, grad_far)
            far_down = dot(grad_all, active[other], 0, 0).astype(bf16)
            outs, grad_hidden, grad_all, far_down, far_two = tie(
                outs, grad_hidden, grad_all, far_down, far_two
            )
        far_two[n] = {dy: send(outs[dy], "y", dy) for dy in neighbours}

    low_all = gather_rows(low_two, low_far)
    far_up = dot(low_all, grad_hidden[other], 0, 0).astype(bf16)
    sent_down, sent_up = send(far_down, "core", 1), send(far_up, "core", 1)
    hold_down = (dot(grad_all, active[0], 0, 0) + sent_down.astype(f32)).astype(bf16)
    halves_down = split_x([[hold_down]], n_x, places)
    hold_up = (dot(low_all, grad_hidden[0], 0, 0) + sent_up.astype(f32)).astype(bf16)
    halves_up = split_x([[hold_up]], n_x, places)
    far_two, halves_down, halves_up = tie(far_two, halves_down, halves_up)
    far_two = [far_two[n][dy] for n in chunks for dy in neighbours]
    grad_residual, grad_low, sums_two = plain_call(
        functools.partial(middle_kernel, len(chunks), each),
        (shaped(tokens.shape, f32), shaped(tokens.shape, bf16), shaped((8, model), f32)),
        own_two,
        *far_two,
        residual,
        grad_output,
        norm_params,
        grid=(len(chunks),),
        in_specs=row_blocks(chunk, model)
        + [fixed((chunk, model))] * len(far_two)
        + row_blocks(chunk, model, model)
        + [fixed(norm_params.shape)],
        out_specs=tuple(row_blocks(chunk, model, model) + [fixed((8, model))]),
        scratch=[pltpu.VMEM((chunk, model), f32)],
        mebibytes=20,
        name="middle",
    )
    pieces_attn = spread_call(grad_low, full_proj, n_y)
    pieces_attn, halves_down, halves_up, grad_low = tie(
        pieces_attn, halves_down, halves_up, grad_low
    )

    def send_back(pieces):
        return [
            piece if key == (0, 0) else send_col(piece, key[1], key[0])
            for key, piece in zip(offsets, pieces)
        ]

    def hop_x(halves):
        return [halves[0]] + [send(halves[dx], "x", dx) for dx in range(1, n_x)]

    def spread_z(pieces):
        return [pieces[0]] + [send(pieces[k], "z", k) for k in range(1, N_Z)]

    lanes = 3 * min(128, width)
    tiles = 3 * width // lanes
    sent_attn = send_back(pieces_attn[0])
    parts_down = hop_x(halves_down)
    far_proj, grad_proj = outer_proj_call(grad_low, blocks_mixed)
    sent_attn, far_proj, grad_proj = tie(sent_attn, far_proj, grad_proj)

    sent_later = [send_back(pieces) for pieces in pieces_attn[1:]]
    sent_proj = send(far_proj, "core", 1)
    grad_projected = attend_backward(projected, sent_attn, spots, geometry[0], bias, 0, ())
    grad_projected, sent_later, sent_proj, parts_down, halves_up = tie(
        grad_projected, sent_later, sent_proj, parts_down, halves_up
    )

    hold_proj = add_lanes(grad_proj, sent_proj)
    pieces_down = split_z(parts_down, places)
    grad_projected, pieces_down, hold_proj, halves_up = tie(
        grad_projected, pieces_down, hold_proj, halves_up
    )
    parts_up = hop_x(halves_up)
    last_down = spread_z(pieces_down)
    part_proj = [hold_proj[0]] + [send(hold_proj[k], "y", k) for k in range(1, n_y)]
    for tile in range(1, tiles):
        grad_projected = attend_backward(
            projected, sent_later[tile - 1], spots, geometry[0], bias, tile, (grad_projected,)
        )
    grad_projected, parts_up, last_down, part_proj = tie(
        grad_projected, parts_up, last_down, part_proj
    )

    far_one, near_one = unproject_call(
        grad_projected,
        full_qkv,
        [place(dy, dc) // rows for dc in reversed(range(N_CORE)) for dy in range(n_y)],
        rows,
    )
    far_one, grad_projected = tie(far_one, grad_projected)
    sent_one = send(far_one, "core", 1)
    grad_qkv = dot(group_one, grad_projected, 0, 0).astype(bf16)
    halves_qkv = split_x([[grad_qkv], part_proj], n_x, places)
    pieces_up = split_z(parts_up, places)
    halves_qkv, sent_one, near_one, pieces_up = tie(halves_qkv, sent_one, near_one, pieces_up)

    parts = [
        near_one[dy * rows : (dy + 1) * rows] + sent_one[dy * rows : (dy + 1) * rows].astype(f32)
        for dy in range(n_y)
    ]
    sent_parts = [parts[k].astype(bf16) for k in range(1, n_y)]
    halves_qkv, sent_parts, pieces_up = tie(halves_qkv, sent_parts, pieces_up)
    received = [send(part, "y", k) for k, part in enumerate(sent_parts, 1)]
    parts_qkv = hop_x(halves_qkv)
    last_up = spread_z(pieces_up)
    (new_down,) = adam_call(
        [last_down], [(0, 0, unit, True)], weight_down, first_down, second_down
    )
    parts_qkv, received, last_up, new_down = tie(parts_qkv, received, last_up, new_down)

    pieces_qkv = split_z(parts_qkv, places)
    token_grad, sums = plain_call(
        functools.partial(leave_kernel, len(received)),
        (shaped(tokens.shape, f32), shaped((8, model), f32)),
        parts[0],
        *received,
        tokens,
        grad_residual,
        norm_params,
        sums_two,
        loss_rows,
        grid=(rows // part_rows,),
        in_specs=row_blocks(part_rows, *([model] * (3 + len(received))))
        + [fixed(norm_params.shape), fixed((8, model)), fixed((8, model))],
        out_specs=tuple(row_blocks(part_rows, model) + [fixed((8, model))]),
        scratch=[pltpu.VMEM((8, model), f32)],
        mebibytes=14,
        name="leave",
    )
    sums, token_grad, pieces_qkv = tie(sums, token_grad, pieces_qkv)
    last_qkv = spread_z(pieces_qkv)
    for axis in ("core", "y", "x", "z"):
        step = 1
        while step < sizes[axis]:
            pairs = [(i, i ^ step) for i in range(sizes[axis])]
            sums = sums + lax.ppermute(sums, axis, pairs)
            step *= 2
    (new_up,) = adam_call([last_up], [(0, 0, unit, False)], weight_up, first_up, second_up)
    sums, last_qkv, new_up = tie(sums, last_qkv, new_up)
    loss_sum = jnp.sum(sums[4])
    live_count = live_count[0, 0]

    new_qkv, new_proj = adam_call(
        [last_qkv],
        [(0, [(0, n * lanes) for n in range(tiles)], lanes, False), (0, 3 * width, width, True)],
        weight_qkv,
        first_qkv,
        second_qkv,
        weight_proj,
        first_proj,
        second_proj,
    )
    new_norms = adam_step(norm_params, sums[:4], first_norms, second_norms, 0.0, norm_rate)
    return (
        loss_sum / live_count,
        token_grad,
        new_qkv[0],
        new_proj[0],
        new_up[0],
        new_down[0],
        new_norms[0],
        new_qkv[1],
        new_proj[1],
        new_up[1],
        new_down[1],
        new_norms[1],
        new_qkv[2],
        new_proj[2],
        new_up[2],
        new_down[2],
        new_norms[2],
    )


def solution(mesh):
    n_x = mesh.shape["row"] // N_Z
    n_y = mesh.shape["col"] // N_CORE
    mesh = jax.sharding.Mesh(
        mesh.devices.reshape(N_Z, n_x, n_y, N_CORE), ("z", "x", "y", "core")
    )
    row, col = ("z", "x"), ("y", "core")
    matrices = (P(None, row, col), P(col, row), P(row, col), P(col, row), P())
    tokens = P(row + col, None)
    return jax.shard_map(
        functools.partial(local, n_x, n_y),
        mesh=mesh,
        in_specs=(tokens, tokens, P(row), P(row)) + matrices * 3,
        out_specs=(P(), tokens) + matrices * 3,
        check_vma=False,
    )
```

profile of v0, /device:TPU:0, one launch (start us, length us, event | category | flops | bytes accessed | tf_op | source)
XLA Modules:
  0.0 361.5 jit_solution(1323127818923766771)
XLA Ops:
  6.2 3.0 collective-permute-start
  9.3 2.6 collective-permute-start.1
  15.7 2.9 collective-permute-done.refs_1_
  18.6 10.4 %collective-permute-done.1.refs_2_ = bf16[128,1024]{1,0:T(8,128)(2,1)S(1)} collective-permute-done((bf16[128,1024]{1,0:T(8,128)(2,1)S(1)}, bf16[128,1024]{1,0:T(8,128)(2,1)S(1)}, u32[]{:S(2)}, u32[]{:S(2)}) %collective-permute-start.1) | collective-permute-done | bytes 262176 | tf_op jit(solution)/shard_map/ppermute | solution.py:881
  29.0 1.6 stack_z.3.refs_0_
  35.2 6.2 %collective-permute-start.4 = (bf16[144,1024]{1,0:T(8,128)(2,1)S(1)}, bf16[144,1024]{1,0:T(8,128)(2,1)S(1)}, u32[]{:S(2)}, u32[]{:S(2)}) collective-permute-start(bf16[144,1024]{1,0:T(8,128)(2,1)S(1)} %get-tuple-element.293.refs_0_), channel_id=1, source_target_pairs={{0,8},{8,16},{16,24},{24,0},{1,9},{9,17},{17,25},{25,1},{2,10},{10... | collective-permute-start | bytes 884744 | tf_op jit(solution)/shard_map/ppermute | solution.py:881
  43.7 6.6 %collective-permute-done.4.refs_1_ = bf16[144,1024]{1,0:T(8,128)(2,1)S(1)} collective-permute-done((bf16[144,1024]{1,0:T(8,128)(2,1)S(1)}, bf16[144,1024]{1,0:T(8,128)(2,1)S(1)}, u32[]{:S(2)}, u32[]{:S(2)}) %collective-permute-start.4) | collective-permute-done | bytes 294944 | tf_op jit(solution)/shard_map/ppermute | solution.py:881
  50.3 10.3 %collective-permute-done.5.refs_2_ = bf16[144,1024]{1,0:T(8,128)(2,1)S(1)} collective-permute-done((bf16[144,1024]{1,0:T(8,128)(2,1)S(1)}, bf16[144,1024]{1,0:T(8,128)(2,1)S(1)}, u32[]{:S(2)}, u32[]{:S(2)}) %collective-permute-start.5) | collective-permute-done | bytes 294944 | tf_op jit(solution)/shard_map/ppermute | solution.py:881
  63.2 6.8 %collective-permute-start.11 = (bf16[128,1024]{1,0:T(8,128)(2,1)S(1)}, bf16[128,1024]{1,0:T(8,128)(2,1)S(1)}, u32[]{:S(2)}, u32[]{:S(2)}) collective-permute-start(bf16[128,1024]{1,0:T(8,128)(2,1)S(1)} %copy-done.71), channel_id=1, source_target_pairs={{0,8},{8,16},{16,24},{24,0},{1,9},{9,17},{17,25},{25,1},{2,10},{10... | collective-permute-start | bytes 786440 | tf_op jit(solution)/shard_map/ppermute | solution.py:881
  69.9 2.5 collective-permute-start.12
  74.8 3.8 %convolution_convert_fusion.refs_0_.refs_1_.refs_2_.refs_3_.refs_4_.refs_5_ = bf16[2048,768]{1,0:T(8,128)(2,1)S(1)} fusion(bf16[2048,1024]{1,0:T(8,128)(2,1)S(1)} %place_blocks.1, bf16[1024,768]{1,0:T(8,128)(2,1)S(1)} %get-tuple-element.307.part_ref), kind=kOutput, calls=%fused_computation.2 | convolution fusion | flops 3222798336 | bytes 8912896 | tf_op jit(solution)/shard_map/dot_general | solution.py:66
  78.6 13.7 %attention_forward.1 = (bf16[512,256]{1,0:T(8,128)(2,1)S(1)}, bf16[512,256]{1,0:T(8,128)(2,1)S(1)}, bf16[512,256]{1,0:T(8,128)(2,1)S(1)}, bf16[512,256]{1,0:T(8,128)(2,1)S(1)}, f32[3,8,640]{2,1,0:T(8,128)S(1)}) custom-call(s32[3]{0:T(128)S(1)} %select_reduce_fusion.begin, s32[4]{0:T(128)S(1)} %get-tuple-element.305.spots, ...), custom_call_target="tpu_custom_call" | custom-call | flops 1024 | bytes 1024 | tf_op jit(solution)/shard_map/attention_forward/pallas_call | solution.py:295
  103.1 4.2 %collective-permute-done.17.refs_3_ = bf16[512,256]{1,0:T(8,128)(2,1)S(1)} collective-permute-done((bf16[512,256]{1,0:T(8,128)(2,1)S(1)}, bf16[512,256]{1,0:T(8,128)(2,1)S(1)}, u32[]{:S(2)}, u32[]{:S(2)}) %collective-permute-start.17) | collective-permute-done | bytes 262176 | tf_op jit(solution)/shard_map/ppermute | solution.py:889
  109.4 2.1 proj.1
  111.9 1.6 collective-permute-start.21
  113.5 8.9 %up.3 = (bf16[1024,1024]{1,0:T(8,128)(2,1)S(1)}, bf16[1024,1024]{1,0:T(8,128)(2,1)S(1)}, bf16[1024,1024]{1,0:T(8,128)(2,1)S(1)}, bf16[1024,1024]{1,0:T(8,128)(2,1)S(1)}) custom-call(bf16[512,1024]{1,0:T(8,128)(2,1)S(1)} %get-tuple-element.362.low_ref, bf16[1024,1024]{1,0:T(8,128)(2,1)S(1)} %weave.4.refs_0_.refs_2_, ...), custom_call_target="tpu_custom_call" | custom-call | flops 1024 | bytes 1024 | tf_op jit(solution)/shard_map/up/pallas_call | solution.py:295
  122.4 3.6 collective-permute-done.21.low_ref
  128.5 5.1 %up.4 = (bf16[1024,1024]{1,0:T(8,128)(2,1)S(1)}, bf16[1024,1024]{1,0:T(8,128)(2,1)S(1)}, bf16[1024,1024]{1,0:T(8,128)(2,1)S(1)}, bf16[1024,1024]{1,0:T(8,128)(2,1)S(1)}) custom-call(bf16[256,1024]{1,0:T(8,128)(2,1)S(1)} %collective-permute-done.21.low_ref, ...), custom_call_target="tpu_custom_call", output_to_operand_aliasing={{0}: (3, {}), {1}: (4, {}), {2}: (5, {}), {3}: (6, {})} | custom-call | flops 1024 | bytes 1024 | tf_op jit(solution)/shard_map/up/pallas_call | solution.py:295
  133.6 2.9 wide.6
  136.5 4.7 %collective-permute-done.24.low_ref = bf16[256,1024]{1,0:T(8,128)(2,1)S(1)} collective-permute-done((bf16[256,1024]{1,0:T(8,128)(2,1)S(1)}, bf16[256,1024]{1,0:T(8,128)(2,1)S(1)}, u32[]{:S(2)}, u32[]{:S(2)}) %collective-permute-start.24) | collective-permute-done | bytes 524320 | tf_op jit(solution)/shard_map/ppermute | solution.py:881
  142.8 5.5 %up.5 = (bf16[1024,1024]{1,0:T(8,128)(2,1)S(1)}, bf16[1024,1024]{1,0:T(8,128)(2,1)S(1)}, bf16[1024,1024]{1,0:T(8,128)(2,1)S(1)}, bf16[1024,1024]{1,0:T(8,128)(2,1)S(1)}) custom-call(bf16[256,1024]{1,0:T(8,128)(2,1)S(1)} %collective-permute-done.24.low_ref, ...), custom_call_target="tpu_custom_call", output_to_operand_aliasing={{0}: (3, {}), {1}: (4, {}), {2}: (5, {}), {3}: (6, {})} | custom-call | flops 1024 | bytes 1024 | tf_op jit(solution)/shard_map/up/pallas_call | solution.py:295
  148.3 3.4 wide.7
  152.5 1.6 copy-done.4
  154.1 1.6 copy-done.9
  155.7 1.6 copy-done.12
  157.2 1.6 copy-done.15
  158.8 3.1 wide.8.refs_2_
  162.0 4.4 %collective-permute-done.26.refs_4_ = bf16[256,1024]{1,0:T(8,128)(2,1)} collective-permute-done((bf16[256,1024]{1,0:T(8,128)(2,1)}, bf16[256,1024]{1,0:T(8,128)(2,1)}, u32[]{:S(2)}, u32[]{:S(2)}) %collective-permute-start.26) | collective-permute-done | bytes 524320 | tf_op jit(solution)/shard_map/ppermute | solution.py:881
  166.4 2.5 loss.1
  170.5 4.0 %hidden.3 = (bf16[1024,1024]{1,0:T(8,128)(2,1)S(1)}, bf16[1024,1024]{1,0:T(8,128)(2,1)S(1)}) custom-call(bf16[512,1024]{1,0:T(8,128)(2,1)S(1)} %get-tuple-element.393.low_ref, bf16[1024,1024]{1,0:T(8,128)(2,1)S(1)} %copy-done.18, bf16[1024,1024]{1,0:T(8,128)(2,1)S(1)} %copy-done.20, bf16[1024,1024]{1,0:T(8,128)(2,1)S(1)} %copy-done.5, ...), custom_call_target="tpu_custom_call" | custom-call | flops 1024 | bytes 1024 | tf_op jit(solution)/shard_map/hidden/pallas_call | solution.py:295
  174.5 3.1 wide.9.refs_0_
  177.7 4.3 %collective-permute-done.27.low_ref = bf16[256,1024]{1,0:T(8,128)(2,1)S(1)} collective-permute-done((bf16[256,1024]{1,0:T(8,128)(2,1)S(1)}, bf16[256,1024]{1,0:T(8,128)(2,1)S(1)}, u32[]{:S(2)}, u32[]{:S(2)}) %collective-permute-start.27) | collective-permute-done | bytes 524320 | tf_op jit(solution)/shard_map/ppermute | solution.py:881
  183.4 2.6 hidden.4
  186.0 2.0 wide.10
  188.1 6.1 %collective-permute-done.28.low_ref = bf16[256,1024]{1,0:T(8,128)(2,1)S(1)} collective-permute-done((bf16[256,1024]{1,0:T(8,128)(2,1)S(1)}, bf16[256,1024]{1,0:T(8,128)(2,1)S(1)}, u32[]{:S(2)}, u32[]{:S(2)}) %collective-permute-start.28) | collective-permute-done | bytes 524320 | tf_op jit(solution)/shard_map/ppermute | solution.py:881
  195.4 2.6 hidden.5
  198.0 2.0 wide.11
  200.0 2.5 convolution_convert_fusion.2
  202.5 3.0 collective-permute-done.29.refs_1_
  205.5 2.4 convolution_convert_fusion.1
  209.6 2.5 add_convert_fusion.1.refs_0_
  212.6 2.5 add_convert_fusion.refs_0_
  215.8 1.7 split_x.4
  218.4 4.0 %collective-permute-done.30.refs_2_ = bf16[256,1024]{1,0:T(8,128)(2,1)S(1)} collective-permute-done((bf16[256,1024]{1,0:T(8,128)(2,1)S(1)}, bf16[256,1024]{1,0:T(8,128)(2,1)S(1)}, u32[]{:S(2)}, u32[]{:S(2)}) %collective-permute-start.30) | collective-permute-done | bytes 524320 | tf_op jit(solution)/shard_map/ppermute | solution.py:881
  222.5 2.1 middle.1
  236.0 13.4 %attention_backward.2.refs_7_ = bf16[2048,768]{1,0:T(8,128)(2,1)S(1)} custom-call(s32[3]{0:T(128)S(1)} %copy-done.78, s32[4]{0:T(128)S(1)} %copy-done.80, f32[3,8,640]{2,1,0:T(8,128)S(1)} %get-tuple-element.308.bias_ref, bf16[2048,768]{1,0:T(8,128)(2,1)S(1)} %convolution_convert_fusion.refs_0_.refs_1_.refs_2_.refs_3_.refs_4_.refs_5_, ...), custom_call_target="tpu_custom_call" | custom-call | flops 1024 | bytes 1024 | tf_op jit(solution)/shard_map/attention_backward/pallas_call | solution.py:295
  249.5 5.1 %collective-permute-done.40.refs_1_ = bf16[512,1024]{1,0:T(8,128)(2,1)S(1)} collective-permute-done((bf16[512,1024]{1,0:T(8,128)(2,1)S(1)}, bf16[512,1024]{1,0:T(8,128)(2,1)S(1)}, u32[]{:S(2)}, u32[]{:S(2)}) %collective-permute-start.40) | collective-permute-done | bytes 1048608 | tf_op jit(solution)/shard_map/ppermute | solution.py:881
  259.3 2.9 collective-permute-start.42
  262.3 2.1 collective-permute-start.43
  264.7 16.7 %attention_backward.3.grad_ref = bf16[2048,768]{1,0:T(8,128)(2,1)} custom-call(s32[3]{0:T(128)} %copy-done.77, s32[4]{0:T(128)} %copy-done.79, f32[3,8,640]{2,1,0:T(8,128)} %copy-done.72, bf16[2048,768]{1,0:T(8,128)(2,1)} %copy-done, bf16[2048,768]{1,0:T(8,128)(2,1)} %copy-done, bf16[2048,768]{1,0:T(8,128)(2,1)} %copy-done, ...), custom_call_target="tpu_custom_call", output_to_operand_aliasing={{}: (10, {})} | custom-call | flops 1024 | bytes 1024 | tf_op jit(solution)/shard_map/attention_backward/pallas_call | solution.py:295
  281.6 7.8 %unproject.1 = (bf16[1024,1024]{1,0:T(8,128)(2,1)S(1)}, f32[1024,1024]{1,0:T(8,128)}) custom-call(s32[4]{0:T(128)S(1)} %pad_add_fusion.3.spots, bf16[2048,768]{1,0:T(8,128)(2,1)} %attention_backward.3.grad_ref, bf16[1024,768]{1,0:T(8,128)(2,1)S(1)} %copy-done.48), custom_call_target="tpu_custom_call" | custom-call | flops 1024 | bytes 1024 | tf_op jit(solution)/shard_map/unproject/pallas_call | solution.py:295
  290.2 3.6 convolution_convert_fusion.3.refs_0_
  293.8 1.8 split_x.5
  298.8 4.3 %collective-permute-start.49 = (bf16[128,1024]{1,0:T(8,128)(2,1)S(1)}, bf16[128,1024]{1,0:T(8,128)(2,1)S(1)}, u32[]{:S(2)}, u32[]{:S(2)}) collective-permute-start(bf16[128,1024]{1,0:T(8,128)(2,1)S(1)} %get-tuple-element.501), channel_id=1, source_target_pairs={{0,8},{8,16},{16,24},{24,0},{1,9},{9,17},{17,25},{25,1},{2,10},{10... | collective-permute-start | bytes 786440 | tf_op jit(solution)/shard_map/ppermute | solution.py:881
  303.0 1.7 collective-permute-start.50
  305.4 2.6 adam.3
  308.1 3.3 collective-permute-done.49.refs_1_
  311.4 10.5 %collective-permute-done.50.refs_2_ = bf16[128,1024]{1,0:T(8,128)(2,1)S(1)} collective-permute-done((bf16[128,1024]{1,0:T(8,128)(2,1)S(1)}, bf16[128,1024]{1,0:T(8,128)(2,1)S(1)}, u32[]{:S(2)}, u32[]{:S(2)}) %collective-permute-start.50) | collective-permute-done | bytes 262176 | tf_op jit(solution)/shard_map/ppermute | solution.py:881
  324.2 3.1 leave.1
  327.3 4.7 %collective-permute-start.57 = (bf16[128,1024]{1,0:T(8,128)(2,1)S(1)}, bf16[128,1024]{1,0:T(8,128)(2,1)S(1)}, u32[]{:S(2)}, u32[]{:S(2)}) collective-permute-start(bf16[128,1024]{1,0:T(8,128)(2,1)S(1)} %get-tuple-element.525), channel_id=1, source_target_pairs={{0,8},{8,16},{16,24},{24,0},{1,9},{9,17},{17,25},{25,1},{2,10},{10... | collective-permute-start | bytes 786440 | tf_op jit(solution)/shard_map/ppermute | solution.py:881
  337.0 2.6 collective-permute-done.53
  340.6 2.9 collective-permute-done.54
  344.4 6.2 %collective-permute-done.55 = f32[8,1024]{1,0:T(8,128)S(1)} collective-permute-done((f32[8,1024]{1,0:T(8,128)S(1)}, f32[8,1024]{1,0:T(8,128)S(1)}, u32[]{:S(2)}, u32[]{:S(2)}) %collective-permute-start.55) | collective-permute-done | bytes 32800 | tf_op jit(solution)/shard_map/ppermute | solution.py:1207
  350.5 3.1 collective-permute-start.56
  (306 shorter events, 79.1 us)
Async XLA Ops:
  6.2 12.3 %collective-permute-start = (bf16[128,1024]{1,0:T(8,128)(2,1)S(1)}, bf16[128,1024]{1,0:T(8,128)(2,1)S(1)}, u32[]{:S(2)}, u32[]{:S(2)}) collective-permute-start(bf16[128,1024]{1,0:T(8,128)(2,1)S(1)} %get-tuple-element.285.refs_0_), channel_id=1, source_target_pairs={{0,8},{8,16},{16,24},{24,0},{1,9},{9,17},{17,25},{25,1},{2,10},{10... | collective-permute-start | bytes 786440 | tf_op jit(solution)/shard_map/ppermute | solution.py:881
  9.3 19.7 %collective-permute-start.1 = (bf16[128,1024]{1,0:T(8,128)(2,1)S(1)}, bf16[128,1024]{1,0:T(8,128)(2,1)S(1)}, u32[]{:S(2)}, u32[]{:S(2)}) collective-permute-start(bf16[128,1024]{1,0:T(8,128)(2,1)S(1)} %get-tuple-element.285.refs_0_), channel_id=1, source_target_pairs={{0,16},{8,24},{16,0},{24,8},{1,17},{9,25},{17,1},{25,9},{2,18},{10... | collective-permute-start | bytes 786440 | tf_op jit(solution)/shard_map/ppermute | solution.py:881
  11.9 17.1 %collective-permute-start.2 = (bf16[128,1024]{1,0:T(8,128)(2,1)S(1)}, bf16[128,1024]{1,0:T(8,128)(2,1)}, u32[]{:S(2)}, u32[]{:S(2)}) collective-permute-start(bf16[128,1024]{1,0:T(8,128)(2,1)S(1)} %get-tuple-element.285.refs_0_), channel_id=1, source_target_pairs={{0,24},{8,0},{16,8},{24,16},{1,25},{9,1},{17,9},{25,17},{2,26},{10... | collective-permute-start | bytes 786440 | tf_op jit(solution)/shard_map/ppermute | solution.py:881
  14.0 64.6 %copy-start.77 = (s32[3]{0:T(128)}, s32[3]{0:T(128)S(1)}, u32[]{:S(2)}) copy-start(s32[3]{0:T(128)S(1)} %select_reduce_fusion.begin) | copy-start | bytes 40
  14.9 63.7 %copy-start.79 = (s32[4]{0:T(128)}, s32[4]{0:T(128)S(1)}, u32[]{:S(2)}) copy-start(s32[4]{0:T(128)S(1)} %get-tuple-element.305.spots) | copy-start | bytes 52
  30.9 29.7 %collective-permute-start.3 = (bf16[512,1024]{1,0:T(8,128)(2,1)S(1)}, bf16[512,1024]{1,0:T(8,128)(2,1)S(1)}, u32[]{:S(2)}, u32[]{:S(2)}) collective-permute-start(bf16[512,1024]{1,0:T(8,128)(2,1)S(1)} %stack_z.3.refs_0_), channel_id=1, source_target_pairs={{0,4},{4,0},{1,5},{5,1},{2,6},{6,2},{3,7},{7,3},{8,12},{12,8},{9,1... | collective-permute-start | bytes 3145736 | tf_op jit(solution)/shard_map/ppermute | solution.py:881
  33.6 27.1 %collective-permute-start.7 = (bf16[512,1024]{1,0:T(8,128)(2,1)S(1)}, bf16[512,1024]{1,0:T(8,128)(2,1)S(1)}, u32[]{:S(2)}, u32[]{:S(2)}) collective-permute-start(bf16[512,1024]{1,0:T(8,128)(2,1)S(1)} %first.1.refs_0_), channel_id=1, source_target_pairs={{0,2},{2,0},{1,3},{3,1},{4,6},{6,4},{5,7},{7,5},{8,10},{10,8},{9,1... | collective-permute-start | bytes 3145736 | tf_op jit(solution)/shard_map/ppermute | solution.py:881
  35.2 15.2 %collective-permute-start.4 = (bf16[144,1024]{1,0:T(8,128)(2,1)S(1)}, bf16[144,1024]{1,0:T(8,128)(2,1)S(1)}, u32[]{:S(2)}, u32[]{:S(2)}) collective-permute-start(bf16[144,1024]{1,0:T(8,128)(2,1)S(1)} %get-tuple-element.293.refs_0_), channel_id=1, source_target_pairs={{0,8},{8,16},{16,24},{24,0},{1,9},{9,17},{17,25},{25,1},{2,10},{10... | collective-permute-start | bytes 884744 | tf_op jit(solution)/shard_map/ppermute | solution.py:881
  41.3 19.3 %collective-permute-start.5 = (bf16[144,1024]{1,0:T(8,128)(2,1)S(1)}, bf16[144,1024]{1,0:T(8,128)(2,1)S(1)}, u32[]{:S(2)}, u32[]{:S(2)}) collective-permute-start(bf16[144,1024]{1,0:T(8,128)(2,1)S(1)} %get-tuple-element.293.refs_0_), channel_id=1, source_target_pairs={{0,16},{8,24},{16,0},{24,8},{1,17},{9,25},{17,1},{25,9},{2,18},{10... | collective-permute-start | bytes 884744 | tf_op jit(solution)/shard_map/ppermute | solution.py:881
  42.8 17.8 %collective-permute-start.6 = (bf16[144,1024]{1,0:T(8,128)(2,1)S(1)}, bf16[144,1024]{1,0:T(8,128)(2,1)S(1)}, u32[]{:S(2)}, u32[]{:S(2)}) collective-permute-start(bf16[144,1024]{1,0:T(8,128)(2,1)S(1)} %get-tuple-element.293.refs_0_), channel_id=1, source_target_pairs={{0,24},{8,0},{16,8},{24,16},{1,25},{9,1},{17,9},{25,17},{2,26},{10... | collective-permute-start | bytes 884744 | tf_op jit(solution)/shard_map/ppermute | solution.py:881
  62.0 10.4 %collective-permute-start.8 = (bf16[512,1024]{1,0:T(8,128)(2,1)S(1)}, bf16[512,1024]{1,0:T(8,128)(2,1)S(1)}, u32[]{:S(2)}, u32[]{:S(2)}) collective-permute-start(bf16[512,1024]{1,0:T(8,128)(2,1)S(1)} %first.1.refs_0_), channel_id=1, source_target_pairs={{0,1},{1,0},{2,3},{3,2},{4,5},{5,4},{6,7},{7,6},{8,9},{9,8},{10,11... | collective-permute-start | bytes 3145736 | tf_op jit(solution)/shard_map/ppermute | solution.py:881
  62.1 11.3 %collective-permute-start.9 = (bf16[512,1024]{1,0:T(8,128)(2,1)S(1)}, bf16[512,1024]{1,0:T(8,128)(2,1)S(1)}, u32[]{:S(2)}, u32[]{:S(2)}) collective-permute-start(bf16[512,1024]{1,0:T(8,128)(2,1)S(1)} %collective-permute-done.7.refs_1_), channel_id=1, source_target_pairs={{0,1},{1,0},{2,3},{3,2},{4,5},{5,4},{6,7},{7,6},{8,9},{9,8},{10,11... | collective-permute-start | bytes 3145736 | tf_op jit(solution)/shard_map/ppermute | solution.py:881
  62.6 29.8 %collective-permute-start.10 = (bf16[528,1024]{1,0:T(8,128)(2,1)S(1)}, bf16[528,1024]{1,0:T(8,128)(2,1)S(1)}, u32[]{:S(2)}, u32[]{:S(2)}) collective-permute-start(bf16[528,1024]{1,0:T(8,128)(2,1)S(1)} %stack_z.4.refs_0_), channel_id=1, source_target_pairs={{0,4},{4,0},{1,5},{5,1},{2,6},{6,2},{3,7},{7,3},{8,12},{12,8},{9,1... | collective-permute-start | bytes 3244040 | tf_op jit(solution)/shard_map/ppermute | solution.py:881
  63.2 29.2 %collective-permute-start.11 = (bf16[128,1024]{1,0:T(8,128)(2,1)S(1)}, bf16[128,1024]{1,0:T(8,128)(2,1)S(1)}, u32[]{:S(2)}, u32[]{:S(2)}) collective-permute-start(bf16[128,1024]{1,0:T(8,128)(2,1)S(1)} %copy-done.71), channel_id=1, source_target_pairs={{0,8},{8,16},{16,24},{24,0},{1,9},{9,17},{17,25},{25,1},{2,10},{10... | collective-permute-start | bytes 786440 | tf_op jit(solution)/shard_map/ppermute | solution.py:881
  69.9 22.5 %collective-permute-start.12 = (bf16[128,1024]{1,0:T(8,128)(2,1)S(1)}, bf16[128,1024]{1,0:T(8,128)(2,1)S(1)}, u32[]{:S(2)}, u32[]{:S(2)}) collective-permute-start(bf16[128,1024]{1,0:T(8,128)(2,1)S(1)} %copy-done.71), channel_id=1, source_target_pairs={{0,16},{8,24},{16,0},{24,8},{1,17},{9,25},{17,1},{25,9},{2,18},{10... | collective-permute-start | bytes 786440 | tf_op jit(solution)/shard_map/ppermute | solution.py:881
  72.4 20.0 %collective-permute-start.13 = (bf16[128,1024]{1,0:T(8,128)(2,1)S(1)}, bf16[128,1024]{1,0:T(8,128)(2,1)S(1)}, u32[]{:S(2)}, u32[]{:S(2)}) collective-permute-start(bf16[128,1024]{1,0:T(8,128)(2,1)S(1)} %copy-done.71), channel_id=1, source_target_pairs={{0,24},{8,0},{16,8},{24,16},{1,25},{9,1},{17,9},{25,17},{2,26},{10... | collective-permute-start | bytes 786440 | tf_op jit(solution)/shard_map/ppermute | solution.py:881
  73.4 19.0 %collective-permute-start.14 = (bf16[1024,256]{1,0:T(8,128)(2,1)S(1)}, bf16[1024,256]{1,0:T(8,128)(2,1)S(1)}, u32[]{:S(2)}, u32[]{:S(2)}) collective-permute-start(bf16[1024,256]{1,0:T(8,128)(2,1)S(1)} %get-tuple-element.320.refs_0_), channel_id=1, source_target_pairs={{0,2},{2,0},{1,3},{3,1},{4,6},{6,4},{5,7},{7,5},{8,10},{10,8},{9,1... | collective-permute-start | bytes 1572872 | tf_op jit(solution)/shard_map/ppermute | solution.py:881
  78.6 157.4 %copy-start = (bf16[2048,768]{1,0:T(8,128)(2,1)}, bf16[2048,768]{1,0:T(8,128)(2,1)S(1)}, u32[]{:S(2)}) copy-start(bf16[2048,768]{1,0:T(8,128)(2,1)S(1)} %convolution_convert_fusion.refs_0_.refs_1_.refs_2_.refs_3_.refs_4_.refs_5_) | copy-start | bytes 9437188
  92.4 143.6 %copy-start.72 = (f32[3,8,640]{2,1,0:T(8,128)}, f32[3,8,640]{2,1,0:T(8,128)S(1)}, u32[]{:S(2)}) copy-start(f32[3,8,640]{2,1,0:T(8,128)S(1)} %get-tuple-element.308.bias_ref) | copy-start | bytes 184324
  92.5 15.2 %collective-permute-start.18 = (bf16[1024,512]{1,0:T(8,128)(2,1)S(1)}, bf16[1024,512]{1,0:T(8,128)(2,1)S(1)}, u32[]{:S(2)}, u32[]{:S(2)}) collective-permute-start(bf16[1024,512]{1,0:T(8,128)(2,1)S(1)} %beside.1.refs_4_.refs_0_), channel_id=1, source_target_pairs={{0,1},{1,0},{2,3},{3,2},{4,5},{5,4},{6,7},{7,6},{8,9},{9,8},{10,11... | collective-permute-start | bytes 3145736 | tf_op jit(solution)/shard_map/ppermute | solution.py:881
  93.3 14.4 %collective-permute-start.19 = (bf16[256,1024]{1,0:T(8,128)(2,1)S(1)}, bf16[256,1024]{1,0:T(8,128)(2,1)S(1)}, u32[]{:S(2)}, u32[]{:S(2)}) collective-permute-start(bf16[256,1024]{1,0:T(8,128)(2,1)S(1)} %get-tuple-element.356.refs_0_), channel_id=1, source_target_pairs={{0,4},{4,0},{1,5},{5,1},{2,6},{6,2},{3,7},{7,3},{8,12},{12,8},{9,1... | collective-permute-start | bytes 1572872 | tf_op jit(solution)/shard_map/ppermute | solution.py:881
  94.0 9.1 %collective-permute-start.15 = (bf16[512,256]{1,0:T(8,128)(2,1)S(1)}, bf16[512,256]{1,0:T(8,128)(2,1)S(1)}, u32[]{:S(2)}, u32[]{:S(2)}) collective-permute-start(bf16[512,256]{1,0:T(8,128)(2,1)S(1)} %get-tuple-element.317), channel_id=1, source_target_pairs={{0,2},{1,3},{2,0},{3,1},{4,6},{5,7},{6,4},{7,5},{8,10},{9,11},{10,... | collective-permute-start | bytes 786440 | tf_op jit(solution)/shard_map/ppermute | solution.py:889
  95.5 7.6 %collective-permute-start.16 = (bf16[512,256]{1,0:T(8,128)(2,1)S(1)}, bf16[512,256]{1,0:T(8,128)(2,1)S(1)}, u32[]{:S(2)}, u32[]{:S(2)}) collective-permute-start(bf16[512,256]{1,0:T(8,128)(2,1)S(1)} %get-tuple-element.318), channel_id=1, source_target_pairs={{0,1},{1,0},{2,3},{3,2},{4,5},{5,4},{6,7},{7,6},{8,9},{9,8},{10,11... | collective-permute-start | bytes 786440 | tf_op jit(solution)/shard_map/ppermute | solution.py:889
  95.5 11.8 %collective-permute-start.17 = (bf16[512,256]{1,0:T(8,128)(2,1)S(1)}, bf16[512,256]{1,0:T(8,128)(2,1)S(1)}, u32[]{:S(2)}, u32[]{:S(2)}) collective-permute-start(bf16[512,256]{1,0:T(8,128)(2,1)S(1)} %get-tuple-element.319), channel_id=1, source_target_pairs={{0,3},{1,2},{2,1},{3,0},{4,7},{5,6},{6,5},{7,4},{8,11},{9,10},{10,... | collective-permute-start | bytes 786440 | tf_op jit(solution)/shard_map/ppermute | solution.py:889
  107.7 4.2 %collective-permute-start.20 = (bf16[1024,1024]{1,0:T(8,128)(2,1)S(1)}, bf16[1024,1024]{1,0:T(8,128)(2,1)S(1)}, u32[]{:S(2)}, u32[]{:S(2)}) collective-permute-start(bf16[1024,1024]{1,0:T(8,128)(2,1)S(1)} %weave.4.refs_0_.refs_2_), channel_id=1, source_target_pairs={{0,1},{1,0},{2,3},{3,2},{4,5},{5,4},{6,7},{7,6},{8,9},{9,8},{10,11... | collective-permute-start | bytes 6291464 | tf_op jit(solution)/shard_map/ppermute | solution.py:881
  107.9 14.5 %collective-permute-start.22 = (bf16[256,1024]{1,0:T(8,128)(2,1)S(1)}, bf16[256,1024]{1,0:T(8,128)(2,1)S(1)}, u32[]{:S(2)}, u32[]{:S(2)}) collective-permute-start(bf16[256,1024]{1,0:T(8,128)(2,1)S(1)} %get-tuple-element.357.refs_1_), channel_id=1, source_target_pairs={{0,4},{4,0},{1,5},{5,1},{2,6},{6,2},{3,7},{7,3},{8,12},{12,8},{9,1... | collective-permute-start | bytes 1572872 | tf_op jit(solution)/shard_map/ppermute | solution.py:881
  111.9 14.1 %collective-permute-start.21 = (bf16[256,1024]{1,0:T(8,128)(2,1)S(1)}, bf16[256,1024]{1,0:T(8,128)(2,1)S(1)}, u32[]{:S(2)}, u32[]{:S(2)}) collective-permute-start(bf16[256,1024]{1,0:T(8,128)(2,1)S(1)} %slice.54), channel_id=1, source_target_pairs={{0,2},{2,0},{1,3},{3,1},{4,6},{6,4},{5,7},{7,5},{8,10},{10,8},{9,1... | collective-permute-start | bytes 1572872 | tf_op jit(solution)/shard_map/ppermute | solution.py:881
  126.7 6.8 %collective-permute-start.23 = (bf16[1024,1024]{1,0:T(8,128)(2,1)S(1)}, bf16[1024,1024]{1,0:T(8,128)(2,1)S(1)}, u32[]{:S(2)}, u32[]{:S(2)}) collective-permute-start(bf16[1024,1024]{1,0:T(8,128)(2,1)S(1)} %weave.5.refs_2_), channel_id=1, source_target_pairs={{0,1},{1,0},{2,3},{3,2},{4,5},{5,4},{6,7},{7,6},{8,9},{9,8},{10,11... | collective-permute-start | bytes 6291464 | tf_op jit(solution)/shard_map/ppermute | solution.py:881
  126.9 14.4 %collective-permute-start.24 = (bf16[256,1024]{1,0:T(8,128)(2,1)S(1)}, bf16[256,1024]{1,0:T(8,128)(2,1)S(1)}, u32[]{:S(2)}, u32[]{:S(2)}) collective-permute-start(bf16[256,1024]{1,0:T(8,128)(2,1)S(1)} %slice.55), channel_id=1, source_target_pairs={{0,2},{2,0},{1,3},{3,1},{4,6},{6,4},{5,7},{7,5},{8,10},{10,8},{9,1... | collective-permute-start | bytes 1572872 | tf_op jit(solution)/shard_map/ppermute | solution.py:881
  141.3 20.7 %collective-permute-start.25 = (bf16[256,1024]{1,0:T(8,128)(2,1)}, bf16[256,1024]{1,0:T(8,128)(2,1)}, u32[]{:S(2)}, u32[]{:S(2)}) collective-permute-start(bf16[256,1024]{1,0:T(8,128)(2,1)} %wide.6), channel_id=1, source_target_pairs={{0,2},{2,0},{1,3},{3,1},{4,6},{6,4},{5,7},{7,5},{8,10},{10,8},{9,1... | collective-permute-start | bytes 1572872 | tf_op jit(solution)/shard_map/ppermute | solution.py:881
  151.7 14.6 %collective-permute-start.26 = (bf16[256,1024]{1,0:T(8,128)(2,1)}, bf16[256,1024]{1,0:T(8,128)(2,1)}, u32[]{:S(2)}, u32[]{:S(2)}) collective-permute-start(bf16[256,1024]{1,0:T(8,128)(2,1)} %wide.7), channel_id=1, source_target_pairs={{0,2},{2,0},{1,3},{3,1},{4,6},{6,4},{5,7},{7,5},{8,10},{10,8},{9,1... | collective-permute-start | bytes 1572872 | tf_op jit(solution)/shard_map/ppermute | solution.py:881
  168.9 13.1 %collective-permute-start.27 = (bf16[256,1024]{1,0:T(8,128)(2,1)S(1)}, bf16[256,1024]{1,0:T(8,128)(2,1)S(1)}, u32[]{:S(2)}, u32[]{:S(2)}) collective-permute-start(bf16[256,1024]{1,0:T(8,128)(2,1)S(1)} %slice.56), channel_id=1, source_target_pairs={{0,2},{2,0},{1,3},{3,1},{4,6},{6,4},{5,7},{7,5},{8,10},{10,8},{9,1... | collective-permute-start | bytes 1572872 | tf_op jit(solution)/shard_map/ppermute | solution.py:881
  182.1 12.2 %collective-permute-start.28 = (bf16[256,1024]{1,0:T(8,128)(2,1)S(1)}, bf16[256,1024]{1,0:T(8,128)(2,1)S(1)}, u32[]{:S(2)}, u32[]{:S(2)}) collective-permute-start(bf16[256,1024]{1,0:T(8,128)(2,1)S(1)} %slice.57), channel_id=1, source_target_pairs={{0,2},{2,0},{1,3},{3,1},{4,6},{6,4},{5,7},{7,5},{8,10},{10,8},{9,1... | collective-permute-start | bytes 1572872 | tf_op jit(solution)/shard_map/ppermute | solution.py:881
  194.2 11.2 %collective-permute-start.29 = (bf16[256,1024]{1,0:T(8,128)(2,1)S(1)}, bf16[256,1024]{1,0:T(8,128)(2,1)S(1)}, u32[]{:S(2)}, u32[]{:S(2)}) collective-permute-start(bf16[256,1024]{1,0:T(8,128)(2,1)S(1)} %wide.10), channel_id=1, source_target_pairs={{0,2},{2,0},{1,3},{3,1},{4,6},{6,4},{5,7},{7,5},{8,10},{10,8},{9,1... | collective-permute-start | bytes 1572872 | tf_op jit(solution)/shard_map/ppermute | solution.py:881
  205.5 4.2 %collective-permute-start.31 = (bf16[1024,1024]{1,0:T(8,128)(2,1)S(1)}, bf16[1024,1024]{1,0:T(8,128)(2,1)S(1)}, u32[]{:S(2)}, u32[]{:S(2)}) collective-permute-start(bf16[1024,1024]{1,0:T(8,128)(2,1)S(1)} %convolution_convert_fusion.2), channel_id=1, source_target_pairs={{0,1},{1,0},{2,3},{3,2},{4,5},{5,4},{6,7},{7,6},{8,9},{9,8},{10,11... | collective-permute-start | bytes 6291464 | tf_op jit(solution)/shard_map/ppermute | solution.py:881
  208.0 4.7 %collective-permute-start.32 = (bf16[1024,1024]{1,0:T(8,128)(2,1)S(1)}, bf16[1024,1024]{1,0:T(8,128)(2,1)S(1)}, u32[]{:S(2)}, u32[]{:S(2)}) collective-permute-start(bf16[1024,1024]{1,0:T(8,128)(2,1)S(1)} %convolution_convert_fusion.1), channel_id=1, source_target_pairs={{0,1},{1,0},{2,3},{3,2},{4,5},{5,4},{6,7},{7,6},{8,9},{9,8},{10,11... | collective-permute-start | bytes 6291464 | tf_op jit(solution)/shard_map/ppermute | solution.py:881
  208.6 13.9 %collective-permute-start.30 = (bf16[256,1024]{1,0:T(8,128)(2,1)S(1)}, bf16[256,1024]{1,0:T(8,128)(2,1)S(1)}, u32[]{:S(2)}, u32[]{:S(2)}) collective-permute-start(bf16[256,1024]{1,0:T(8,128)(2,1)S(1)} %wide.11), channel_id=1, source_target_pairs={{0,2},{2,0},{1,3},{3,1},{4,6},{6,4},{5,7},{7,5},{8,10},{10,8},{9,1... | collective-permute-start | bytes 1572872 | tf_op jit(solution)/shard_map/ppermute | solution.py:881
  225.9 6.3 %collective-permute-start.33 = (bf16[512,128]{1,0:T(8,128)(2,1)S(1)}, bf16[512,128]{1,0:T(8,128)(2,1)S(1)}, u32[]{:S(2)}, u32[]{:S(2)}) collective-permute-start(bf16[512,128]{1,0:T(8,128)(2,1)S(1)} %get-tuple-element.427), channel_id=1, source_target_pairs={{0,2},{1,3},{2,0},{3,1},{4,6},{5,7},{6,4},{7,5},{8,10},{9,11},{10,... | collective-permute-start | bytes 393224 | tf_op jit(solution)/shard_map/ppermute | solution.py:889
  226.7 5.5 %collective-permute-start.34 = (bf16[512,128]{1,0:T(8,128)(2,1)S(1)}, bf16[512,128]{1,0:T(8,128)(2,1)S(1)}, u32[]{:S(2)}, u32[]{:S(2)}) collective-permute-start(bf16[512,128]{1,0:T(8,128)(2,1)S(1)} %get-tuple-element.428), channel_id=1, source_target_pairs={{0,1},{1,0},{2,3},{3,2},{4,5},{5,4},{6,7},{7,6},{8,9},{9,8},{10,11... | collective-permute-start | bytes 393224 | tf_op jit(solution)/shard_map/ppermute | solution.py:889
  226.7 5.8 %collective-permute-start.35 = (bf16[512,128]{1,0:T(8,128)(2,1)S(1)}, bf16[512,128]{1,0:T(8,128)(2,1)S(1)}, u32[]{:S(2)}, u32[]{:S(2)}) collective-permute-start(bf16[512,128]{1,0:T(8,128)(2,1)S(1)} %get-tuple-element.429), channel_id=1, source_target_pairs={{0,3},{1,2},{2,1},{3,0},{4,7},{5,6},{6,5},{7,4},{8,11},{9,10},{10,... | collective-permute-start | bytes 393224 | tf_op jit(solution)/shard_map/ppermute | solution.py:889
  229.4 25.1 %collective-permute-start.40 = (bf16[512,1024]{1,0:T(8,128)(2,1)S(1)}, bf16[512,1024]{1,0:T(8,128)(2,1)S(1)}, u32[]{:S(2)}, u32[]{:S(2)}) collective-permute-start(bf16[512,1024]{1,0:T(8,128)(2,1)S(1)} %get-tuple-element.444), channel_id=1, source_target_pairs={{0,4},{4,0},{1,5},{5,1},{2,6},{6,2},{3,7},{7,3},{8,12},{12,8},{9,1... | collective-permute-start | bytes 3145736 | tf_op jit(solution)/shard_map/ppermute | solution.py:881
  232.5 22.1 %collective-permute-start.39 = (bf16[1024,512]{1,0:T(8,128)(2,1)S(1)}, bf16[1024,512]{1,0:T(8,128)(2,1)S(1)}, u32[]{:S(2)}, u32[]{:S(2)}) collective-permute-start(bf16[1024,512]{1,0:T(8,128)(2,1)S(1)} %get-tuple-element.442), channel_id=1, source_target_pairs={{0,1},{1,0},{2,3},{3,2},{4,5},{5,4},{6,7},{7,6},{8,9},{9,8},{10,11... | collective-permute-start | bytes 3145736 | tf_op jit(solution)/shard_map/ppermute | solution.py:881
  233.9 15.6 %collective-permute-start.36 = (bf16[512,128]{1,0:T(8,128)(2,1)S(1)}, bf16[512,128]{1,0:T(8,128)(2,1)S(1)}, u32[]{:S(2)}, u32[]{:S(2)}) collective-permute-start(bf16[512,128]{1,0:T(8,128)(2,1)S(1)} %get-tuple-element.439), channel_id=1, source_target_pairs={{0,2},{1,3},{2,0},{3,1},{4,6},{5,7},{6,4},{7,5},{8,10},{9,11},{10,... | collective-permute-start | bytes 393224 | tf_op jit(solution)/shard_map/ppermute | solution.py:889
  234.6 14.9 %collective-permute-start.37 = (bf16[512,128]{1,0:T(8,128)(2,1)S(1)}, bf16[512,128]{1,0:T(8,128)(2,1)S(1)}, u32[]{:S(2)}, u32[]{:S(2)}) collective-permute-start(bf16[512,128]{1,0:T(8,128)(2,1)S(1)} %get-tuple-element.440), channel_id=1, source_target_pairs={{0,1},{1,0},{2,3},{3,2},{4,5},{5,4},{6,7},{7,6},{8,9},{9,8},{10,11... | collective-permute-start | bytes 393224 | tf_op jit(solution)/shard_map/ppermute | solution.py:889
  234.6 14.9 %collective-permute-start.38 = (bf16[512,128]{1,0:T(8,128)(2,1)S(1)}, bf16[512,128]{1,0:T(8,128)(2,1)S(1)}, u32[]{:S(2)}, u32[]{:S(2)}) collective-permute-start(bf16[512,128]{1,0:T(8,128)(2,1)S(1)} %get-tuple-element.441), channel_id=1, source_target_pairs={{0,3},{1,2},{2,1},{3,0},{4,7},{5,6},{6,5},{7,4},{8,11},{9,10},{10,... | collective-permute-start | bytes 393224 | tf_op jit(solution)/shard_map/ppermute | solution.py:889
  257.1 24.5 %collective-permute-start.41 = (bf16[512,1024]{1,0:T(8,128)(2,1)}, bf16[512,1024]{1,0:T(8,128)(2,1)S(1)}, u32[]{:S(2)}, u32[]{:S(2)}) collective-permute-start(bf16[512,1024]{1,0:T(8,128)(2,1)} %get-tuple-element.467), channel_id=1, source_target_pairs={{0,4},{4,0},{1,5},{5,1},{2,6},{6,2},{3,7},{7,3},{8,12},{12,8},{9,1... | collective-permute-start | bytes 3145736 | tf_op jit(solution)/shard_map/ppermute | solution.py:881
  258.6 22.8 %collective-permute-start.45 = (bf16[1024,256]{1,0:T(8,128)(2,1)}, bf16[1024,256]{1,0:T(8,128)(2,1)}, u32[]{:S(2)}, u32[]{:S(2)}) collective-permute-start(bf16[1024,256]{1,0:T(8,128)(2,1)} %get-tuple-element.473), channel_id=1, source_target_pairs={{0,2},{2,0},{1,3},{3,1},{4,6},{6,4},{5,7},{7,5},{8,10},{10,8},{9,1... | collective-permute-start | bytes 1572872 | tf_op jit(solution)/shard_map/ppermute | solution.py:881
  259.3 22.1 %collective-permute-start.42 = (bf16[128,1024]{1,0:T(8,128)(2,1)}, bf16[128,1024]{1,0:T(8,128)(2,1)S(1)}, u32[]{:S(2)}, u32[]{:S(2)}) collective-permute-start(bf16[128,1024]{1,0:T(8,128)(2,1)} %get-tuple-element.469), channel_id=1, source_target_pairs={{0,8},{8,16},{16,24},{24,0},{1,9},{9,17},{17,25},{25,1},{2,10},{10... | collective-permute-start | bytes 786440 | tf_op jit(solution)/shard_map/ppermute | solution.py:881
  262.3 19.2 %collective-permute-start.43 = (bf16[128,1024]{1,0:T(8,128)(2,1)}, bf16[128,1024]{1,0:T(8,128)(2,1)}, u32[]{:S(2)}, u32[]{:S(2)}) collective-permute-start(bf16[128,1024]{1,0:T(8,128)(2,1)} %get-tuple-element.470), channel_id=1, source_target_pairs={{0,16},{8,24},{16,0},{24,8},{1,17},{9,25},{17,1},{25,9},{2,18},{10... | collective-permute-start | bytes 786440 | tf_op jit(solution)/shard_map/ppermute | solution.py:881
  264.4 17.1 %collective-permute-start.44 = (bf16[128,1024]{1,0:T(8,128)(2,1)}, bf16[128,1024]{1,0:T(8,128)(2,1)}, u32[]{:S(2)}, u32[]{:S(2)}) collective-permute-start(bf16[128,1024]{1,0:T(8,128)(2,1)} %get-tuple-element.471), channel_id=1, source_target_pairs={{0,24},{8,0},{16,8},{24,16},{1,25},{9,1},{17,9},{25,17},{2,26},{10... | collective-permute-start | bytes 786440 | tf_op jit(solution)/shard_map/ppermute | solution.py:881
  289.4 6.2 %collective-permute-start.46 = (bf16[1024,1024]{1,0:T(8,128)(2,1)S(1)}, bf16[1024,1024]{1,0:T(8,128)(2,1)S(1)}, u32[]{:S(2)}, u32[]{:S(2)}) collective-permute-start(bf16[1024,1024]{1,0:T(8,128)(2,1)S(1)} %get-tuple-element.481), channel_id=1, source_target_pairs={{0,1},{1,0},{2,3},{3,2},{4,5},{5,4},{6,7},{7,6},{8,9},{9,8},{10,11... | collective-permute-start | bytes 6291464 | tf_op jit(solution)/shard_map/ppermute | solution.py:881
  296.5 25.6 %collective-permute-start.47 = (bf16[512,1024]{1,0:T(8,128)(2,1)S(1)}, bf16[512,1024]{1,0:T(8,128)(2,1)S(1)}, u32[]{:S(2)}, u32[]{:S(2)}) collective-permute-start(bf16[512,1024]{1,0:T(8,128)(2,1)S(1)} %get-tuple-element.498), channel_id=1, source_target_pairs={{0,4},{4,0},{1,5},{5,1},{2,6},{6,2},{3,7},{7,3},{8,12},{12,8},{9,1... | collective-permute-start | bytes 3145736 | tf_op jit(solution)/shard_map/ppermute | solution.py:881
  298.1 25.3 %collective-permute-start.48 = (bf16[512,1024]{1,0:T(8,128)(2,1)S(1)}, bf16[512,1024]{1,0:T(8,128)(2,1)S(1)}, u32[]{:S(2)}, u32[]{:S(2)}) collective-permute-start(bf16[512,1024]{1,0:T(8,128)(2,1)S(1)} %get-tuple-element.499), channel_id=1, source_target_pairs={{0,2},{2,0},{1,3},{3,1},{4,6},{6,4},{5,7},{7,5},{8,10},{10,8},{9,1... | collective-permute-start | bytes 3145736 | tf_op jit(solution)/shard_map/ppermute | solution.py:881
  298.8 12.6 %collective-permute-start.49 = (bf16[128,1024]{1,0:T(8,128)(2,1)S(1)}, bf16[128,1024]{1,0:T(8,128)(2,1)S(1)}, u32[]{:S(2)}, u32[]{:S(2)}) collective-permute-start(bf16[128,1024]{1,0:T(8,128)(2,1)S(1)} %get-tuple-element.501), channel_id=1, source_target_pairs={{0,8},{8,16},{16,24},{24,0},{1,9},{9,17},{17,25},{25,1},{2,10},{10... | collective-permute-start | bytes 786440 | tf_op jit(solution)/shard_map/ppermute | solution.py:881
  303.0 18.9 %collective-permute-start.50 = (bf16[128,1024]{1,0:T(8,128)(2,1)S(1)}, bf16[128,1024]{1,0:T(8,128)(2,1)S(1)}, u32[]{:S(2)}, u32[]{:S(2)}) collective-permute-start(bf16[128,1024]{1,0:T(8,128)(2,1)S(1)} %get-tuple-element.502), channel_id=1, source_target_pairs={{0,16},{8,24},{16,0},{24,8},{1,17},{9,25},{17,1},{25,9},{2,18},{10... | collective-permute-start | bytes 786440 | tf_op jit(solution)/shard_map/ppermute | solution.py:881
  304.7 17.2 %collective-permute-start.51 = (bf16[128,1024]{1,0:T(8,128)(2,1)S(1)}, bf16[128,1024]{1,0:T(8,128)(2,1)S(1)}, u32[]{:S(2)}, u32[]{:S(2)}) collective-permute-start(bf16[128,1024]{1,0:T(8,128)(2,1)S(1)} %get-tuple-element.503), channel_id=1, source_target_pairs={{0,24},{8,0},{16,8},{24,16},{1,25},{9,1},{17,9},{25,17},{2,26},{10... | collective-permute-start | bytes 786440 | tf_op jit(solution)/shard_map/ppermute | solution.py:881
  327.3 29.3 %collective-permute-start.57 = (bf16[128,1024]{1,0:T(8,128)(2,1)S(1)}, bf16[128,1024]{1,0:T(8,128)(2,1)S(1)}, u32[]{:S(2)}, u32[]{:S(2)}) collective-permute-start(bf16[128,1024]{1,0:T(8,128)(2,1)S(1)} %get-tuple-element.525), channel_id=1, source_target_pairs={{0,8},{8,16},{16,24},{24,0},{1,9},{9,17},{17,25},{25,1},{2,10},{10... | collective-permute-start | bytes 786440 | tf_op jit(solution)/shard_map/ppermute | solution.py:881
  332.0 24.6 %collective-permute-start.58 = (bf16[128,1024]{1,0:T(8,128)(2,1)S(1)}, bf16[128,1024]{1,0:T(8,128)(2,1)S(1)}, u32[]{:S(2)}, u32[]{:S(2)}) collective-permute-start(bf16[128,1024]{1,0:T(8,128)(2,1)S(1)} %get-tuple-element.526), channel_id=1, source_target_pairs={{0,16},{8,24},{16,0},{24,8},{1,17},{9,25},{17,1},{25,9},{2,18},{10... | collective-permute-start | bytes 786440 | tf_op jit(solution)/shard_map/ppermute | solution.py:881
  333.3 23.3 %collective-permute-start.59 = (bf16[128,1024]{1,0:T(8,128)(2,1)S(1)}, bf16[128,1024]{1,0:T(8,128)(2,1)S(1)}, u32[]{:S(2)}, u32[]{:S(2)}) collective-permute-start(bf16[128,1024]{1,0:T(8,128)(2,1)S(1)} %get-tuple-element.527), channel_id=1, source_target_pairs={{0,24},{8,0},{16,8},{24,16},{1,25},{9,1},{17,9},{25,17},{2,26},{10... | collective-permute-start | bytes 786440 | tf_op jit(solution)/shard_map/ppermute | solution.py:881
  334.5 1.2 collective-permute-start.52
  335.7 3.9 %collective-permute-start.53 = (f32[8,1024]{1,0:T(8,128)S(1)}, f32[8,1024]{1,0:T(8,128)S(1)}, u32[]{:S(2)}, u32[]{:S(2)}) collective-permute-start(f32[8,1024]{1,0:T(8,128)S(1)} %add.188), channel_id=1, source_target_pairs={{0,2},{2,0},{1,3},{3,1},{4,6},{6,4},{5,7},{7,5},{8,10},{10,8},{9,1... | collective-permute-start | bytes 98312 | tf_op jit(solution)/shard_map/ppermute | solution.py:1207
  339.6 3.9 %collective-permute-start.54 = (f32[8,1024]{1,0:T(8,128)S(1)}, f32[8,1024]{1,0:T(8,128)S(1)}, u32[]{:S(2)}, u32[]{:S(2)}) collective-permute-start(f32[8,1024]{1,0:T(8,128)S(1)} %add.189), channel_id=1, source_target_pairs={{0,4},{4,0},{1,5},{5,1},{2,6},{6,2},{3,7},{7,3},{8,12},{12,8},{9,1... | collective-permute-start | bytes 98312 | tf_op jit(solution)/shard_map/ppermute | solution.py:1207
  343.5 7.0 %collective-permute-start.55 = (f32[8,1024]{1,0:T(8,128)S(1)}, f32[8,1024]{1,0:T(8,128)S(1)}, u32[]{:S(2)}, u32[]{:S(2)}) collective-permute-start(f32[8,1024]{1,0:T(8,128)S(1)} %add.190), channel_id=1, source_target_pairs={{0,8},{8,0},{16,24},{24,16},{1,9},{9,1},{17,25},{25,17},{2,10},{10... | collective-permute-start | bytes 98312 | tf_op jit(solution)/shard_map/ppermute | solution.py:1207
  350.5 6.0 %collective-permute-start.56 = (f32[8,1024]{1,0:T(8,128)S(1)}, f32[8,1024]{1,0:T(8,128)S(1)}, u32[]{:S(2)}, u32[]{:S(2)}) collective-permute-start(f32[8,1024]{1,0:T(8,128)S(1)} %add.191), channel_id=1, source_target_pairs={{0,16},{8,24},{16,0},{24,8},{1,17},{9,25},{17,1},{25,9},{2,18},{10... | collective-permute-start | bytes 98312 | tf_op jit(solution)/shard_map/ppermute | solution.py:1207
  (83 other events, 991.8 us)
where the time goes:
time: 365 us; the launch traced here: 362 us
  Pallas kernels  130 us (36%)
  waiting for transfers between devices  104 us (28%)
  starting transfers between devices  82.6 us (23%)
  matrix products  17.2 us (5%)
  local copies, waits for them, and re-layouts  15 us (4%)
  between operations  7.96 us (2%)
  other arithmetic  4.69 us (1%)
    pallas_call x42, Pallas kernels, plain_call(): pl.pallas_call(kernel, grid_spec=pltpu.PrefetchScalarGridSpec(num_scalar_...  130 us
    ppermute x46, waiting for transfers between devices, send(): lax.ppermute(value, axis, [(i, (i + step) % size) for i in range(size)])  82.6 us
    ppermute x46, starting transfers between devices, send(): lax.ppermute(value, axis, [(i, (i + step) % size) for i in range(size)])  69.8 us
    dot_general x6, matrix products, dot(): lax.dot_general(left, right, (((left_dim,), (right_dim,)), ((), ())), pre...  17.2 us
    ppermute x5, waiting for transfers between devices, local(): sums = sums + lax.ppermute(sums, axis, pairs)  14.4 us
    unnamed x178, local copies, waits for them, and re-layouts  13.3 us
  transfers between devices with their start and end apart: 60, of which 30 were waited for; matrix products, arithmetic and copies ran while one was open for 6% of the time, Pallas kernels for 29%

commit v1 on v0

--- a/solution.py
+++ b/solution.py
@@ -629,7 +629,7 @@
 
     @pl.when(pl.program_id(0) >= half)
     def _():
-        near_out[...] = piece
+        near_out[...] = piece.astype(bf16)
 
 
 def unproject_call(grads, part, blocks, rows):
@@ -637,7 +637,7 @@
     model, width = part.shape
     return plain_call(
         functools.partial(unproject_kernel, half),
-        (shaped((half * rows, model), bf16), shaped((half * rows, model), f32)),
+        (shaped((half * rows, model), bf16),) * 2,
         grads,
         part,
         grid=(len(blocks),),
@@ -909,7 +909,7 @@
         weight_proj,
         weight_up,
         weight_down,
-        mebibytes=8,
+        mebibytes=56,
         name="pack",
     )
     near_qkv = fetch_z(shard_qkv)
@@ -1166,7 +1166,8 @@
     halves_qkv, sent_one, near_one, pieces_up = tie(halves_qkv, sent_one, near_one, pieces_up)
 
     parts = [
-        near_one[dy * rows : (dy + 1) * rows] + sent_one[dy * rows : (dy + 1) * rows].astype(f32)
+        near_one[dy * rows : (dy + 1) * rows].astype(f32)
+        + sent_one[dy * rows : (dy + 1) * rows].astype(f32)
         for dy in range(n_y)
     ]
     sent_parts = [parts[k].astype(bf16) for k in range(1, n_y)]

time: 365 us -> 361 us (0.989)
    unnamed x178 -> x172, local copies, waits for them, and re-layouts: 13.3 us -> 9.66 us
where the time goes in v1:
time: 361 us; the launch traced here: 358 us
  Pallas kernels  130 us (36%)
  waiting for transfers between devices  104 us (29%)
  starting transfers between devices  82 us (23%)
  matrix products  17.3 us (5%)
  local copies, waits for them, and re-layouts  11.4 us (3%)
  between operations  7.97 us (2%)
  other arithmetic  4.75 us (1%)
    pallas_call x42, Pallas kernels, plain_call(): pl.pallas_call(kernel, grid_spec=pltpu.PrefetchScalarGridSpec(num_scalar_...  130 us
    ppermute x46, waiting for transfers between devices, send(): lax.ppermute(value, axis, [(i, (i + step) % size) for i in range(size)])  83.1 us
    ppermute x46, starting transfers between devices, send(): lax.ppermute(value, axis, [(i, (i + step) % size) for i in range(size)])  69.2 us
    dot_general x6, matrix products, dot(): lax.dot_general(left, right, (((left_dim,), (right_dim,)), ((), ())), pre...  17.3 us
    ppermute x5, waiting for transfers between devices, local(): sums = sums + lax.ppermute(sums, axis, pairs)  14.3 us
    unnamed x172, local copies, waits for them, and re-layouts  9.66 us
  transfers between devices with their start and end apart: 60, of which 30 were waited for; matrix products, arithmetic and copies ran while one was open for 6% of the time, Pallas kernels for 29%

profile of v1, /device:TPU:0, one launch (start us, length us, event | category | flops | bytes accessed | tf_op | source)
XLA Modules:
  0.0 358.1 jit_solution(11644878212314194382)
XLA Ops:
  0.7 2.4 pack.1
  3.0 3.0 collective-permute-start
  6.1 2.6 collective-permute-start.1
  12.5 3.1 collective-permute-done.refs_1_
  15.6 10.4 %collective-permute-done.1.refs_2_ = bf16[128,1024]{1,0:T(8,128)(2,1)S(1)} collective-permute-done((bf16[128,1024]{1,0:T(8,128)(2,1)}, bf16[128,1024]{1,0:T(8,128)(2,1)S(1)}, u32[]{:S(2)}, u32[]{:S(2)}) %collective-permute-start.1) | collective-permute-done | bytes 262176 | tf_op jit(solution)/shard_map/ppermute | solution.py:881
  32.2 6.1 %collective-permute-start.4 = (bf16[144,1024]{1,0:T(8,128)(2,1)S(1)}, bf16[144,1024]{1,0:T(8,128)(2,1)S(1)}, u32[]{:S(2)}, u32[]{:S(2)}) collective-permute-start(bf16[144,1024]{1,0:T(8,128)(2,1)S(1)} %copy-done.68), channel_id=1, source_target_pairs={{0,8},{8,16},{16,24},{24,0},{1,9},{9,17},{17,25},{25,1},{2,10},{10... | collective-permute-start | bytes 884744 | tf_op jit(solution)/shard_map/ppermute | solution.py:881
  38.3 1.6 collective-permute-start.5
  40.6 6.7 %collective-permute-done.4.refs_1_ = bf16[144,1024]{1,0:T(8,128)(2,1)S(1)} collective-permute-done((bf16[144,1024]{1,0:T(8,128)(2,1)S(1)}, bf16[144,1024]{1,0:T(8,128)(2,1)S(1)}, u32[]{:S(2)}, u32[]{:S(2)}) %collective-permute-start.4) | collective-permute-done | bytes 294944 | tf_op jit(solution)/shard_map/ppermute | solution.py:881
  47.4 10.3 %collective-permute-done.5.refs_2_ = bf16[144,1024]{1,0:T(8,128)(2,1)S(1)} collective-permute-done((bf16[144,1024]{1,0:T(8,128)(2,1)S(1)}, bf16[144,1024]{1,0:T(8,128)(2,1)S(1)}, u32[]{:S(2)}, u32[]{:S(2)}) %collective-permute-start.5) | collective-permute-done | bytes 294944 | tf_op jit(solution)/shard_map/ppermute | solution.py:881
  60.2 6.8 %collective-permute-start.11 = (bf16[128,1024]{1,0:T(8,128)(2,1)S(1)}, bf16[128,1024]{1,0:T(8,128)(2,1)S(1)}, u32[]{:S(2)}, u32[]{:S(2)}) collective-permute-start(bf16[128,1024]{1,0:T(8,128)(2,1)S(1)} %copy-done.70), channel_id=1, source_target_pairs={{0,8},{8,16},{16,24},{24,0},{1,9},{9,17},{17,25},{25,1},{2,10},{10... | collective-permute-start | bytes 786440 | tf_op jit(solution)/shard_map/ppermute | solution.py:881
  67.0 2.4 collective-permute-start.12
  71.7 3.8 %convolution_convert_fusion.refs_0_.refs_1_.refs_2_.refs_3_.refs_4_.refs_5_ = bf16[2048,768]{1,0:T(8,128)(2,1)S(1)} fusion(bf16[2048,1024]{1,0:T(8,128)(2,1)S(1)} %place_blocks.1, bf16[1024,768]{1,0:T(8,128)(2,1)S(1)} %get-tuple-element.307.part_ref), kind=kOutput, calls=%fused_computation.2 | convolution fusion | flops 3222798336 | bytes 8912896 | tf_op jit(solution)/shard_map/dot_general | solution.py:66
  75.6 13.8 %attention_forward.1 = (bf16[512,256]{1,0:T(8,128)(2,1)S(1)}, bf16[512,256]{1,0:T(8,128)(2,1)S(1)}, bf16[512,256]{1,0:T(8,128)(2,1)S(1)}, bf16[512,256]{1,0:T(8,128)(2,1)S(1)}, f32[3,8,640]{2,1,0:T(8,128)S(1)}) custom-call(s32[3]{0:T(128)S(1)} %select_reduce_fusion.begin, s32[4]{0:T(128)S(1)} %get-tuple-element.305.spots, ...), custom_call_target="tpu_custom_call" | custom-call | flops 1024 | bytes 1024 | tf_op jit(solution)/shard_map/attention_forward/pallas_call | solution.py:295
  100.0 4.2 %collective-permute-done.17.refs_3_ = bf16[512,256]{1,0:T(8,128)(2,1)S(1)} collective-permute-done((bf16[512,256]{1,0:T(8,128)(2,1)S(1)}, bf16[512,256]{1,0:T(8,128)(2,1)S(1)}, u32[]{:S(2)}, u32[]{:S(2)}) %collective-permute-start.17) | collective-permute-done | bytes 262176 | tf_op jit(solution)/shard_map/ppermute | solution.py:889
  106.4 2.1 proj.1
  110.5 8.9 %up.3 = (bf16[1024,1024]{1,0:T(8,128)(2,1)S(1)}, bf16[1024,1024]{1,0:T(8,128)(2,1)S(1)}, bf16[1024,1024]{1,0:T(8,128)(2,1)S(1)}, bf16[1024,1024]{1,0:T(8,128)(2,1)S(1)}) custom-call(bf16[512,1024]{1,0:T(8,128)(2,1)S(1)} %get-tuple-element.362.low_ref, bf16[1024,1024]{1,0:T(8,128)(2,1)S(1)} %weave.4.refs_0_.refs_2_, ...), custom_call_target="tpu_custom_call" | custom-call | flops 1024 | bytes 1024 | tf_op jit(solution)/shard_map/up/pallas_call | solution.py:295
  119.5 3.6 %collective-permute-done.21.low_ref = bf16[256,1024]{1,0:T(8,128)(2,1)S(1)} collective-permute-done((bf16[256,1024]{1,0:T(8,128)(2,1)S(1)}, bf16[256,1024]{1,0:T(8,128)(2,1)S(1)}, u32[]{:S(2)}, u32[]{:S(2)}) %collective-permute-start.21) | collective-permute-done | bytes 524320 | tf_op jit(solution)/shard_map/ppermute | solution.py:881
  125.5 5.1 %up.4 = (bf16[1024,1024]{1,0:T(8,128)(2,1)S(1)}, bf16[1024,1024]{1,0:T(8,128)(2,1)S(1)}, bf16[1024,1024]{1,0:T(8,128)(2,1)S(1)}, bf16[1024,1024]{1,0:T(8,128)(2,1)S(1)}) custom-call(bf16[256,1024]{1,0:T(8,128)(2,1)S(1)} %collective-permute-done.21.low_ref, ...), custom_call_target="tpu_custom_call", output_to_operand_aliasing={{0}: (3, {}), {1}: (4, {}), {2}: (5, {}), {3}: (6, {})} | custom-call | flops 1024 | bytes 1024 | tf_op jit(solution)/shard_map/up/pallas_call | solution.py:295
  130.6 2.9 wide.6
  133.5 4.7 %collective-permute-done.24.low_ref = bf16[256,1024]{1,0:T(8,128)(2,1)S(1)} collective-permute-done((bf16[256,1024]{1,0:T(8,128)(2,1)S(1)}, bf16[256,1024]{1,0:T(8,128)(2,1)S(1)}, u32[]{:S(2)}, u32[]{:S(2)}) %collective-permute-start.24) | collective-permute-done | bytes 524320 | tf_op jit(solution)/shard_map/ppermute | solution.py:881
  139.8 5.5 %up.5 = (bf16[1024,1024]{1,0:T(8,128)(2,1)S(1)}, bf16[1024,1024]{1,0:T(8,128)(2,1)S(1)}, bf16[1024,1024]{1,0:T(8,128)(2,1)S(1)}, bf16[1024,1024]{1,0:T(8,128)(2,1)S(1)}) custom-call(bf16[256,1024]{1,0:T(8,128)(2,1)S(1)} %collective-permute-done.24.low_ref, ...), custom_call_target="tpu_custom_call", output_to_operand_aliasing={{0}: (3, {}), {1}: (4, {}), {2}: (5, {}), {3}: (6, {})} | custom-call | flops 1024 | bytes 1024 | tf_op jit(solution)/shard_map/up/pallas_call | solution.py:295
  145.3 3.4 wide.7
  149.5 1.6 copy-done.4
  151.1 1.6 copy-done.9
  152.7 1.6 copy-done.12
  154.3 1.6 copy-done.15
  155.9 3.1 wide.8.refs_2_
  159.0 4.4 %collective-permute-done.26.refs_4_ = bf16[256,1024]{1,0:T(8,128)(2,1)} collective-permute-done((bf16[256,1024]{1,0:T(8,128)(2,1)}, bf16[256,1024]{1,0:T(8,128)(2,1)}, u32[]{:S(2)}, u32[]{:S(2)}) %collective-permute-start.26) | collective-permute-done | bytes 524320 | tf_op jit(solution)/shard_map/ppermute | solution.py:881
  163.4 2.5 loss.1
  167.5 4.0 %hidden.3 = (bf16[1024,1024]{1,0:T(8,128)(2,1)S(1)}, bf16[1024,1024]{1,0:T(8,128)(2,1)S(1)}) custom-call(bf16[512,1024]{1,0:T(8,128)(2,1)S(1)} %get-tuple-element.393.low_ref, bf16[1024,1024]{1,0:T(8,128)(2,1)S(1)} %copy-done.18, bf16[1024,1024]{1,0:T(8,128)(2,1)S(1)} %copy-done.20, bf16[1024,1024]{1,0:T(8,128)(2,1)S(1)} %copy-done.5, ...), custom_call_target="tpu_custom_call" | custom-call | flops 1024 | bytes 1024 | tf_op jit(solution)/shard_map/hidden/pallas_call | solution.py:295
  171.5 3.1 wide.9.refs_0_
  174.7 4.4 %collective-permute-done.27.low_ref = bf16[256,1024]{1,0:T(8,128)(2,1)S(1)} collective-permute-done((bf16[256,1024]{1,0:T(8,128)(2,1)S(1)}, bf16[256,1024]{1,0:T(8,128)(2,1)S(1)}, u32[]{:S(2)}, u32[]{:S(2)}) %collective-permute-start.27) | collective-permute-done | bytes 524320 | tf_op jit(solution)/shard_map/ppermute | solution.py:881
  180.4 2.6 hidden.4
  183.0 2.0 wide.10
  185.1 6.1 %collective-permute-done.28.low_ref = bf16[256,1024]{1,0:T(8,128)(2,1)S(1)} collective-permute-done((bf16[256,1024]{1,0:T(8,128)(2,1)S(1)}, bf16[256,1024]{1,0:T(8,128)(2,1)S(1)}, u32[]{:S(2)}, u32[]{:S(2)}) %collective-permute-start.28) | collective-permute-done | bytes 524320 | tf_op jit(solution)/shard_map/ppermute | solution.py:881
  192.4 2.6 hidden.5
  195.0 2.0 wide.11
  197.1 2.5 convolution_convert_fusion.2
  199.5 3.0 collective-permute-done.29.refs_1_
  202.6 2.4 convolution_convert_fusion.1
  206.7 2.5 add_convert_fusion.1.refs_0_
  209.7 2.5 add_convert_fusion.refs_0_
  212.9 1.7 split_x.4
  215.5 4.0 %collective-permute-done.30.refs_2_ = bf16[256,1024]{1,0:T(8,128)(2,1)S(1)} collective-permute-done((bf16[256,1024]{1,0:T(8,128)(2,1)S(1)}, bf16[256,1024]{1,0:T(8,128)(2,1)S(1)}, u32[]{:S(2)}, u32[]{:S(2)}) %collective-permute-start.30) | collective-permute-done | bytes 524320 | tf_op jit(solution)/shard_map/ppermute | solution.py:881
  219.5 2.1 middle.1
  233.1 13.4 %attention_backward.2.refs_7_ = bf16[2048,768]{1,0:T(8,128)(2,1)S(1)} custom-call(s32[3]{0:T(128)S(1)} %copy-done.76, s32[4]{0:T(128)S(1)} %copy-done.78, f32[3,8,640]{2,1,0:T(8,128)S(1)} %get-tuple-element.308.bias_ref, bf16[2048,768]{1,0:T(8,128)(2,1)S(1)} %convolution_convert_fusion.refs_0_.refs_1_.refs_2_.refs_3_.refs_4_.refs_5_, ...), custom_call_target="tpu_custom_call" | custom-call | flops 1024 | bytes 1024 | tf_op jit(solution)/shard_map/attention_backward/pallas_call | solution.py:295
  246.6 5.1 %collective-permute-done.40.refs_1_ = bf16[512,1024]{1,0:T(8,128)(2,1)S(1)} collective-permute-done((bf16[512,1024]{1,0:T(8,128)(2,1)S(1)}, bf16[512,1024]{1,0:T(8,128)(2,1)S(1)}, u32[]{:S(2)}, u32[]{:S(2)}) %collective-permute-start.40) | collective-permute-done | bytes 1048608 | tf_op jit(solution)/shard_map/ppermute | solution.py:881
  257.1 2.9 collective-permute-start.42
  259.9 2.1 collective-permute-start.43
  262.4 16.8 %attention_backward.3.grad_ref = bf16[2048,768]{1,0:T(8,128)(2,1)} custom-call(s32[3]{0:T(128)} %copy-done.75, s32[4]{0:T(128)} %copy-done.77, f32[3,8,640]{2,1,0:T(8,128)} %copy-done.71, bf16[2048,768]{1,0:T(8,128)(2,1)} %copy-done, bf16[2048,768]{1,0:T(8,128)(2,1)} %copy-done, bf16[2048,768]{1,0:T(8,128)(2,1)} %copy-done, ...), custom_call_target="tpu_custom_call", output_to_operand_aliasing={{}: (10, {})} | custom-call | flops 1024 | bytes 1024 | tf_op jit(solution)/shard_map/attention_backward/pallas_call | solution.py:295
  279.4 6.4 %unproject.1 = (bf16[1024,1024]{1,0:T(8,128)(2,1)S(1)}, bf16[1024,1024]{1,0:T(8,128)(2,1)S(1)}) custom-call(s32[4]{0:T(128)S(1)} %pad_add_fusion.3.spots, bf16[2048,768]{1,0:T(8,128)(2,1)} %attention_backward.3.grad_ref, bf16[1024,768]{1,0:T(8,128)(2,1)S(1)} %copy-done.46), custom_call_target="tpu_custom_call" | custom-call | flops 1024 | bytes 1024 | tf_op jit(solution)/shard_map/unproject/pallas_call | solution.py:295
  286.7 3.7 %convolution_convert_fusion.3.refs_0_ = bf16[1024,768]{1,0:T(8,128)(2,1)S(1)} fusion(bf16[2048,1024]{1,0:T(8,128)(2,1)S(1)} %copy-done.35, bf16[2048,768]{1,0:T(8,128)(2,1)S(1)} %copy-done.22), kind=kOutput, calls=%fused_computation.7 | convolution fusion | flops 3222011904 | bytes 8912896 | tf_op jit(solution)/shard_map/dot_general | solution.py:66
  290.4 1.8 split_x.5
  295.4 4.2 %collective-permute-start.49 = (bf16[128,1024]{1,0:T(8,128)(2,1)S(1)}, bf16[128,1024]{1,0:T(8,128)(2,1)S(1)}, u32[]{:S(2)}, u32[]{:S(2)}) collective-permute-start(bf16[128,1024]{1,0:T(8,128)(2,1)S(1)} %get-tuple-element.501), channel_id=1, source_target_pairs={{0,8},{8,16},{16,24},{24,0},{1,9},{9,17},{17,25},{25,1},{2,10},{10... | collective-permute-start | bytes 786440 | tf_op jit(solution)/shard_map/ppermute | solution.py:881
  299.5 1.7 collective-permute-start.50
  301.9 2.7 adam.3
  304.6 3.3 collective-permute-done.49.refs_1_
  307.9 10.5 %collective-permute-done.50.refs_2_ = bf16[128,1024]{1,0:T(8,128)(2,1)S(1)} collective-permute-done((bf16[128,1024]{1,0:T(8,128)(2,1)S(1)}, bf16[128,1024]{1,0:T(8,128)(2,1)S(1)}, u32[]{:S(2)}, u32[]{:S(2)}) %collective-permute-start.50) | collective-permute-done | bytes 262176 | tf_op jit(solution)/shard_map/ppermute | solution.py:881
  320.8 3.1 leave.1
  323.9 4.6 %collective-permute-start.57 = (bf16[128,1024]{1,0:T(8,128)(2,1)S(1)}, bf16[128,1024]{1,0:T(8,128)(2,1)S(1)}, u32[]{:S(2)}, u32[]{:S(2)}) collective-permute-start(bf16[128,1024]{1,0:T(8,128)(2,1)S(1)} %get-tuple-element.525), channel_id=1, source_target_pairs={{0,8},{8,16},{16,24},{24,0},{1,9},{9,17},{17,25},{25,1},{2,10},{10... | collective-permute-start | bytes 786440 | tf_op jit(solution)/shard_map/ppermute | solution.py:881
  333.6 2.6 collective-permute-done.53
  337.2 2.8 collective-permute-done.54
  340.9 6.1 %collective-permute-done.55 = f32[8,1024]{1,0:T(8,128)S(1)} collective-permute-done((f32[8,1024]{1,0:T(8,128)S(1)}, f32[8,1024]{1,0:T(8,128)S(1)}, u32[]{:S(2)}, u32[]{:S(2)}) %collective-permute-start.55) | collective-permute-done | bytes 32800 | tf_op jit(solution)/shard_map/ppermute | solution.py:1208
  347.1 3.1 collective-permute-start.56
  (300 shorter events, 76.2 us)
Async XLA Ops:
  3.0 12.5 %collective-permute-start = (bf16[128,1024]{1,0:T(8,128)(2,1)}, bf16[128,1024]{1,0:T(8,128)(2,1)S(1)}, u32[]{:S(2)}, u32[]{:S(2)}) collective-permute-start(bf16[128,1024]{1,0:T(8,128)(2,1)} %get-tuple-element.285.refs_0_), channel_id=1, source_target_pairs={{0,8},{8,16},{16,24},{24,0},{1,9},{9,17},{17,25},{25,1},{2,10},{10... | collective-permute-start | bytes 786440 | tf_op jit(solution)/shard_map/ppermute | solution.py:881
  6.1 19.9 %collective-permute-start.1 = (bf16[128,1024]{1,0:T(8,128)(2,1)}, bf16[128,1024]{1,0:T(8,128)(2,1)S(1)}, u32[]{:S(2)}, u32[]{:S(2)}) collective-permute-start(bf16[128,1024]{1,0:T(8,128)(2,1)} %get-tuple-element.285.refs_0_), channel_id=1, source_target_pairs={{0,16},{8,24},{16,0},{24,8},{1,17},{9,25},{17,1},{25,9},{2,18},{10... | collective-permute-start | bytes 786440 | tf_op jit(solution)/shard_map/ppermute | solution.py:881
  8.7 17.3 %collective-permute-start.2 = (bf16[128,1024]{1,0:T(8,128)(2,1)}, bf16[128,1024]{1,0:T(8,128)(2,1)S(1)}, u32[]{:S(2)}, u32[]{:S(2)}) collective-permute-start(bf16[128,1024]{1,0:T(8,128)(2,1)} %get-tuple-element.285.refs_0_), channel_id=1, source_target_pairs={{0,24},{8,0},{16,8},{24,16},{1,25},{9,1},{17,9},{25,17},{2,26},{10... | collective-permute-start | bytes 786440 | tf_op jit(solution)/shard_map/ppermute | solution.py:881
  10.8 64.7 %copy-start.75 = (s32[3]{0:T(128)}, s32[3]{0:T(128)S(1)}, u32[]{:S(2)}) copy-start(s32[3]{0:T(128)S(1)} %select_reduce_fusion.begin) | copy-start | bytes 40
  11.7 63.9 %copy-start.77 = (s32[4]{0:T(128)}, s32[4]{0:T(128)S(1)}, u32[]{:S(2)}) copy-start(s32[4]{0:T(128)S(1)} %get-tuple-element.305.spots) | copy-start | bytes 52
  28.0 29.7 %collective-permute-start.3 = (bf16[512,1024]{1,0:T(8,128)(2,1)S(1)}, bf16[512,1024]{1,0:T(8,128)(2,1)S(1)}, u32[]{:S(2)}, u32[]{:S(2)}) collective-permute-start(bf16[512,1024]{1,0:T(8,128)(2,1)S(1)} %stack_z.3.refs_0_), channel_id=1, source_target_pairs={{0,4},{4,0},{1,5},{5,1},{2,6},{6,2},{3,7},{7,3},{8,12},{12,8},{9,1... | collective-permute-start | bytes 3145736 | tf_op jit(solution)/shard_map/ppermute | solution.py:881
  30.6 27.1 %collective-permute-start.7 = (bf16[512,1024]{1,0:T(8,128)(2,1)S(1)}, bf16[512,1024]{1,0:T(8,128)(2,1)S(1)}, u32[]{:S(2)}, u32[]{:S(2)}) collective-permute-start(bf16[512,1024]{1,0:T(8,128)(2,1)S(1)} %first.1.refs_0_), channel_id=1, source_target_pairs={{0,2},{2,0},{1,3},{3,1},{4,6},{6,4},{5,7},{7,5},{8,10},{10,8},{9,1... | collective-permute-start | bytes 3145736 | tf_op jit(solution)/shard_map/ppermute | solution.py:881
  32.2 15.2 %collective-permute-start.4 = (bf16[144,1024]{1,0:T(8,128)(2,1)S(1)}, bf16[144,1024]{1,0:T(8,128)(2,1)S(1)}, u32[]{:S(2)}, u32[]{:S(2)}) collective-permute-start(bf16[144,1024]{1,0:T(8,128)(2,1)S(1)} %copy-done.68), channel_id=1, source_target_pairs={{0,8},{8,16},{16,24},{24,0},{1,9},{9,17},{17,25},{25,1},{2,10},{10... | collective-permute-start | bytes 884744 | tf_op jit(solution)/shard_map/ppermute | solution.py:881
  38.3 19.4 %collective-permute-start.5 = (bf16[144,1024]{1,0:T(8,128)(2,1)S(1)}, bf16[144,1024]{1,0:T(8,128)(2,1)S(1)}, u32[]{:S(2)}, u32[]{:S(2)}) collective-permute-start(bf16[144,1024]{1,0:T(8,128)(2,1)S(1)} %copy-done.68), channel_id=1, source_target_pairs={{0,16},{8,24},{16,0},{24,8},{1,17},{9,25},{17,1},{25,9},{2,18},{10... | collective-permute-start | bytes 884744 | tf_op jit(solution)/shard_map/ppermute | solution.py:881
  39.9 17.8 %collective-permute-start.6 = (bf16[144,1024]{1,0:T(8,128)(2,1)S(1)}, bf16[144,1024]{1,0:T(8,128)(2,1)S(1)}, u32[]{:S(2)}, u32[]{:S(2)}) collective-permute-start(bf16[144,1024]{1,0:T(8,128)(2,1)S(1)} %copy-done.68), channel_id=1, source_target_pairs={{0,24},{8,0},{16,8},{24,16},{1,25},{9,1},{17,9},{25,17},{2,26},{10... | collective-permute-start | bytes 884744 | tf_op jit(solution)/shard_map/ppermute | solution.py:881
  59.1 10.3 %collective-permute-start.8 = (bf16[512,1024]{1,0:T(8,128)(2,1)S(1)}, bf16[512,1024]{1,0:T(8,128)(2,1)S(1)}, u32[]{:S(2)}, u32[]{:S(2)}) collective-permute-start(bf16[512,1024]{1,0:T(8,128)(2,1)S(1)} %first.1.refs_0_), channel_id=1, source_target_pairs={{0,1},{1,0},{2,3},{3,2},{4,5},{5,4},{6,7},{7,6},{8,9},{9,8},{10,11... | collective-permute-start | bytes 3145736 | tf_op jit(solution)/shard_map/ppermute | solution.py:881
  59.2 11.2 %collective-permute-start.9 = (bf16[512,1024]{1,0:T(8,128)(2,1)S(1)}, bf16[512,1024]{1,0:T(8,128)(2,1)S(1)}, u32[]{:S(2)}, u32[]{:S(2)}) collective-permute-start(bf16[512,1024]{1,0:T(8,128)(2,1)S(1)} %collective-permute-done.7.refs_1_), channel_id=1, source_target_pairs={{0,1},{1,0},{2,3},{3,2},{4,5},{5,4},{6,7},{7,6},{8,9},{9,8},{10,11... | collective-permute-start | bytes 3145736 | tf_op jit(solution)/shard_map/ppermute | solution.py:881
  59.7 29.8 %collective-permute-start.10 = (bf16[528,1024]{1,0:T(8,128)(2,1)S(1)}, bf16[528,1024]{1,0:T(8,128)(2,1)S(1)}, u32[]{:S(2)}, u32[]{:S(2)}) collective-permute-start(bf16[528,1024]{1,0:T(8,128)(2,1)S(1)} %stack_z.4.refs_0_), channel_id=1, source_target_pairs={{0,4},{4,0},{1,5},{5,1},{2,6},{6,2},{3,7},{7,3},{8,12},{12,8},{9,1... | collective-permute-start | bytes 3244040 | tf_op jit(solution)/shard_map/ppermute | solution.py:881
  60.2 29.2 %collective-permute-start.11 = (bf16[128,1024]{1,0:T(8,128)(2,1)S(1)}, bf16[128,1024]{1,0:T(8,128)(2,1)S(1)}, u32[]{:S(2)}, u32[]{:S(2)}) collective-permute-start(bf16[128,1024]{1,0:T(8,128)(2,1)S(1)} %copy-done.70), channel_id=1, source_target_pairs={{0,8},{8,16},{16,24},{24,0},{1,9},{9,17},{17,25},{25,1},{2,10},{10... | collective-permute-start | bytes 786440 | tf_op jit(solution)/shard_map/ppermute | solution.py:881
  67.0 22.5 %collective-permute-start.12 = (bf16[128,1024]{1,0:T(8,128)(2,1)S(1)}, bf16[128,1024]{1,0:T(8,128)(2,1)S(1)}, u32[]{:S(2)}, u32[]{:S(2)}) collective-permute-start(bf16[128,1024]{1,0:T(8,128)(2,1)S(1)} %copy-done.70), channel_id=1, source_target_pairs={{0,16},{8,24},{16,0},{24,8},{1,17},{9,25},{17,1},{25,9},{2,18},{10... | collective-permute-start | bytes 786440 | tf_op jit(solution)/shard_map/ppermute | solution.py:881
  69.3 20.1 %collective-permute-start.13 = (bf16[128,1024]{1,0:T(8,128)(2,1)S(1)}, bf16[128,1024]{1,0:T(8,128)(2,1)S(1)}, u32[]{:S(2)}, u32[]{:S(2)}) collective-permute-start(bf16[128,1024]{1,0:T(8,128)(2,1)S(1)} %copy-done.70), channel_id=1, source_target_pairs={{0,24},{8,0},{16,8},{24,16},{1,25},{9,1},{17,9},{25,17},{2,26},{10... | collective-permute-start | bytes 786440 | tf_op jit(solution)/shard_map/ppermute | solution.py:881
  70.4 19.1 %collective-permute-start.14 = (bf16[1024,256]{1,0:T(8,128)(2,1)S(1)}, bf16[1024,256]{1,0:T(8,128)(2,1)S(1)}, u32[]{:S(2)}, u32[]{:S(2)}) collective-permute-start(bf16[1024,256]{1,0:T(8,128)(2,1)S(1)} %get-tuple-element.320.refs_0_), channel_id=1, source_target_pairs={{0,2},{2,0},{1,3},{3,1},{4,6},{6,4},{5,7},{7,5},{8,10},{10,8},{9,1... | collective-permute-start | bytes 1572872 | tf_op jit(solution)/shard_map/ppermute | solution.py:881
  75.6 157.5 %copy-start = (bf16[2048,768]{1,0:T(8,128)(2,1)}, bf16[2048,768]{1,0:T(8,128)(2,1)S(1)}, u32[]{:S(2)}) copy-start(bf16[2048,768]{1,0:T(8,128)(2,1)S(1)} %convolution_convert_fusion.refs_0_.refs_1_.refs_2_.refs_3_.refs_4_.refs_5_) | copy-start | bytes 9437188
  89.4 143.6 %copy-start.71 = (f32[3,8,640]{2,1,0:T(8,128)}, f32[3,8,640]{2,1,0:T(8,128)S(1)}, u32[]{:S(2)}) copy-start(f32[3,8,640]{2,1,0:T(8,128)S(1)} %get-tuple-element.308.bias_ref) | copy-start | bytes 184324
  89.6 15.2 %collective-permute-start.18 = (bf16[1024,512]{1,0:T(8,128)(2,1)S(1)}, bf16[1024,512]{1,0:T(8,128)(2,1)S(1)}, u32[]{:S(2)}, u32[]{:S(2)}) collective-permute-start(bf16[1024,512]{1,0:T(8,128)(2,1)S(1)} %beside.1.refs_4_.refs_0_), channel_id=1, source_target_pairs={{0,1},{1,0},{2,3},{3,2},{4,5},{5,4},{6,7},{7,6},{8,9},{9,8},{10,11... | collective-permute-start | bytes 3145736 | tf_op jit(solution)/shard_map/ppermute | solution.py:881
  90.4 14.4 %collective-permute-start.19 = (bf16[256,1024]{1,0:T(8,128)(2,1)S(1)}, bf16[256,1024]{1,0:T(8,128)(2,1)S(1)}, u32[]{:S(2)}, u32[]{:S(2)}) collective-permute-start(bf16[256,1024]{1,0:T(8,128)(2,1)S(1)} %get-tuple-element.356.refs_0_), channel_id=1, source_target_pairs={{0,4},{4,0},{1,5},{5,1},{2,6},{6,2},{3,7},{7,3},{8,12},{12,8},{9,1... | collective-permute-start | bytes 1572872 | tf_op jit(solution)/shard_map/ppermute | solution.py:881
  90.9 9.1 %collective-permute-start.15 = (bf16[512,256]{1,0:T(8,128)(2,1)S(1)}, bf16[512,256]{1,0:T(8,128)(2,1)S(1)}, u32[]{:S(2)}, u32[]{:S(2)}) collective-permute-start(bf16[512,256]{1,0:T(8,128)(2,1)S(1)} %get-tuple-element.317), channel_id=1, source_target_pairs={{0,2},{1,3},{2,0},{3,1},{4,6},{5,7},{6,4},{7,5},{8,10},{9,11},{10,... | collective-permute-start | bytes 786440 | tf_op jit(solution)/shard_map/ppermute | solution.py:889
  92.4 7.6 %collective-permute-start.16 = (bf16[512,256]{1,0:T(8,128)(2,1)S(1)}, bf16[512,256]{1,0:T(8,128)(2,1)S(1)}, u32[]{:S(2)}, u32[]{:S(2)}) collective-permute-start(bf16[512,256]{1,0:T(8,128)(2,1)S(1)} %get-tuple-element.318), channel_id=1, source_target_pairs={{0,1},{1,0},{2,3},{3,2},{4,5},{5,4},{6,7},{7,6},{8,9},{9,8},{10,11... | collective-permute-start | bytes 786440 | tf_op jit(solution)/shard_map/ppermute | solution.py:889
  92.4 11.8 %collective-permute-start.17 = (bf16[512,256]{1,0:T(8,128)(2,1)S(1)}, bf16[512,256]{1,0:T(8,128)(2,1)S(1)}, u32[]{:S(2)}, u32[]{:S(2)}) collective-permute-start(bf16[512,256]{1,0:T(8,128)(2,1)S(1)} %get-tuple-element.319), channel_id=1, source_target_pairs={{0,3},{1,2},{2,1},{3,0},{4,7},{5,6},{6,5},{7,4},{8,11},{9,10},{10,... | collective-permute-start | bytes 786440 | tf_op jit(solution)/shard_map/ppermute | solution.py:889
  104.8 4.2 %collective-permute-start.20 = (bf16[1024,1024]{1,0:T(8,128)(2,1)S(1)}, bf16[1024,1024]{1,0:T(8,128)(2,1)S(1)}, u32[]{:S(2)}, u32[]{:S(2)}) collective-permute-start(bf16[1024,1024]{1,0:T(8,128)(2,1)S(1)} %weave.4.refs_0_.refs_2_), channel_id=1, source_target_pairs={{0,1},{1,0},{2,3},{3,2},{4,5},{5,4},{6,7},{7,6},{8,9},{9,8},{10,11... | collective-permute-start | bytes 6291464 | tf_op jit(solution)/shard_map/ppermute | solution.py:881
  105.0 14.5 %collective-permute-start.22 = (bf16[256,1024]{1,0:T(8,128)(2,1)S(1)}, bf16[256,1024]{1,0:T(8,128)(2,1)S(1)}, u32[]{:S(2)}, u32[]{:S(2)}) collective-permute-start(bf16[256,1024]{1,0:T(8,128)(2,1)S(1)} %get-tuple-element.357.refs_1_), channel_id=1, source_target_pairs={{0,4},{4,0},{1,5},{5,1},{2,6},{6,2},{3,7},{7,3},{8,12},{12,8},{9,1... | collective-permute-start | bytes 1572872 | tf_op jit(solution)/shard_map/ppermute | solution.py:881
  109.0 14.1 %collective-permute-start.21 = (bf16[256,1024]{1,0:T(8,128)(2,1)S(1)}, bf16[256,1024]{1,0:T(8,128)(2,1)S(1)}, u32[]{:S(2)}, u32[]{:S(2)}) collective-permute-start(bf16[256,1024]{1,0:T(8,128)(2,1)S(1)} %slice.54), channel_id=1, source_target_pairs={{0,2},{2,0},{1,3},{3,1},{4,6},{6,4},{5,7},{7,5},{8,10},{10,8},{9,1... | collective-permute-start | bytes 1572872 | tf_op jit(solution)/shard_map/ppermute | solution.py:881
  123.8 6.8 %collective-permute-start.23 = (bf16[1024,1024]{1,0:T(8,128)(2,1)S(1)}, bf16[1024,1024]{1,0:T(8,128)(2,1)S(1)}, u32[]{:S(2)}, u32[]{:S(2)}) collective-permute-start(bf16[1024,1024]{1,0:T(8,128)(2,1)S(1)} %weave.5.refs_2_), channel_id=1, source_target_pairs={{0,1},{1,0},{2,3},{3,2},{4,5},{5,4},{6,7},{7,6},{8,9},{9,8},{10,11... | collective-permute-start | bytes 6291464 | tf_op jit(solution)/shard_map/ppermute | solution.py:881
  123.9 14.4 %collective-permute-start.24 = (bf16[256,1024]{1,0:T(8,128)(2,1)S(1)}, bf16[256,1024]{1,0:T(8,128)(2,1)S(1)}, u32[]{:S(2)}, u32[]{:S(2)}) collective-permute-start(bf16[256,1024]{1,0:T(8,128)(2,1)S(1)} %slice.55), channel_id=1, source_target_pairs={{0,2},{2,0},{1,3},{3,1},{4,6},{6,4},{5,7},{7,5},{8,10},{10,8},{9,1... | collective-permute-start | bytes 1572872 | tf_op jit(solution)/shard_map/ppermute | solution.py:881
  138.3 20.7 %collective-permute-start.25 = (bf16[256,1024]{1,0:T(8,128)(2,1)}, bf16[256,1024]{1,0:T(8,128)(2,1)}, u32[]{:S(2)}, u32[]{:S(2)}) collective-permute-start(bf16[256,1024]{1,0:T(8,128)(2,1)} %wide.6), channel_id=1, source_target_pairs={{0,2},{2,0},{1,3},{3,1},{4,6},{6,4},{5,7},{7,5},{8,10},{10,8},{9,1... | collective-permute-start | bytes 1572872 | tf_op jit(solution)/shard_map/ppermute | solution.py:881
  148.8 14.6 %collective-permute-start.26 = (bf16[256,1024]{1,0:T(8,128)(2,1)}, bf16[256,1024]{1,0:T(8,128)(2,1)}, u32[]{:S(2)}, u32[]{:S(2)}) collective-permute-start(bf16[256,1024]{1,0:T(8,128)(2,1)} %wide.7), channel_id=1, source_target_pairs={{0,2},{2,0},{1,3},{3,1},{4,6},{6,4},{5,7},{7,5},{8,10},{10,8},{9,1... | collective-permute-start | bytes 1572872 | tf_op jit(solution)/shard_map/ppermute | solution.py:881
  165.9 13.1 %collective-permute-start.27 = (bf16[256,1024]{1,0:T(8,128)(2,1)S(1)}, bf16[256,1024]{1,0:T(8,128)(2,1)S(1)}, u32[]{:S(2)}, u32[]{:S(2)}) collective-permute-start(bf16[256,1024]{1,0:T(8,128)(2,1)S(1)} %slice.56), channel_id=1, source_target_pairs={{0,2},{2,0},{1,3},{3,1},{4,6},{6,4},{5,7},{7,5},{8,10},{10,8},{9,1... | collective-permute-start | bytes 1572872 | tf_op jit(solution)/shard_map/ppermute | solution.py:881
  179.1 12.2 %collective-permute-start.28 = (bf16[256,1024]{1,0:T(8,128)(2,1)S(1)}, bf16[256,1024]{1,0:T(8,128)(2,1)S(1)}, u32[]{:S(2)}, u32[]{:S(2)}) collective-permute-start(bf16[256,1024]{1,0:T(8,128)(2,1)S(1)} %slice.57), channel_id=1, source_target_pairs={{0,2},{2,0},{1,3},{3,1},{4,6},{6,4},{5,7},{7,5},{8,10},{10,8},{9,1... | collective-permute-start | bytes 1572872 | tf_op jit(solution)/shard_map/ppermute | solution.py:881
  191.3 11.2 %collective-permute-start.29 = (bf16[256,1024]{1,0:T(8,128)(2,1)S(1)}, bf16[256,1024]{1,0:T(8,128)(2,1)S(1)}, u32[]{:S(2)}, u32[]{:S(2)}) collective-permute-start(bf16[256,1024]{1,0:T(8,128)(2,1)S(1)} %wide.10), channel_id=1, source_target_pairs={{0,2},{2,0},{1,3},{3,1},{4,6},{6,4},{5,7},{7,5},{8,10},{10,8},{9,1... | collective-permute-start | bytes 1572872 | tf_op jit(solution)/shard_map/ppermute | solution.py:881
  202.5 4.2 %collective-permute-start.31 = (bf16[1024,1024]{1,0:T(8,128)(2,1)S(1)}, bf16[1024,1024]{1,0:T(8,128)(2,1)S(1)}, u32[]{:S(2)}, u32[]{:S(2)}) collective-permute-start(bf16[1024,1024]{1,0:T(8,128)(2,1)S(1)} %convolution_convert_fusion.2), channel_id=1, source_target_pairs={{0,1},{1,0},{2,3},{3,2},{4,5},{5,4},{6,7},{7,6},{8,9},{9,8},{10,11... | collective-permute-start | bytes 6291464 | tf_op jit(solution)/shard_map/ppermute | solution.py:881
  205.0 4.7 %collective-permute-start.32 = (bf16[1024,1024]{1,0:T(8,128)(2,1)S(1)}, bf16[1024,1024]{1,0:T(8,128)(2,1)S(1)}, u32[]{:S(2)}, u32[]{:S(2)}) collective-permute-start(bf16[1024,1024]{1,0:T(8,128)(2,1)S(1)} %convolution_convert_fusion.1), channel_id=1, source_target_pairs={{0,1},{1,0},{2,3},{3,2},{4,5},{5,4},{6,7},{7,6},{8,9},{9,8},{10,11... | collective-permute-start | bytes 6291464 | tf_op jit(solution)/shard_map/ppermute | solution.py:881
  205.6 13.9 %collective-permute-start.30 = (bf16[256,1024]{1,0:T(8,128)(2,1)S(1)}, bf16[256,1024]{1,0:T(8,128)(2,1)S(1)}, u32[]{:S(2)}, u32[]{:S(2)}) collective-permute-start(bf16[256,1024]{1,0:T(8,128)(2,1)S(1)} %wide.11), channel_id=1, source_target_pairs={{0,2},{2,0},{1,3},{3,1},{4,6},{6,4},{5,7},{7,5},{8,10},{10,8},{9,1... | collective-permute-start | bytes 1572872 | tf_op jit(solution)/shard_map/ppermute | solution.py:881
  222.9 6.3 %collective-permute-start.33 = (bf16[512,128]{1,0:T(8,128)(2,1)S(1)}, bf16[512,128]{1,0:T(8,128)(2,1)S(1)}, u32[]{:S(2)}, u32[]{:S(2)}) collective-permute-start(bf16[512,128]{1,0:T(8,128)(2,1)S(1)} %get-tuple-element.427), channel_id=1, source_target_pairs={{0,2},{1,3},{2,0},{3,1},{4,6},{5,7},{6,4},{7,5},{8,10},{9,11},{10,... | collective-permute-start | bytes 393224 | tf_op jit(solution)/shard_map/ppermute | solution.py:889
  223.7 5.6 %collective-permute-start.34 = (bf16[512,128]{1,0:T(8,128)(2,1)S(1)}, bf16[512,128]{1,0:T(8,128)(2,1)S(1)}, u32[]{:S(2)}, u32[]{:S(2)}) collective-permute-start(bf16[512,128]{1,0:T(8,128)(2,1)S(1)} %get-tuple-element.428), channel_id=1, source_target_pairs={{0,1},{1,0},{2,3},{3,2},{4,5},{5,4},{6,7},{7,6},{8,9},{9,8},{10,11... | collective-permute-start | bytes 393224 | tf_op jit(solution)/shard_map/ppermute | solution.py:889
  223.7 5.8 %collective-permute-start.35 = (bf16[512,128]{1,0:T(8,128)(2,1)S(1)}, bf16[512,128]{1,0:T(8,128)(2,1)S(1)}, u32[]{:S(2)}, u32[]{:S(2)}) collective-permute-start(bf16[512,128]{1,0:T(8,128)(2,1)S(1)} %get-tuple-element.429), channel_id=1, source_target_pairs={{0,3},{1,2},{2,1},{3,0},{4,7},{5,6},{6,5},{7,4},{8,11},{9,10},{10,... | collective-permute-start | bytes 393224 | tf_op jit(solution)/shard_map/ppermute | solution.py:889
  226.5 25.1 %collective-permute-start.40 = (bf16[512,1024]{1,0:T(8,128)(2,1)S(1)}, bf16[512,1024]{1,0:T(8,128)(2,1)S(1)}, u32[]{:S(2)}, u32[]{:S(2)}) collective-permute-start(bf16[512,1024]{1,0:T(8,128)(2,1)S(1)} %get-tuple-element.444), channel_id=1, source_target_pairs={{0,4},{4,0},{1,5},{5,1},{2,6},{6,2},{3,7},{7,3},{8,12},{12,8},{9,1... | collective-permute-start | bytes 3145736 | tf_op jit(solution)/shard_map/ppermute | solution.py:881
  229.5 22.1 %collective-permute-start.39 = (bf16[1024,512]{1,0:T(8,128)(2,1)S(1)}, bf16[1024,512]{1,0:T(8,128)(2,1)S(1)}, u32[]{:S(2)}, u32[]{:S(2)}) collective-permute-start(bf16[1024,512]{1,0:T(8,128)(2,1)S(1)} %get-tuple-element.442), channel_id=1, source_target_pairs={{0,1},{1,0},{2,3},{3,2},{4,5},{5,4},{6,7},{7,6},{8,9},{9,8},{10,11... | collective-permute-start | bytes 3145736 | tf_op jit(solution)/shard_map/ppermute | solution.py:881
  230.9 15.6 %collective-permute-start.36 = (bf16[512,128]{1,0:T(8,128)(2,1)S(1)}, bf16[512,128]{1,0:T(8,128)(2,1)S(1)}, u32[]{:S(2)}, u32[]{:S(2)}) collective-permute-start(bf16[512,128]{1,0:T(8,128)(2,1)S(1)} %get-tuple-element.439), channel_id=1, source_target_pairs={{0,2},{1,3},{2,0},{3,1},{4,6},{5,7},{6,4},{7,5},{8,10},{9,11},{10,... | collective-permute-start | bytes 393224 | tf_op jit(solution)/shard_map/ppermute | solution.py:889
  231.6 14.9 %collective-permute-start.37 = (bf16[512,128]{1,0:T(8,128)(2,1)S(1)}, bf16[512,128]{1,0:T(8,128)(2,1)S(1)}, u32[]{:S(2)}, u32[]{:S(2)}) collective-permute-start(bf16[512,128]{1,0:T(8,128)(2,1)S(1)} %get-tuple-element.440), channel_id=1, source_target_pairs={{0,1},{1,0},{2,3},{3,2},{4,5},{5,4},{6,7},{7,6},{8,9},{9,8},{10,11... | collective-permute-start | bytes 393224 | tf_op jit(solution)/shard_map/ppermute | solution.py:889
  231.6 14.9 %collective-permute-start.38 = (bf16[512,128]{1,0:T(8,128)(2,1)S(1)}, bf16[512,128]{1,0:T(8,128)(2,1)S(1)}, u32[]{:S(2)}, u32[]{:S(2)}) collective-permute-start(bf16[512,128]{1,0:T(8,128)(2,1)S(1)} %get-tuple-element.441), channel_id=1, source_target_pairs={{0,3},{1,2},{2,1},{3,0},{4,7},{5,6},{6,5},{7,4},{8,11},{9,10},{10,... | collective-permute-start | bytes 393224 | tf_op jit(solution)/shard_map/ppermute | solution.py:889
  254.9 24.4 %collective-permute-start.41 = (bf16[512,1024]{1,0:T(8,128)(2,1)}, bf16[512,1024]{1,0:T(8,128)(2,1)S(1)}, u32[]{:S(2)}, u32[]{:S(2)}) collective-permute-start(bf16[512,1024]{1,0:T(8,128)(2,1)} %get-tuple-element.467), channel_id=1, source_target_pairs={{0,4},{4,0},{1,5},{5,1},{2,6},{6,2},{3,7},{7,3},{8,12},{12,8},{9,1... | collective-permute-start | bytes 3145736 | tf_op jit(solution)/shard_map/ppermute | solution.py:881
  256.4 22.8 %collective-permute-start.45 = (bf16[1024,256]{1,0:T(8,128)(2,1)}, bf16[1024,256]{1,0:T(8,128)(2,1)}, u32[]{:S(2)}, u32[]{:S(2)}) collective-permute-start(bf16[1024,256]{1,0:T(8,128)(2,1)} %get-tuple-element.473), channel_id=1, source_target_pairs={{0,2},{2,0},{1,3},{3,1},{4,6},{6,4},{5,7},{7,5},{8,10},{10,8},{9,1... | collective-permute-start | bytes 1572872 | tf_op jit(solution)/shard_map/ppermute | solution.py:881
  257.1 22.1 %collective-permute-start.42 = (bf16[128,1024]{1,0:T(8,128)(2,1)}, bf16[128,1024]{1,0:T(8,128)(2,1)S(1)}, u32[]{:S(2)}, u32[]{:S(2)}) collective-permute-start(bf16[128,1024]{1,0:T(8,128)(2,1)} %get-tuple-element.469), channel_id=1, source_target_pairs={{0,8},{8,16},{16,24},{24,0},{1,9},{9,17},{17,25},{25,1},{2,10},{10... | collective-permute-start | bytes 786440 | tf_op jit(solution)/shard_map/ppermute | solution.py:881
  259.9 19.2 %collective-permute-start.43 = (bf16[128,1024]{1,0:T(8,128)(2,1)}, bf16[128,1024]{1,0:T(8,128)(2,1)}, u32[]{:S(2)}, u32[]{:S(2)}) collective-permute-start(bf16[128,1024]{1,0:T(8,128)(2,1)} %get-tuple-element.470), channel_id=1, source_target_pairs={{0,16},{8,24},{16,0},{24,8},{1,17},{9,25},{17,1},{25,9},{2,18},{10... | collective-permute-start | bytes 786440 | tf_op jit(solution)/shard_map/ppermute | solution.py:881
  262.1 17.1 %collective-permute-start.44 = (bf16[128,1024]{1,0:T(8,128)(2,1)}, bf16[128,1024]{1,0:T(8,128)(2,1)}, u32[]{:S(2)}, u32[]{:S(2)}) collective-permute-start(bf16[128,1024]{1,0:T(8,128)(2,1)} %get-tuple-element.471), channel_id=1, source_target_pairs={{0,24},{8,0},{16,8},{24,16},{1,25},{9,1},{17,9},{25,17},{2,26},{10... | collective-permute-start | bytes 786440 | tf_op jit(solution)/shard_map/ppermute | solution.py:881
  285.8 6.4 %collective-permute-start.46 = (bf16[1024,1024]{1,0:T(8,128)(2,1)S(1)}, bf16[1024,1024]{1,0:T(8,128)(2,1)S(1)}, u32[]{:S(2)}, u32[]{:S(2)}) collective-permute-start(bf16[1024,1024]{1,0:T(8,128)(2,1)S(1)} %get-tuple-element.481), channel_id=1, source_target_pairs={{0,1},{1,0},{2,3},{3,2},{4,5},{5,4},{6,7},{7,6},{8,9},{9,8},{10,11... | collective-permute-start | bytes 6291464 | tf_op jit(solution)/shard_map/ppermute | solution.py:881
  293.2 25.6 %collective-permute-start.47 = (bf16[512,1024]{1,0:T(8,128)(2,1)S(1)}, bf16[512,1024]{1,0:T(8,128)(2,1)S(1)}, u32[]{:S(2)}, u32[]{:S(2)}) collective-permute-start(bf16[512,1024]{1,0:T(8,128)(2,1)S(1)} %get-tuple-element.498), channel_id=1, source_target_pairs={{0,4},{4,0},{1,5},{5,1},{2,6},{6,2},{3,7},{7,3},{8,12},{12,8},{9,1... | collective-permute-start | bytes 3145736 | tf_op jit(solution)/shard_map/ppermute | solution.py:881
  294.7 25.3 %collective-permute-start.48 = (bf16[512,1024]{1,0:T(8,128)(2,1)S(1)}, bf16[512,1024]{1,0:T(8,128)(2,1)S(1)}, u32[]{:S(2)}, u32[]{:S(2)}) collective-permute-start(bf16[512,1024]{1,0:T(8,128)(2,1)S(1)} %get-tuple-element.499), channel_id=1, source_target_pairs={{0,2},{2,0},{1,3},{3,1},{4,6},{6,4},{5,7},{7,5},{8,10},{10,8},{9,1... | collective-permute-start | bytes 3145736 | tf_op jit(solution)/shard_map/ppermute | solution.py:881
  295.4 12.6 %collective-permute-start.49 = (bf16[128,1024]{1,0:T(8,128)(2,1)S(1)}, bf16[128,1024]{1,0:T(8,128)(2,1)S(1)}, u32[]{:S(2)}, u32[]{:S(2)}) collective-permute-start(bf16[128,1024]{1,0:T(8,128)(2,1)S(1)} %get-tuple-element.501), channel_id=1, source_target_pairs={{0,8},{8,16},{16,24},{24,0},{1,9},{9,17},{17,25},{25,1},{2,10},{10... | collective-permute-start | bytes 786440 | tf_op jit(solution)/shard_map/ppermute | solution.py:881
  299.5 18.9 %collective-permute-start.50 = (bf16[128,1024]{1,0:T(8,128)(2,1)S(1)}, bf16[128,1024]{1,0:T(8,128)(2,1)S(1)}, u32[]{:S(2)}, u32[]{:S(2)}) collective-permute-start(bf16[128,1024]{1,0:T(8,128)(2,1)S(1)} %get-tuple-element.502), channel_id=1, source_target_pairs={{0,16},{8,24},{16,0},{24,8},{1,17},{9,25},{17,1},{25,9},{2,18},{10... | collective-permute-start | bytes 786440 | tf_op jit(solution)/shard_map/ppermute | solution.py:881
  301.2 17.2 %collective-permute-start.51 = (bf16[128,1024]{1,0:T(8,128)(2,1)S(1)}, bf16[128,1024]{1,0:T(8,128)(2,1)S(1)}, u32[]{:S(2)}, u32[]{:S(2)}) collective-permute-start(bf16[128,1024]{1,0:T(8,128)(2,1)S(1)} %get-tuple-element.503), channel_id=1, source_target_pairs={{0,24},{8,0},{16,8},{24,16},{1,25},{9,1},{17,9},{25,17},{2,26},{10... | collective-permute-start | bytes 786440 | tf_op jit(solution)/shard_map/ppermute | solution.py:881
  323.9 29.2 %collective-permute-start.57 = (bf16[128,1024]{1,0:T(8,128)(2,1)S(1)}, bf16[128,1024]{1,0:T(8,128)(2,1)S(1)}, u32[]{:S(2)}, u32[]{:S(2)}) collective-permute-start(bf16[128,1024]{1,0:T(8,128)(2,1)S(1)} %get-tuple-element.525), channel_id=1, source_target_pairs={{0,8},{8,16},{16,24},{24,0},{1,9},{9,17},{17,25},{25,1},{2,10},{10... | collective-permute-start | bytes 786440 | tf_op jit(solution)/shard_map/ppermute | solution.py:881
  328.6 24.6 %collective-permute-start.58 = (bf16[128,1024]{1,0:T(8,128)(2,1)S(1)}, bf16[128,1024]{1,0:T(8,128)(2,1)S(1)}, u32[]{:S(2)}, u32[]{:S(2)}) collective-permute-start(bf16[128,1024]{1,0:T(8,128)(2,1)S(1)} %get-tuple-element.526), channel_id=1, source_target_pairs={{0,16},{8,24},{16,0},{24,8},{1,17},{9,25},{17,1},{25,9},{2,18},{10... | collective-permute-start | bytes 786440 | tf_op jit(solution)/shard_map/ppermute | solution.py:881
  329.9 23.3 %collective-permute-start.59 = (bf16[128,1024]{1,0:T(8,128)(2,1)S(1)}, bf16[128,1024]{1,0:T(8,128)(2,1)S(1)}, u32[]{:S(2)}, u32[]{:S(2)}) collective-permute-start(bf16[128,1024]{1,0:T(8,128)(2,1)S(1)} %get-tuple-element.527), channel_id=1, source_target_pairs={{0,24},{8,0},{16,8},{24,16},{1,25},{9,1},{17,9},{25,17},{2,26},{10... | collective-permute-start | bytes 786440 | tf_op jit(solution)/shard_map/ppermute | solution.py:881
  331.0 1.2 collective-permute-start.52
  332.2 3.9 %collective-permute-start.53 = (f32[8,1024]{1,0:T(8,128)S(1)}, f32[8,1024]{1,0:T(8,128)S(1)}, u32[]{:S(2)}, u32[]{:S(2)}) collective-permute-start(f32[8,1024]{1,0:T(8,128)S(1)} %add.188), channel_id=1, source_target_pairs={{0,2},{2,0},{1,3},{3,1},{4,6},{6,4},{5,7},{7,5},{8,10},{10,8},{9,1... | collective-permute-start | bytes 98312 | tf_op jit(solution)/shard_map/ppermute | solution.py:1208
  336.2 3.9 %collective-permute-start.54 = (f32[8,1024]{1,0:T(8,128)S(1)}, f32[8,1024]{1,0:T(8,128)S(1)}, u32[]{:S(2)}, u32[]{:S(2)}) collective-permute-start(f32[8,1024]{1,0:T(8,128)S(1)} %add.189), channel_id=1, source_target_pairs={{0,4},{4,0},{1,5},{5,1},{2,6},{6,2},{3,7},{7,3},{8,12},{12,8},{9,1... | collective-permute-start | bytes 98312 | tf_op jit(solution)/shard_map/ppermute | solution.py:1208
  340.1 7.0 %collective-permute-start.55 = (f32[8,1024]{1,0:T(8,128)S(1)}, f32[8,1024]{1,0:T(8,128)S(1)}, u32[]{:S(2)}, u32[]{:S(2)}) collective-permute-start(f32[8,1024]{1,0:T(8,128)S(1)} %add.190), channel_id=1, source_target_pairs={{0,8},{8,0},{16,24},{24,16},{1,9},{9,1},{17,25},{25,17},{2,10},{10... | collective-permute-start | bytes 98312 | tf_op jit(solution)/shard_map/ppermute | solution.py:1208
  347.1 6.0 %collective-permute-start.56 = (f32[8,1024]{1,0:T(8,128)S(1)}, f32[8,1024]{1,0:T(8,128)S(1)}, u32[]{:S(2)}, u32[]{:S(2)}) collective-permute-start(f32[8,1024]{1,0:T(8,128)S(1)} %add.191), channel_id=1, source_target_pairs={{0,16},{8,24},{16,0},{24,8},{1,17},{9,25},{17,1},{25,9},{2,18},{10... | collective-permute-start | bytes 98312 | tf_op jit(solution)/shard_map/ppermute | solution.py:1208
  (80 other events, 986.7 us)

commit v2 on v1

--- a/solution.py
+++ b/solution.py
@@ -11,7 +11,7 @@
 PATCHES = 577
 STEP = 10
 WINDOW = 640
-QROWS = 320
+QROWS = 640
 TILE = 256
 DIGITS = 16
 SMALL = pl.CostEstimate(flops=1024, bytes_accessed=1024, transcendentals=0)
@@ -241,7 +241,7 @@
         + (pl.BlockSpec((1, 8, WINDOW), lambda i, *_: (i, 0, 0)),),
         scratch=[pltpu.VMEM((group_rows, width), bf16), pltpu.VMEM((WINDOW, WINDOW), f32)],
         scalars=(begin, spots),
-        mebibytes=20,
+        mebibytes=24,
         name="attention_forward",
     )
     return out[:blocks], out[blocks]
@@ -266,7 +266,7 @@
         + [pltpu.VMEM((group_rows, lanes), bf16), pltpu.VMEM((WINDOW, WINDOW), f32)],
         scalars=(begin, spots),
         into=into,
-        mebibytes=56 if into else 16,
+        mebibytes=56 if into else 24,
         name="attention_backward",
     )
 

time: 361 us -> 361 us (level)
  starting transfers between devices: 82 us -> 85.8 us
    ppermute x46, starting transfers between devices: 69.2 us -> 72.9 us  [send(): lax.ppermute(value, axis, [(i, (i + step) % size) for i in range(size)])]
  transfers between devices with their start and end apart: 60 -> 60, of which waited for: 30 -> 28; matrix products, arithmetic and copies ran while one was open for 6% -> 6% of each run, Pallas kernels for 29% -> 28%
where the time goes in v2:
time: 361 us; the launch traced here: 358 us
  Pallas kernels  127 us (35%)
  waiting for transfers between devices  104 us (29%)
  starting transfers between devices  85.8 us (24%)
  matrix products  17.1 us (5%)
  local copies, waits for them, and re-layouts  11.4 us (3%)
  between operations  8 us (2%)
  other arithmetic  4.75 us (1%)
    pallas_call x42, Pallas kernels, plain_call(): pl.pallas_call(kernel, grid_spec=pltpu.PrefetchScalarGridSpec(num_scalar_...  127 us
    ppermute x46, waiting for transfers between devices, send(): lax.ppermute(value, axis, [(i, (i + step) % size) for i in range(size)])  82.8 us
    ppermute x46, starting transfers between devices, send(): lax.ppermute(value, axis, [(i, (i + step) % size) for i in range(size)])  72.9 us
    dot_general x6, matrix products, dot(): lax.dot_general(left, right, (((left_dim,), (right_dim,)), ((), ())), pre...  17.1 us
    ppermute x5, waiting for transfers between devices, local(): sums = sums + lax.ppermute(sums, axis, pairs)  14.3 us
    unnamed x172, local copies, waits for them, and re-layouts  9.66 us
  transfers between devices with their start and end apart: 60, of which 28 were waited for; matrix products, arithmetic and copies ran while one was open for 6% of the time, Pallas kernels for 28%

profile of v2, /device:TPU:0, one launch (start us, length us, event | category | flops | bytes accessed | tf_op | source)
XLA Modules:
  0.0 358.1 jit_solution(15535998576664181993)
XLA Ops:
  0.7 2.4 pack.1
  3.0 3.0 collective-permute-start
  6.1 2.6 collective-permute-start.1
  12.5 3.1 collective-permute-done.refs_1_
  15.6 10.4 %collective-permute-done.1.refs_2_ = bf16[128,1024]{1,0:T(8,128)(2,1)S(1)} collective-permute-done((bf16[128,1024]{1,0:T(8,128)(2,1)}, bf16[128,1024]{1,0:T(8,128)(2,1)S(1)}, u32[]{:S(2)}, u32[]{:S(2)}) %collective-permute-start.1) | collective-permute-done | bytes 262176 | tf_op jit(solution)/shard_map/ppermute | solution.py:881
  32.2 6.1 %collective-permute-start.4 = (bf16[144,1024]{1,0:T(8,128)(2,1)S(1)}, bf16[144,1024]{1,0:T(8,128)(2,1)S(1)}, u32[]{:S(2)}, u32[]{:S(2)}) collective-permute-start(bf16[144,1024]{1,0:T(8,128)(2,1)S(1)} %copy-done.68), channel_id=1, source_target_pairs={{0,8},{8,16},{16,24},{24,0},{1,9},{9,17},{17,25},{25,1},{2,10},{10... | collective-permute-start | bytes 884744 | tf_op jit(solution)/shard_map/ppermute | solution.py:881
  38.3 1.6 collective-permute-start.5
  40.6 6.7 %collective-permute-done.4.refs_1_ = bf16[144,1024]{1,0:T(8,128)(2,1)S(1)} collective-permute-done((bf16[144,1024]{1,0:T(8,128)(2,1)S(1)}, bf16[144,1024]{1,0:T(8,128)(2,1)S(1)}, u32[]{:S(2)}, u32[]{:S(2)}) %collective-permute-start.4) | collective-permute-done | bytes 294944 | tf_op jit(solution)/shard_map/ppermute | solution.py:881
  47.4 10.3 %collective-permute-done.5.refs_2_ = bf16[144,1024]{1,0:T(8,128)(2,1)S(1)} collective-permute-done((bf16[144,1024]{1,0:T(8,128)(2,1)S(1)}, bf16[144,1024]{1,0:T(8,128)(2,1)S(1)}, u32[]{:S(2)}, u32[]{:S(2)}) %collective-permute-start.5) | collective-permute-done | bytes 294944 | tf_op jit(solution)/shard_map/ppermute | solution.py:881
  60.2 6.8 %collective-permute-start.11 = (bf16[128,1024]{1,0:T(8,128)(2,1)S(1)}, bf16[128,1024]{1,0:T(8,128)(2,1)S(1)}, u32[]{:S(2)}, u32[]{:S(2)}) collective-permute-start(bf16[128,1024]{1,0:T(8,128)(2,1)S(1)} %copy-done.70), channel_id=1, source_target_pairs={{0,8},{8,16},{16,24},{24,0},{1,9},{9,17},{17,25},{25,1},{2,10},{10... | collective-permute-start | bytes 786440 | tf_op jit(solution)/shard_map/ppermute | solution.py:881
  67.0 2.4 collective-permute-start.12
  71.9 3.6 %convolution_convert_fusion.refs_0_.refs_1_.refs_2_.refs_3_.refs_4_.refs_5_ = bf16[2048,768]{1,0:T(8,128)(2,1)S(1)} fusion(bf16[2048,1024]{1,0:T(8,128)(2,1)S(1)} %place_blocks.1, bf16[1024,768]{1,0:T(8,128)(2,1)S(1)} %get-tuple-element.307.part_ref), kind=kOutput, calls=%fused_computation.2 | convolution fusion | flops 3222798336 | bytes 8912896 | tf_op jit(solution)/shard_map/dot_general | solution.py:66
  75.6 12.3 %attention_forward.1 = (bf16[512,256]{1,0:T(8,128)(2,1)S(1)}, bf16[512,256]{1,0:T(8,128)(2,1)S(1)}, bf16[512,256]{1,0:T(8,128)(2,1)S(1)}, bf16[512,256]{1,0:T(8,128)(2,1)S(1)}, f32[3,8,640]{2,1,0:T(8,128)S(1)}) custom-call(s32[3]{0:T(128)S(1)} %select_reduce_fusion.begin, s32[4]{0:T(128)S(1)} %get-tuple-element.305.spots, ...), custom_call_target="tpu_custom_call" | custom-call | flops 1024 | bytes 1024 | tf_op jit(solution)/shard_map/attention_forward/pallas_call | solution.py:295
  98.5 4.2 %collective-permute-done.17.refs_3_ = bf16[512,256]{1,0:T(8,128)(2,1)S(1)} collective-permute-done((bf16[512,256]{1,0:T(8,128)(2,1)S(1)}, bf16[512,256]{1,0:T(8,128)(2,1)S(1)}, u32[]{:S(2)}, u32[]{:S(2)}) %collective-permute-start.17) | collective-permute-done | bytes 262176 | tf_op jit(solution)/shard_map/ppermute | solution.py:889
  104.8 2.1 proj.1
  109.0 8.9 %up.3 = (bf16[1024,1024]{1,0:T(8,128)(2,1)S(1)}, bf16[1024,1024]{1,0:T(8,128)(2,1)S(1)}, bf16[1024,1024]{1,0:T(8,128)(2,1)S(1)}, bf16[1024,1024]{1,0:T(8,128)(2,1)S(1)}) custom-call(bf16[512,1024]{1,0:T(8,128)(2,1)S(1)} %get-tuple-element.362.low_ref, bf16[1024,1024]{1,0:T(8,128)(2,1)S(1)} %weave.4.refs_0_.refs_2_, ...), custom_call_target="tpu_custom_call" | custom-call | flops 1024 | bytes 1024 | tf_op jit(solution)/shard_map/up/pallas_call | solution.py:295
  117.9 3.6 %collective-permute-done.21.low_ref = bf16[256,1024]{1,0:T(8,128)(2,1)S(1)} collective-permute-done((bf16[256,1024]{1,0:T(8,128)(2,1)S(1)}, bf16[256,1024]{1,0:T(8,128)(2,1)S(1)}, u32[]{:S(2)}, u32[]{:S(2)}) %collective-permute-start.21) | collective-permute-done | bytes 524320 | tf_op jit(solution)/shard_map/ppermute | solution.py:881
  123.9 5.1 %up.4 = (bf16[1024,1024]{1,0:T(8,128)(2,1)S(1)}, bf16[1024,1024]{1,0:T(8,128)(2,1)S(1)}, bf16[1024,1024]{1,0:T(8,128)(2,1)S(1)}, bf16[1024,1024]{1,0:T(8,128)(2,1)S(1)}) custom-call(bf16[256,1024]{1,0:T(8,128)(2,1)S(1)} %collective-permute-done.21.low_ref, ...), custom_call_target="tpu_custom_call", output_to_operand_aliasing={{0}: (3, {}), {1}: (4, {}), {2}: (5, {}), {3}: (6, {})} | custom-call | flops 1024 | bytes 1024 | tf_op jit(solution)/shard_map/up/pallas_call | solution.py:295
  129.0 2.9 wide.6
  132.0 4.7 %collective-permute-done.24.low_ref = bf16[256,1024]{1,0:T(8,128)(2,1)S(1)} collective-permute-done((bf16[256,1024]{1,0:T(8,128)(2,1)S(1)}, bf16[256,1024]{1,0:T(8,128)(2,1)S(1)}, u32[]{:S(2)}, u32[]{:S(2)}) %collective-permute-start.24) | collective-permute-done | bytes 524320 | tf_op jit(solution)/shard_map/ppermute | solution.py:881
  138.2 5.5 %up.5 = (bf16[1024,1024]{1,0:T(8,128)(2,1)S(1)}, bf16[1024,1024]{1,0:T(8,128)(2,1)S(1)}, bf16[1024,1024]{1,0:T(8,128)(2,1)S(1)}, bf16[1024,1024]{1,0:T(8,128)(2,1)S(1)}) custom-call(bf16[256,1024]{1,0:T(8,128)(2,1)S(1)} %collective-permute-done.24.low_ref, ...), custom_call_target="tpu_custom_call", output_to_operand_aliasing={{0}: (3, {}), {1}: (4, {}), {2}: (5, {}), {3}: (6, {})} | custom-call | flops 1024 | bytes 1024 | tf_op jit(solution)/shard_map/up/pallas_call | solution.py:295
  143.8 3.4 wide.7
  147.9 1.6 copy-done.4
  149.5 1.6 copy-done.9
  151.1 1.6 copy-done.12
  152.7 1.6 copy-done.15
  154.3 3.1 wide.8.refs_2_
  157.4 4.4 %collective-permute-done.26.refs_4_ = bf16[256,1024]{1,0:T(8,128)(2,1)} collective-permute-done((bf16[256,1024]{1,0:T(8,128)(2,1)}, bf16[256,1024]{1,0:T(8,128)(2,1)}, u32[]{:S(2)}, u32[]{:S(2)}) %collective-permute-start.26) | collective-permute-done | bytes 524320 | tf_op jit(solution)/shard_map/ppermute | solution.py:881
  161.8 2.5 loss.1
  165.9 4.0 %hidden.3 = (bf16[1024,1024]{1,0:T(8,128)(2,1)S(1)}, bf16[1024,1024]{1,0:T(8,128)(2,1)S(1)}) custom-call(bf16[512,1024]{1,0:T(8,128)(2,1)S(1)} %get-tuple-element.393.low_ref, bf16[1024,1024]{1,0:T(8,128)(2,1)S(1)} %copy-done.18, bf16[1024,1024]{1,0:T(8,128)(2,1)S(1)} %copy-done.20, bf16[1024,1024]{1,0:T(8,128)(2,1)S(1)} %copy-done.5, ...), custom_call_target="tpu_custom_call" | custom-call | flops 1024 | bytes 1024 | tf_op jit(solution)/shard_map/hidden/pallas_call | solution.py:295
  170.0 3.1 wide.9.refs_0_
  173.1 4.4 %collective-permute-done.27.low_ref = bf16[256,1024]{1,0:T(8,128)(2,1)S(1)} collective-permute-done((bf16[256,1024]{1,0:T(8,128)(2,1)S(1)}, bf16[256,1024]{1,0:T(8,128)(2,1)S(1)}, u32[]{:S(2)}, u32[]{:S(2)}) %collective-permute-start.27) | collective-permute-done | bytes 524320 | tf_op jit(solution)/shard_map/ppermute | solution.py:881
  178.8 2.6 hidden.4
  181.4 2.0 wide.10
  183.6 6.1 %collective-permute-done.28.low_ref = bf16[256,1024]{1,0:T(8,128)(2,1)S(1)} collective-permute-done((bf16[256,1024]{1,0:T(8,128)(2,1)S(1)}, bf16[256,1024]{1,0:T(8,128)(2,1)S(1)}, u32[]{:S(2)}, u32[]{:S(2)}) %collective-permute-start.28) | collective-permute-done | bytes 524320 | tf_op jit(solution)/shard_map/ppermute | solution.py:881
  190.8 2.6 hidden.5
  193.5 2.0 wide.11
  195.5 2.5 convolution_convert_fusion.2
  197.9 3.0 collective-permute-done.29.refs_1_
  201.0 2.4 convolution_convert_fusion.1
  205.1 2.5 add_convert_fusion.1.refs_0_
  208.1 2.5 add_convert_fusion.refs_0_
  211.3 1.7 split_x.4
  213.9 4.0 %collective-permute-done.30.refs_2_ = bf16[256,1024]{1,0:T(8,128)(2,1)S(1)} collective-permute-done((bf16[256,1024]{1,0:T(8,128)(2,1)S(1)}, bf16[256,1024]{1,0:T(8,128)(2,1)S(1)}, u32[]{:S(2)}, u32[]{:S(2)}) %collective-permute-start.30) | collective-permute-done | bytes 524320 | tf_op jit(solution)/shard_map/ppermute | solution.py:881
  217.9 2.1 middle.1
  231.5 12.6 %attention_backward.2.refs_7_ = bf16[2048,768]{1,0:T(8,128)(2,1)S(1)} custom-call(s32[3]{0:T(128)S(1)} %copy-done.76, s32[4]{0:T(128)S(1)} %copy-done.78, f32[3,8,640]{2,1,0:T(8,128)S(1)} %get-tuple-element.308.bias_ref, bf16[2048,768]{1,0:T(8,128)(2,1)S(1)} %convolution_convert_fusion.refs_0_.refs_1_.refs_2_.refs_3_.refs_4_.refs_5_, ...), custom_call_target="tpu_custom_call" | custom-call | flops 1024 | bytes 1024 | tf_op jit(solution)/shard_map/attention_backward/pallas_call | solution.py:295
  244.1 5.9 %collective-permute-done.40.refs_1_ = bf16[512,1024]{1,0:T(8,128)(2,1)S(1)} collective-permute-done((bf16[512,1024]{1,0:T(8,128)(2,1)S(1)}, bf16[512,1024]{1,0:T(8,128)(2,1)S(1)}, u32[]{:S(2)}, u32[]{:S(2)}) %collective-permute-start.40) | collective-permute-done | bytes 1048608 | tf_op jit(solution)/shard_map/ppermute | solution.py:881
  255.5 4.4 %collective-permute-start.42 = (bf16[128,1024]{1,0:T(8,128)(2,1)}, bf16[128,1024]{1,0:T(8,128)(2,1)S(1)}, u32[]{:S(2)}, u32[]{:S(2)}) collective-permute-start(bf16[128,1024]{1,0:T(8,128)(2,1)} %get-tuple-element.469), channel_id=1, source_target_pairs={{0,8},{8,16},{16,24},{24,0},{1,9},{9,17},{17,25},{25,1},{2,10},{10... | collective-permute-start | bytes 786440 | tf_op jit(solution)/shard_map/ppermute | solution.py:881
  259.9 2.1 collective-permute-start.43
  262.4 16.0 %attention_backward.3.grad_ref = bf16[2048,768]{1,0:T(8,128)(2,1)} custom-call(s32[3]{0:T(128)} %copy-done.75, s32[4]{0:T(128)} %copy-done.77, f32[3,8,640]{2,1,0:T(8,128)} %copy-done.71, bf16[2048,768]{1,0:T(8,128)(2,1)} %copy-done, bf16[2048,768]{1,0:T(8,128)(2,1)} %copy-done, bf16[2048,768]{1,0:T(8,128)(2,1)} %copy-done, ...), custom_call_target="tpu_custom_call", output_to_operand_aliasing={{}: (10, {})} | custom-call | flops 1024 | bytes 1024 | tf_op jit(solution)/shard_map/attention_backward/pallas_call | solution.py:295
  278.4 6.3 %unproject.1 = (bf16[1024,1024]{1,0:T(8,128)(2,1)S(1)}, bf16[1024,1024]{1,0:T(8,128)(2,1)S(1)}) custom-call(s32[4]{0:T(128)S(1)} %pad_add_fusion.3.spots, bf16[2048,768]{1,0:T(8,128)(2,1)} %attention_backward.3.grad_ref, bf16[1024,768]{1,0:T(8,128)(2,1)S(1)} %copy-done.46), custom_call_target="tpu_custom_call" | custom-call | flops 1024 | bytes 1024 | tf_op jit(solution)/shard_map/unproject/pallas_call | solution.py:295
  285.7 3.7 %convolution_convert_fusion.3.refs_0_ = bf16[1024,768]{1,0:T(8,128)(2,1)S(1)} fusion(bf16[2048,1024]{1,0:T(8,128)(2,1)S(1)} %copy-done.35, bf16[2048,768]{1,0:T(8,128)(2,1)S(1)} %copy-done.22), kind=kOutput, calls=%fused_computation.7 | convolution fusion | flops 3222011904 | bytes 8912896 | tf_op jit(solution)/shard_map/dot_general | solution.py:66
  289.4 1.8 split_x.5
  294.4 5.2 %collective-permute-start.49 = (bf16[128,1024]{1,0:T(8,128)(2,1)S(1)}, bf16[128,1024]{1,0:T(8,128)(2,1)S(1)}, u32[]{:S(2)}, u32[]{:S(2)}) collective-permute-start(bf16[128,1024]{1,0:T(8,128)(2,1)S(1)} %get-tuple-element.501), channel_id=1, source_target_pairs={{0,8},{8,16},{16,24},{24,0},{1,9},{9,17},{17,25},{25,1},{2,10},{10... | collective-permute-start | bytes 786440 | tf_op jit(solution)/shard_map/ppermute | solution.py:881
  299.5 1.7 collective-permute-start.50
  301.9 2.7 adam.3
  304.6 3.4 collective-permute-done.49.refs_1_
  307.9 10.5 %collective-permute-done.50.refs_2_ = bf16[128,1024]{1,0:T(8,128)(2,1)S(1)} collective-permute-done((bf16[128,1024]{1,0:T(8,128)(2,1)S(1)}, bf16[128,1024]{1,0:T(8,128)(2,1)S(1)}, u32[]{:S(2)}, u32[]{:S(2)}) %collective-permute-start.50) | collective-permute-done | bytes 262176 | tf_op jit(solution)/shard_map/ppermute | solution.py:881
  319.8 3.1 leave.1
  323.0 5.6 %collective-permute-start.57 = (bf16[128,1024]{1,0:T(8,128)(2,1)S(1)}, bf16[128,1024]{1,0:T(8,128)(2,1)S(1)}, u32[]{:S(2)}, u32[]{:S(2)}) collective-permute-start(bf16[128,1024]{1,0:T(8,128)(2,1)S(1)} %get-tuple-element.525), channel_id=1, source_target_pairs={{0,8},{8,16},{16,24},{24,0},{1,9},{9,17},{17,25},{25,1},{2,10},{10... | collective-permute-start | bytes 786440 | tf_op jit(solution)/shard_map/ppermute | solution.py:881
  333.6 2.6 collective-permute-done.53
  337.2 2.8 collective-permute-done.54
  340.9 6.1 %collective-permute-done.55 = f32[8,1024]{1,0:T(8,128)S(1)} collective-permute-done((f32[8,1024]{1,0:T(8,128)S(1)}, f32[8,1024]{1,0:T(8,128)S(1)}, u32[]{:S(2)}, u32[]{:S(2)}) %collective-permute-start.55) | collective-permute-done | bytes 32800 | tf_op jit(solution)/shard_map/ppermute | solution.py:1208
  347.1 3.1 collective-permute-start.56
  (300 shorter events, 75.2 us)
Async XLA Ops:
  3.0 12.5 %collective-permute-start = (bf16[128,1024]{1,0:T(8,128)(2,1)}, bf16[128,1024]{1,0:T(8,128)(2,1)S(1)}, u32[]{:S(2)}, u32[]{:S(2)}) collective-permute-start(bf16[128,1024]{1,0:T(8,128)(2,1)} %get-tuple-element.285.refs_0_), channel_id=1, source_target_pairs={{0,8},{8,16},{16,24},{24,0},{1,9},{9,17},{17,25},{25,1},{2,10},{10... | collective-permute-start | bytes 786440 | tf_op jit(solution)/shard_map/ppermute | solution.py:881
  6.1 19.9 %collective-permute-start.1 = (bf16[128,1024]{1,0:T(8,128)(2,1)}, bf16[128,1024]{1,0:T(8,128)(2,1)S(1)}, u32[]{:S(2)}, u32[]{:S(2)}) collective-permute-start(bf16[128,1024]{1,0:T(8,128)(2,1)} %get-tuple-element.285.refs_0_), channel_id=1, source_target_pairs={{0,16},{8,24},{16,0},{24,8},{1,17},{9,25},{17,1},{25,9},{2,18},{10... | collective-permute-start | bytes 786440 | tf_op jit(solution)/shard_map/ppermute | solution.py:881
  8.7 17.3 %collective-permute-start.2 = (bf16[128,1024]{1,0:T(8,128)(2,1)}, bf16[128,1024]{1,0:T(8,128)(2,1)S(1)}, u32[]{:S(2)}, u32[]{:S(2)}) collective-permute-start(bf16[128,1024]{1,0:T(8,128)(2,1)} %get-tuple-element.285.refs_0_), channel_id=1, source_target_pairs={{0,24},{8,0},{16,8},{24,16},{1,25},{9,1},{17,9},{25,17},{2,26},{10... | collective-permute-start | bytes 786440 | tf_op jit(solution)/shard_map/ppermute | solution.py:881
  10.8 64.7 %copy-start.75 = (s32[3]{0:T(128)}, s32[3]{0:T(128)S(1)}, u32[]{:S(2)}) copy-start(s32[3]{0:T(128)S(1)} %select_reduce_fusion.begin) | copy-start | bytes 40
  11.7 63.8 %copy-start.77 = (s32[4]{0:T(128)}, s32[4]{0:T(128)S(1)}, u32[]{:S(2)}) copy-start(s32[4]{0:T(128)S(1)} %get-tuple-element.305.spots) | copy-start | bytes 52
  28.0 29.7 %collective-permute-start.3 = (bf16[512,1024]{1,0:T(8,128)(2,1)S(1)}, bf16[512,1024]{1,0:T(8,128)(2,1)S(1)}, u32[]{:S(2)}, u32[]{:S(2)}) collective-permute-start(bf16[512,1024]{1,0:T(8,128)(2,1)S(1)} %stack_z.3.refs_0_), channel_id=1, source_target_pairs={{0,4},{4,0},{1,5},{5,1},{2,6},{6,2},{3,7},{7,3},{8,12},{12,8},{9,1... | collective-permute-start | bytes 3145736 | tf_op jit(solution)/shard_map/ppermute | solution.py:881
  30.6 27.1 %collective-permute-start.7 = (bf16[512,1024]{1,0:T(8,128)(2,1)S(1)}, bf16[512,1024]{1,0:T(8,128)(2,1)S(1)}, u32[]{:S(2)}, u32[]{:S(2)}) collective-permute-start(bf16[512,1024]{1,0:T(8,128)(2,1)S(1)} %first.1.refs_0_), channel_id=1, source_target_pairs={{0,2},{2,0},{1,3},{3,1},{4,6},{6,4},{5,7},{7,5},{8,10},{10,8},{9,1... | collective-permute-start | bytes 3145736 | tf_op jit(solution)/shard_map/ppermute | solution.py:881
  32.2 15.2 %collective-permute-start.4 = (bf16[144,1024]{1,0:T(8,128)(2,1)S(1)}, bf16[144,1024]{1,0:T(8,128)(2,1)S(1)}, u32[]{:S(2)}, u32[]{:S(2)}) collective-permute-start(bf16[144,1024]{1,0:T(8,128)(2,1)S(1)} %copy-done.68), channel_id=1, source_target_pairs={{0,8},{8,16},{16,24},{24,0},{1,9},{9,17},{17,25},{25,1},{2,10},{10... | collective-permute-start | bytes 884744 | tf_op jit(solution)/shard_map/ppermute | solution.py:881
  38.3 19.4 %collective-permute-start.5 = (bf16[144,1024]{1,0:T(8,128)(2,1)S(1)}, bf16[144,1024]{1,0:T(8,128)(2,1)S(1)}, u32[]{:S(2)}, u32[]{:S(2)}) collective-permute-start(bf16[144,1024]{1,0:T(8,128)(2,1)S(1)} %copy-done.68), channel_id=1, source_target_pairs={{0,16},{8,24},{16,0},{24,8},{1,17},{9,25},{17,1},{25,9},{2,18},{10... | collective-permute-start | bytes 884744 | tf_op jit(solution)/shard_map/ppermute | solution.py:881
  39.9 17.8 %collective-permute-start.6 = (bf16[144,1024]{1,0:T(8,128)(2,1)S(1)}, bf16[144,1024]{1,0:T(8,128)(2,1)S(1)}, u32[]{:S(2)}, u32[]{:S(2)}) collective-permute-start(bf16[144,1024]{1,0:T(8,128)(2,1)S(1)} %copy-done.68), channel_id=1, source_target_pairs={{0,24},{8,0},{16,8},{24,16},{1,25},{9,1},{17,9},{25,17},{2,26},{10... | collective-permute-start | bytes 884744 | tf_op jit(solution)/shard_map/ppermute | solution.py:881
  59.1 10.3 %collective-permute-start.8 = (bf16[512,1024]{1,0:T(8,128)(2,1)S(1)}, bf16[512,1024]{1,0:T(8,128)(2,1)S(1)}, u32[]{:S(2)}, u32[]{:S(2)}) collective-permute-start(bf16[512,1024]{1,0:T(8,128)(2,1)S(1)} %first.1.refs_0_), channel_id=1, source_target_pairs={{0,1},{1,0},{2,3},{3,2},{4,5},{5,4},{6,7},{7,6},{8,9},{9,8},{10,11... | collective-permute-start | bytes 3145736 | tf_op jit(solution)/shard_map/ppermute | solution.py:881
  59.2 11.4 %collective-permute-start.9 = (bf16[512,1024]{1,0:T(8,128)(2,1)S(1)}, bf16[512,1024]{1,0:T(8,128)(2,1)S(1)}, u32[]{:S(2)}, u32[]{:S(2)}) collective-permute-start(bf16[512,1024]{1,0:T(8,128)(2,1)S(1)} %collective-permute-done.7.refs_1_), channel_id=1, source_target_pairs={{0,1},{1,0},{2,3},{3,2},{4,5},{5,4},{6,7},{7,6},{8,9},{9,8},{10,11... | collective-permute-start | bytes 3145736 | tf_op jit(solution)/shard_map/ppermute | solution.py:881
  59.7 28.2 %collective-permute-start.10 = (bf16[528,1024]{1,0:T(8,128)(2,1)S(1)}, bf16[528,1024]{1,0:T(8,128)(2,1)S(1)}, u32[]{:S(2)}, u32[]{:S(2)}) collective-permute-start(bf16[528,1024]{1,0:T(8,128)(2,1)S(1)} %stack_z.4.refs_0_), channel_id=1, source_target_pairs={{0,4},{4,0},{1,5},{5,1},{2,6},{6,2},{3,7},{7,3},{8,12},{12,8},{9,1... | collective-permute-start | bytes 3244040 | tf_op jit(solution)/shard_map/ppermute | solution.py:881
  60.2 27.7 %collective-permute-start.11 = (bf16[128,1024]{1,0:T(8,128)(2,1)S(1)}, bf16[128,1024]{1,0:T(8,128)(2,1)S(1)}, u32[]{:S(2)}, u32[]{:S(2)}) collective-permute-start(bf16[128,1024]{1,0:T(8,128)(2,1)S(1)} %copy-done.70), channel_id=1, source_target_pairs={{0,8},{8,16},{16,24},{24,0},{1,9},{9,17},{17,25},{25,1},{2,10},{10... | collective-permute-start | bytes 786440 | tf_op jit(solution)/shard_map/ppermute | solution.py:881
  67.0 20.9 %collective-permute-start.12 = (bf16[128,1024]{1,0:T(8,128)(2,1)S(1)}, bf16[128,1024]{1,0:T(8,128)(2,1)S(1)}, u32[]{:S(2)}, u32[]{:S(2)}) collective-permute-start(bf16[128,1024]{1,0:T(8,128)(2,1)S(1)} %copy-done.70), channel_id=1, source_target_pairs={{0,16},{8,24},{16,0},{24,8},{1,17},{9,25},{17,1},{25,9},{2,18},{10... | collective-permute-start | bytes 786440 | tf_op jit(solution)/shard_map/ppermute | solution.py:881
  69.3 18.6 %collective-permute-start.13 = (bf16[128,1024]{1,0:T(8,128)(2,1)S(1)}, bf16[128,1024]{1,0:T(8,128)(2,1)S(1)}, u32[]{:S(2)}, u32[]{:S(2)}) collective-permute-start(bf16[128,1024]{1,0:T(8,128)(2,1)S(1)} %copy-done.70), channel_id=1, source_target_pairs={{0,24},{8,0},{16,8},{24,16},{1,25},{9,1},{17,9},{25,17},{2,26},{10... | collective-permute-start | bytes 786440 | tf_op jit(solution)/shard_map/ppermute | solution.py:881
  70.5 17.4 %collective-permute-start.14 = (bf16[1024,256]{1,0:T(8,128)(2,1)S(1)}, bf16[1024,256]{1,0:T(8,128)(2,1)S(1)}, u32[]{:S(2)}, u32[]{:S(2)}) collective-permute-start(bf16[1024,256]{1,0:T(8,128)(2,1)S(1)} %get-tuple-element.320.refs_0_), channel_id=1, source_target_pairs={{0,2},{2,0},{1,3},{3,1},{4,6},{6,4},{5,7},{7,5},{8,10},{10,8},{9,1... | collective-permute-start | bytes 1572872 | tf_op jit(solution)/shard_map/ppermute | solution.py:881
  75.5 155.9 %copy-start = (bf16[2048,768]{1,0:T(8,128)(2,1)}, bf16[2048,768]{1,0:T(8,128)(2,1)S(1)}, u32[]{:S(2)}) copy-start(bf16[2048,768]{1,0:T(8,128)(2,1)S(1)} %convolution_convert_fusion.refs_0_.refs_1_.refs_2_.refs_3_.refs_4_.refs_5_) | copy-start | bytes 9437188
  87.8 143.6 %copy-start.71 = (f32[3,8,640]{2,1,0:T(8,128)}, f32[3,8,640]{2,1,0:T(8,128)S(1)}, u32[]{:S(2)}) copy-start(f32[3,8,640]{2,1,0:T(8,128)S(1)} %get-tuple-element.308.bias_ref) | copy-start | bytes 184324
  88.0 15.2 %collective-permute-start.18 = (bf16[1024,512]{1,0:T(8,128)(2,1)S(1)}, bf16[1024,512]{1,0:T(8,128)(2,1)S(1)}, u32[]{:S(2)}, u32[]{:S(2)}) collective-permute-start(bf16[1024,512]{1,0:T(8,128)(2,1)S(1)} %beside.1.refs_4_.refs_0_), channel_id=1, source_target_pairs={{0,1},{1,0},{2,3},{3,2},{4,5},{5,4},{6,7},{7,6},{8,9},{9,8},{10,11... | collective-permute-start | bytes 3145736 | tf_op jit(solution)/shard_map/ppermute | solution.py:881
  88.8 14.4 %collective-permute-start.19 = (bf16[256,1024]{1,0:T(8,128)(2,1)S(1)}, bf16[256,1024]{1,0:T(8,128)(2,1)S(1)}, u32[]{:S(2)}, u32[]{:S(2)}) collective-permute-start(bf16[256,1024]{1,0:T(8,128)(2,1)S(1)} %get-tuple-element.356.refs_0_), channel_id=1, source_target_pairs={{0,4},{4,0},{1,5},{5,1},{2,6},{6,2},{3,7},{7,3},{8,12},{12,8},{9,1... | collective-permute-start | bytes 1572872 | tf_op jit(solution)/shard_map/ppermute | solution.py:881
  89.4 9.1 %collective-permute-start.15 = (bf16[512,256]{1,0:T(8,128)(2,1)S(1)}, bf16[512,256]{1,0:T(8,128)(2,1)S(1)}, u32[]{:S(2)}, u32[]{:S(2)}) collective-permute-start(bf16[512,256]{1,0:T(8,128)(2,1)S(1)} %get-tuple-element.317), channel_id=1, source_target_pairs={{0,2},{1,3},{2,0},{3,1},{4,6},{5,7},{6,4},{7,5},{8,10},{9,11},{10,... | collective-permute-start | bytes 786440 | tf_op jit(solution)/shard_map/ppermute | solution.py:889
  90.9 7.6 %collective-permute-start.16 = (bf16[512,256]{1,0:T(8,128)(2,1)S(1)}, bf16[512,256]{1,0:T(8,128)(2,1)S(1)}, u32[]{:S(2)}, u32[]{:S(2)}) collective-permute-start(bf16[512,256]{1,0:T(8,128)(2,1)S(1)} %get-tuple-element.318), channel_id=1, source_target_pairs={{0,1},{1,0},{2,3},{3,2},{4,5},{5,4},{6,7},{7,6},{8,9},{9,8},{10,11... | collective-permute-start | bytes 786440 | tf_op jit(solution)/shard_map/ppermute | solution.py:889
  90.9 11.8 %collective-permute-start.17 = (bf16[512,256]{1,0:T(8,128)(2,1)S(1)}, bf16[512,256]{1,0:T(8,128)(2,1)S(1)}, u32[]{:S(2)}, u32[]{:S(2)}) collective-permute-start(bf16[512,256]{1,0:T(8,128)(2,1)S(1)} %get-tuple-element.319), channel_id=1, source_target_pairs={{0,3},{1,2},{2,1},{3,0},{4,7},{5,6},{6,5},{7,4},{8,11},{9,10},{10,... | collective-permute-start | bytes 786440 | tf_op jit(solution)/shard_map/ppermute | solution.py:889
  103.2 4.2 %collective-permute-start.20 = (bf16[1024,1024]{1,0:T(8,128)(2,1)S(1)}, bf16[1024,1024]{1,0:T(8,128)(2,1)S(1)}, u32[]{:S(2)}, u32[]{:S(2)}) collective-permute-start(bf16[1024,1024]{1,0:T(8,128)(2,1)S(1)} %weave.4.refs_0_.refs_2_), channel_id=1, source_target_pairs={{0,1},{1,0},{2,3},{3,2},{4,5},{5,4},{6,7},{7,6},{8,9},{9,8},{10,11... | collective-permute-start | bytes 6291464 | tf_op jit(solution)/shard_map/ppermute | solution.py:881
  103.4 14.5 %collective-permute-start.22 = (bf16[256,1024]{1,0:T(8,128)(2,1)S(1)}, bf16[256,1024]{1,0:T(8,128)(2,1)S(1)}, u32[]{:S(2)}, u32[]{:S(2)}) collective-permute-start(bf16[256,1024]{1,0:T(8,128)(2,1)S(1)} %get-tuple-element.357.refs_1_), channel_id=1, source_target_pairs={{0,4},{4,0},{1,5},{5,1},{2,6},{6,2},{3,7},{7,3},{8,12},{12,8},{9,1... | collective-permute-start | bytes 1572872 | tf_op jit(solution)/shard_map/ppermute | solution.py:881
  107.4 14.1 %collective-permute-start.21 = (bf16[256,1024]{1,0:T(8,128)(2,1)S(1)}, bf16[256,1024]{1,0:T(8,128)(2,1)S(1)}, u32[]{:S(2)}, u32[]{:S(2)}) collective-permute-start(bf16[256,1024]{1,0:T(8,128)(2,1)S(1)} %slice.54), channel_id=1, source_target_pairs={{0,2},{2,0},{1,3},{3,1},{4,6},{6,4},{5,7},{7,5},{8,10},{10,8},{9,1... | collective-permute-start | bytes 1572872 | tf_op jit(solution)/shard_map/ppermute | solution.py:881
  122.2 6.8 %collective-permute-start.23 = (bf16[1024,1024]{1,0:T(8,128)(2,1)S(1)}, bf16[1024,1024]{1,0:T(8,128)(2,1)S(1)}, u32[]{:S(2)}, u32[]{:S(2)}) collective-permute-start(bf16[1024,1024]{1,0:T(8,128)(2,1)S(1)} %weave.5.refs_2_), channel_id=1, source_target_pairs={{0,1},{1,0},{2,3},{3,2},{4,5},{5,4},{6,7},{7,6},{8,9},{9,8},{10,11... | collective-permute-start | bytes 6291464 | tf_op jit(solution)/shard_map/ppermute | solution.py:881
  122.3 14.4 %collective-permute-start.24 = (bf16[256,1024]{1,0:T(8,128)(2,1)S(1)}, bf16[256,1024]{1,0:T(8,128)(2,1)S(1)}, u32[]{:S(2)}, u32[]{:S(2)}) collective-permute-start(bf16[256,1024]{1,0:T(8,128)(2,1)S(1)} %slice.55), channel_id=1, source_target_pairs={{0,2},{2,0},{1,3},{3,1},{4,6},{6,4},{5,7},{7,5},{8,10},{10,8},{9,1... | collective-permute-start | bytes 1572872 | tf_op jit(solution)/shard_map/ppermute | solution.py:881
  136.7 20.7 %collective-permute-start.25 = (bf16[256,1024]{1,0:T(8,128)(2,1)}, bf16[256,1024]{1,0:T(8,128)(2,1)}, u32[]{:S(2)}, u32[]{:S(2)}) collective-permute-start(bf16[256,1024]{1,0:T(8,128)(2,1)} %wide.6), channel_id=1, source_target_pairs={{0,2},{2,0},{1,3},{3,1},{4,6},{6,4},{5,7},{7,5},{8,10},{10,8},{9,1... | collective-permute-start | bytes 1572872 | tf_op jit(solution)/shard_map/ppermute | solution.py:881
  147.2 14.6 %collective-permute-start.26 = (bf16[256,1024]{1,0:T(8,128)(2,1)}, bf16[256,1024]{1,0:T(8,128)(2,1)}, u32[]{:S(2)}, u32[]{:S(2)}) collective-permute-start(bf16[256,1024]{1,0:T(8,128)(2,1)} %wide.7), channel_id=1, source_target_pairs={{0,2},{2,0},{1,3},{3,1},{4,6},{6,4},{5,7},{7,5},{8,10},{10,8},{9,1... | collective-permute-start | bytes 1572872 | tf_op jit(solution)/shard_map/ppermute | solution.py:881
  164.3 13.1 %collective-permute-start.27 = (bf16[256,1024]{1,0:T(8,128)(2,1)S(1)}, bf16[256,1024]{1,0:T(8,128)(2,1)S(1)}, u32[]{:S(2)}, u32[]{:S(2)}) collective-permute-start(bf16[256,1024]{1,0:T(8,128)(2,1)S(1)} %slice.56), channel_id=1, source_target_pairs={{0,2},{2,0},{1,3},{3,1},{4,6},{6,4},{5,7},{7,5},{8,10},{10,8},{9,1... | collective-permute-start | bytes 1572872 | tf_op jit(solution)/shard_map/ppermute | solution.py:881
  177.5 12.2 %collective-permute-start.28 = (bf16[256,1024]{1,0:T(8,128)(2,1)S(1)}, bf16[256,1024]{1,0:T(8,128)(2,1)S(1)}, u32[]{:S(2)}, u32[]{:S(2)}) collective-permute-start(bf16[256,1024]{1,0:T(8,128)(2,1)S(1)} %slice.57), channel_id=1, source_target_pairs={{0,2},{2,0},{1,3},{3,1},{4,6},{6,4},{5,7},{7,5},{8,10},{10,8},{9,1... | collective-permute-start | bytes 1572872 | tf_op jit(solution)/shard_map/ppermute | solution.py:881
  189.7 11.2 %collective-permute-start.29 = (bf16[256,1024]{1,0:T(8,128)(2,1)S(1)}, bf16[256,1024]{1,0:T(8,128)(2,1)S(1)}, u32[]{:S(2)}, u32[]{:S(2)}) collective-permute-start(bf16[256,1024]{1,0:T(8,128)(2,1)S(1)} %wide.10), channel_id=1, source_target_pairs={{0,2},{2,0},{1,3},{3,1},{4,6},{6,4},{5,7},{7,5},{8,10},{10,8},{9,1... | collective-permute-start | bytes 1572872 | tf_op jit(solution)/shard_map/ppermute | solution.py:881
  200.9 4.2 %collective-permute-start.31 = (bf16[1024,1024]{1,0:T(8,128)(2,1)S(1)}, bf16[1024,1024]{1,0:T(8,128)(2,1)S(1)}, u32[]{:S(2)}, u32[]{:S(2)}) collective-permute-start(bf16[1024,1024]{1,0:T(8,128)(2,1)S(1)} %convolution_convert_fusion.2), channel_id=1, source_target_pairs={{0,1},{1,0},{2,3},{3,2},{4,5},{5,4},{6,7},{7,6},{8,9},{9,8},{10,11... | collective-permute-start | bytes 6291464 | tf_op jit(solution)/shard_map/ppermute | solution.py:881
  203.4 4.7 %collective-permute-start.32 = (bf16[1024,1024]{1,0:T(8,128)(2,1)S(1)}, bf16[1024,1024]{1,0:T(8,128)(2,1)S(1)}, u32[]{:S(2)}, u32[]{:S(2)}) collective-permute-start(bf16[1024,1024]{1,0:T(8,128)(2,1)S(1)} %convolution_convert_fusion.1), channel_id=1, source_target_pairs={{0,1},{1,0},{2,3},{3,2},{4,5},{5,4},{6,7},{7,6},{8,9},{9,8},{10,11... | collective-permute-start | bytes 6291464 | tf_op jit(solution)/shard_map/ppermute | solution.py:881
  204.0 13.9 %collective-permute-start.30 = (bf16[256,1024]{1,0:T(8,128)(2,1)S(1)}, bf16[256,1024]{1,0:T(8,128)(2,1)S(1)}, u32[]{:S(2)}, u32[]{:S(2)}) collective-permute-start(bf16[256,1024]{1,0:T(8,128)(2,1)S(1)} %wide.11), channel_id=1, source_target_pairs={{0,2},{2,0},{1,3},{3,1},{4,6},{6,4},{5,7},{7,5},{8,10},{10,8},{9,1... | collective-permute-start | bytes 1572872 | tf_op jit(solution)/shard_map/ppermute | solution.py:881
  221.4 6.3 %collective-permute-start.33 = (bf16[512,128]{1,0:T(8,128)(2,1)S(1)}, bf16[512,128]{1,0:T(8,128)(2,1)S(1)}, u32[]{:S(2)}, u32[]{:S(2)}) collective-permute-start(bf16[512,128]{1,0:T(8,128)(2,1)S(1)} %get-tuple-element.427), channel_id=1, source_target_pairs={{0,2},{1,3},{2,0},{3,1},{4,6},{5,7},{6,4},{7,5},{8,10},{9,11},{10,... | collective-permute-start | bytes 393224 | tf_op jit(solution)/shard_map/ppermute | solution.py:889
  222.1 5.6 %collective-permute-start.34 = (bf16[512,128]{1,0:T(8,128)(2,1)S(1)}, bf16[512,128]{1,0:T(8,128)(2,1)S(1)}, u32[]{:S(2)}, u32[]{:S(2)}) collective-permute-start(bf16[512,128]{1,0:T(8,128)(2,1)S(1)} %get-tuple-element.428), channel_id=1, source_target_pairs={{0,1},{1,0},{2,3},{3,2},{4,5},{5,4},{6,7},{7,6},{8,9},{9,8},{10,11... | collective-permute-start | bytes 393224 | tf_op jit(solution)/shard_map/ppermute | solution.py:889
  222.1 5.8 %collective-permute-start.35 = (bf16[512,128]{1,0:T(8,128)(2,1)S(1)}, bf16[512,128]{1,0:T(8,128)(2,1)S(1)}, u32[]{:S(2)}, u32[]{:S(2)}) collective-permute-start(bf16[512,128]{1,0:T(8,128)(2,1)S(1)} %get-tuple-element.429), channel_id=1, source_target_pairs={{0,3},{1,2},{2,1},{3,0},{4,7},{5,6},{6,5},{7,4},{8,11},{9,10},{10,... | collective-permute-start | bytes 393224 | tf_op jit(solution)/shard_map/ppermute | solution.py:889
  224.9 25.1 %collective-permute-start.40 = (bf16[512,1024]{1,0:T(8,128)(2,1)S(1)}, bf16[512,1024]{1,0:T(8,128)(2,1)S(1)}, u32[]{:S(2)}, u32[]{:S(2)}) collective-permute-start(bf16[512,1024]{1,0:T(8,128)(2,1)S(1)} %get-tuple-element.444), channel_id=1, source_target_pairs={{0,4},{4,0},{1,5},{5,1},{2,6},{6,2},{3,7},{7,3},{8,12},{12,8},{9,1... | collective-permute-start | bytes 3145736 | tf_op jit(solution)/shard_map/ppermute | solution.py:881
  227.9 22.1 %collective-permute-start.39 = (bf16[1024,512]{1,0:T(8,128)(2,1)S(1)}, bf16[1024,512]{1,0:T(8,128)(2,1)S(1)}, u32[]{:S(2)}, u32[]{:S(2)}) collective-permute-start(bf16[1024,512]{1,0:T(8,128)(2,1)S(1)} %get-tuple-element.442), channel_id=1, source_target_pairs={{0,1},{1,0},{2,3},{3,2},{4,5},{5,4},{6,7},{7,6},{8,9},{9,8},{10,11... | collective-permute-start | bytes 3145736 | tf_op jit(solution)/shard_map/ppermute | solution.py:881
  229.3 14.7 %collective-permute-start.36 = (bf16[512,128]{1,0:T(8,128)(2,1)S(1)}, bf16[512,128]{1,0:T(8,128)(2,1)S(1)}, u32[]{:S(2)}, u32[]{:S(2)}) collective-permute-start(bf16[512,128]{1,0:T(8,128)(2,1)S(1)} %get-tuple-element.439), channel_id=1, source_target_pairs={{0,2},{1,3},{2,0},{3,1},{4,6},{5,7},{6,4},{7,5},{8,10},{9,11},{10,... | collective-permute-start | bytes 393224 | tf_op jit(solution)/shard_map/ppermute | solution.py:889
  230.0 14.1 %collective-permute-start.37 = (bf16[512,128]{1,0:T(8,128)(2,1)S(1)}, bf16[512,128]{1,0:T(8,128)(2,1)S(1)}, u32[]{:S(2)}, u32[]{:S(2)}) collective-permute-start(bf16[512,128]{1,0:T(8,128)(2,1)S(1)} %get-tuple-element.440), channel_id=1, source_target_pairs={{0,1},{1,0},{2,3},{3,2},{4,5},{5,4},{6,7},{7,6},{8,9},{9,8},{10,11... | collective-permute-start | bytes 393224 | tf_op jit(solution)/shard_map/ppermute | solution.py:889
  230.0 14.1 %collective-permute-start.38 = (bf16[512,128]{1,0:T(8,128)(2,1)S(1)}, bf16[512,128]{1,0:T(8,128)(2,1)S(1)}, u32[]{:S(2)}, u32[]{:S(2)}) collective-permute-start(bf16[512,128]{1,0:T(8,128)(2,1)S(1)} %get-tuple-element.441), channel_id=1, source_target_pairs={{0,3},{1,2},{2,1},{3,0},{4,7},{5,6},{6,5},{7,4},{8,11},{9,10},{10,... | collective-permute-start | bytes 393224 | tf_op jit(solution)/shard_map/ppermute | solution.py:889
  253.3 25.1 %collective-permute-start.41 = (bf16[512,1024]{1,0:T(8,128)(2,1)}, bf16[512,1024]{1,0:T(8,128)(2,1)S(1)}, u32[]{:S(2)}, u32[]{:S(2)}) collective-permute-start(bf16[512,1024]{1,0:T(8,128)(2,1)} %get-tuple-element.467), channel_id=1, source_target_pairs={{0,4},{4,0},{1,5},{5,1},{2,6},{6,2},{3,7},{7,3},{8,12},{12,8},{9,1... | collective-permute-start | bytes 3145736 | tf_op jit(solution)/shard_map/ppermute | solution.py:881
  254.8 23.6 %collective-permute-start.45 = (bf16[1024,256]{1,0:T(8,128)(2,1)}, bf16[1024,256]{1,0:T(8,128)(2,1)}, u32[]{:S(2)}, u32[]{:S(2)}) collective-permute-start(bf16[1024,256]{1,0:T(8,128)(2,1)} %get-tuple-element.473), channel_id=1, source_target_pairs={{0,2},{2,0},{1,3},{3,1},{4,6},{6,4},{5,7},{7,5},{8,10},{10,8},{9,1... | collective-permute-start | bytes 1572872 | tf_op jit(solution)/shard_map/ppermute | solution.py:881
  255.5 22.9 %collective-permute-start.42 = (bf16[128,1024]{1,0:T(8,128)(2,1)}, bf16[128,1024]{1,0:T(8,128)(2,1)S(1)}, u32[]{:S(2)}, u32[]{:S(2)}) collective-permute-start(bf16[128,1024]{1,0:T(8,128)(2,1)} %get-tuple-element.469), channel_id=1, source_target_pairs={{0,8},{8,16},{16,24},{24,0},{1,9},{9,17},{17,25},{25,1},{2,10},{10... | collective-permute-start | bytes 786440 | tf_op jit(solution)/shard_map/ppermute | solution.py:881
  259.9 18.5 %collective-permute-start.43 = (bf16[128,1024]{1,0:T(8,128)(2,1)}, bf16[128,1024]{1,0:T(8,128)(2,1)}, u32[]{:S(2)}, u32[]{:S(2)}) collective-permute-start(bf16[128,1024]{1,0:T(8,128)(2,1)} %get-tuple-element.470), channel_id=1, source_target_pairs={{0,16},{8,24},{16,0},{24,8},{1,17},{9,25},{17,1},{25,9},{2,18},{10... | collective-permute-start | bytes 786440 | tf_op jit(solution)/shard_map/ppermute | solution.py:881
  262.0 16.4 %collective-permute-start.44 = (bf16[128,1024]{1,0:T(8,128)(2,1)}, bf16[128,1024]{1,0:T(8,128)(2,1)}, u32[]{:S(2)}, u32[]{:S(2)}) collective-permute-start(bf16[128,1024]{1,0:T(8,128)(2,1)} %get-tuple-element.471), channel_id=1, source_target_pairs={{0,24},{8,0},{16,8},{24,16},{1,25},{9,1},{17,9},{25,17},{2,26},{10... | collective-permute-start | bytes 786440 | tf_op jit(solution)/shard_map/ppermute | solution.py:881
  284.8 6.4 %collective-permute-start.46 = (bf16[1024,1024]{1,0:T(8,128)(2,1)S(1)}, bf16[1024,1024]{1,0:T(8,128)(2,1)S(1)}, u32[]{:S(2)}, u32[]{:S(2)}) collective-permute-start(bf16[1024,1024]{1,0:T(8,128)(2,1)S(1)} %get-tuple-element.481), channel_id=1, source_target_pairs={{0,1},{1,0},{2,3},{3,2},{4,5},{5,4},{6,7},{7,6},{8,9},{9,8},{10,11... | collective-permute-start | bytes 6291464 | tf_op jit(solution)/shard_map/ppermute | solution.py:881
  292.2 26.2 %collective-permute-start.47 = (bf16[512,1024]{1,0:T(8,128)(2,1)S(1)}, bf16[512,1024]{1,0:T(8,128)(2,1)S(1)}, u32[]{:S(2)}, u32[]{:S(2)}) collective-permute-start(bf16[512,1024]{1,0:T(8,128)(2,1)S(1)} %get-tuple-element.498), channel_id=1, source_target_pairs={{0,4},{4,0},{1,5},{5,1},{2,6},{6,2},{3,7},{7,3},{8,12},{12,8},{9,1... | collective-permute-start | bytes 3145736 | tf_op jit(solution)/shard_map/ppermute | solution.py:881
  293.7 25.3 %collective-permute-start.48 = (bf16[512,1024]{1,0:T(8,128)(2,1)S(1)}, bf16[512,1024]{1,0:T(8,128)(2,1)S(1)}, u32[]{:S(2)}, u32[]{:S(2)}) collective-permute-start(bf16[512,1024]{1,0:T(8,128)(2,1)S(1)} %get-tuple-element.499), channel_id=1, source_target_pairs={{0,2},{2,0},{1,3},{3,1},{4,6},{6,4},{5,7},{7,5},{8,10},{10,8},{9,1... | collective-permute-start | bytes 3145736 | tf_op jit(solution)/shard_map/ppermute | solution.py:881
  294.4 13.5 %collective-permute-start.49 = (bf16[128,1024]{1,0:T(8,128)(2,1)S(1)}, bf16[128,1024]{1,0:T(8,128)(2,1)S(1)}, u32[]{:S(2)}, u32[]{:S(2)}) collective-permute-start(bf16[128,1024]{1,0:T(8,128)(2,1)S(1)} %get-tuple-element.501), channel_id=1, source_target_pairs={{0,8},{8,16},{16,24},{24,0},{1,9},{9,17},{17,25},{25,1},{2,10},{10... | collective-permute-start | bytes 786440 | tf_op jit(solution)/shard_map/ppermute | solution.py:881
  299.5 18.9 %collective-permute-start.50 = (bf16[128,1024]{1,0:T(8,128)(2,1)S(1)}, bf16[128,1024]{1,0:T(8,128)(2,1)S(1)}, u32[]{:S(2)}, u32[]{:S(2)}) collective-permute-start(bf16[128,1024]{1,0:T(8,128)(2,1)S(1)} %get-tuple-element.502), channel_id=1, source_target_pairs={{0,16},{8,24},{16,0},{24,8},{1,17},{9,25},{17,1},{25,9},{2,18},{10... | collective-permute-start | bytes 786440 | tf_op jit(solution)/shard_map/ppermute | solution.py:881
  301.2 17.2 %collective-permute-start.51 = (bf16[128,1024]{1,0:T(8,128)(2,1)S(1)}, bf16[128,1024]{1,0:T(8,128)(2,1)S(1)}, u32[]{:S(2)}, u32[]{:S(2)}) collective-permute-start(bf16[128,1024]{1,0:T(8,128)(2,1)S(1)} %get-tuple-element.503), channel_id=1, source_target_pairs={{0,24},{8,0},{16,8},{24,16},{1,25},{9,1},{17,9},{25,17},{2,26},{10... | collective-permute-start | bytes 786440 | tf_op jit(solution)/shard_map/ppermute | solution.py:881
  323.0 30.2 %collective-permute-start.57 = (bf16[128,1024]{1,0:T(8,128)(2,1)S(1)}, bf16[128,1024]{1,0:T(8,128)(2,1)S(1)}, u32[]{:S(2)}, u32[]{:S(2)}) collective-permute-start(bf16[128,1024]{1,0:T(8,128)(2,1)S(1)} %get-tuple-element.525), channel_id=1, source_target_pairs={{0,8},{8,16},{16,24},{24,0},{1,9},{9,17},{17,25},{25,1},{2,10},{10... | collective-permute-start | bytes 786440 | tf_op jit(solution)/shard_map/ppermute | solution.py:881
  328.6 24.6 %collective-permute-start.58 = (bf16[128,1024]{1,0:T(8,128)(2,1)S(1)}, bf16[128,1024]{1,0:T(8,128)(2,1)S(1)}, u32[]{:S(2)}, u32[]{:S(2)}) collective-permute-start(bf16[128,1024]{1,0:T(8,128)(2,1)S(1)} %get-tuple-element.526), channel_id=1, source_target_pairs={{0,16},{8,24},{16,0},{24,8},{1,17},{9,25},{17,1},{25,9},{2,18},{10... | collective-permute-start | bytes 786440 | tf_op jit(solution)/shard_map/ppermute | solution.py:881
  329.9 23.3 %collective-permute-start.59 = (bf16[128,1024]{1,0:T(8,128)(2,1)S(1)}, bf16[128,1024]{1,0:T(8,128)(2,1)S(1)}, u32[]{:S(2)}, u32[]{:S(2)}) collective-permute-start(bf16[128,1024]{1,0:T(8,128)(2,1)S(1)} %get-tuple-element.527), channel_id=1, source_target_pairs={{0,24},{8,0},{16,8},{24,16},{1,25},{9,1},{17,9},{25,17},{2,26},{10... | collective-permute-start | bytes 786440 | tf_op jit(solution)/shard_map/ppermute | solution.py:881
  331.0 1.2 collective-permute-start.52
  332.2 3.9 %collective-permute-start.53 = (f32[8,1024]{1,0:T(8,128)S(1)}, f32[8,1024]{1,0:T(8,128)S(1)}, u32[]{:S(2)}, u32[]{:S(2)}) collective-permute-start(f32[8,1024]{1,0:T(8,128)S(1)} %add.188), channel_id=1, source_target_pairs={{0,2},{2,0},{1,3},{3,1},{4,6},{6,4},{5,7},{7,5},{8,10},{10,8},{9,1... | collective-permute-start | bytes 98312 | tf_op jit(solution)/shard_map/ppermute | solution.py:1208
  336.2 3.9 %collective-permute-start.54 = (f32[8,1024]{1,0:T(8,128)S(1)}, f32[8,1024]{1,0:T(8,128)S(1)}, u32[]{:S(2)}, u32[]{:S(2)}) collective-permute-start(f32[8,1024]{1,0:T(8,128)S(1)} %add.189), channel_id=1, source_target_pairs={{0,4},{4,0},{1,5},{5,1},{2,6},{6,2},{3,7},{7,3},{8,12},{12,8},{9,1... | collective-permute-start | bytes 98312 | tf_op jit(solution)/shard_map/ppermute | solution.py:1208
  340.1 7.0 %collective-permute-start.55 = (f32[8,1024]{1,0:T(8,128)S(1)}, f32[8,1024]{1,0:T(8,128)S(1)}, u32[]{:S(2)}, u32[]{:S(2)}) collective-permute-start(f32[8,1024]{1,0:T(8,128)S(1)} %add.190), channel_id=1, source_target_pairs={{0,8},{8,0},{16,24},{24,16},{1,9},{9,1},{17,25},{25,17},{2,10},{10... | collective-permute-start | bytes 98312 | tf_op jit(solution)/shard_map/ppermute | solution.py:1208
  347.1 6.0 %collective-permute-start.56 = (f32[8,1024]{1,0:T(8,128)S(1)}, f32[8,1024]{1,0:T(8,128)S(1)}, u32[]{:S(2)}, u32[]{:S(2)}) collective-permute-start(f32[8,1024]{1,0:T(8,128)S(1)} %add.191), channel_id=1, source_target_pairs={{0,16},{8,24},{16,0},{24,8},{1,17},{9,25},{17,1},{25,9},{2,18},{10... | collective-permute-start | bytes 98312 | tf_op jit(solution)/shard_map/ppermute | solution.py:1208
  (80 other events, 1001.4 us)

commit v3 on v2

--- a/solution.py
+++ b/solution.py
@@ -1132,8 +1132,14 @@
     sent_later = [send_back(pieces) for pieces in pieces_attn[1:]]
     sent_proj = send(far_proj, "core", 1)
     grad_projected = attend_backward(projected, sent_attn, spots, geometry[0], bias, 0, ())
-    grad_projected, sent_later, sent_proj, parts_down, halves_up = tie(
-        grad_projected, sent_later, sent_proj, parts_down, halves_up
+
+    def grad_tile(tile):
+        cols = slice(tile * lanes, (tile + 1) * lanes)
+        return dot(group_one, grad_projected[:, cols], 0, 0).astype(bf16)
+
+    tile_grads = [grad_tile(0)] if tiles > 1 else []
+    grad_projected, sent_later, sent_proj, parts_down, halves_up, tile_grads = tie(
+        grad_projected, sent_later, sent_proj, parts_down, halves_up, tile_grads
     )
 
     hold_proj = add_lanes(grad_proj, sent_proj)
@@ -1160,8 +1166,8 @@
     )
     far_one, grad_projected = tie(far_one, grad_projected)
     sent_one = send(far_one, "core", 1)
-    grad_qkv = dot(group_one, grad_projected, 0, 0).astype(bf16)
-    halves_qkv = split_x([[grad_qkv], part_proj], n_x, places)
+    tile_grads += [grad_tile(tile) for tile in range(len(tile_grads), tiles)]
+    halves_qkv = split_x([[part] for part in tile_grads] + [part_proj], n_x, places)
     pieces_up = split_z(parts_up, places)
     halves_qkv, sent_one, near_one, pieces_up = tie(halves_qkv, sent_one, near_one, pieces_up)
 
@@ -1208,10 +1214,6 @@
             sums = sums + lax.ppermute(sums, axis, pairs)
             step *= 2
     (new_up,) = adam_call([last_up], [(0, 0, unit, False)], weight_up, first_up, second_up)
-    sums, last_qkv, new_up = tie(sums, last_qkv, new_up)
-    loss_sum = jnp.sum(sums[4])
-    live_count = live_count[0, 0]
-
     new_qkv, new_proj = adam_call(
         [last_qkv],
         [(0, [(0, n * lanes) for n in range(tiles)], lanes, False), (0, 3 * width, width, True)],
@@ -1222,6 +1224,10 @@
         first_proj,
         second_proj,
     )
+    sums, new_qkv, new_proj, new_up = tie(sums, new_qkv, new_proj, new_up)
+    loss_sum = jnp.sum(sums[4])
+    live_count = live_count[0, 0]
+
     new_norms = adam_step(norm_params, sums[:4], first_norms, second_norms, 0.0, norm_rate)
     return (
         loss_sum / live_count,

time: 361 us -> 361 us (level)
    dot_general x6 -> x7, matrix products: 17.1 us -> 18.2 us  [dot(): lax.dot_general(left, right, (((left_dim,), (right_dim,)), ((), ())), pre...]
    unnamed x172 -> x178, local copies, waits for them, and re-layouts: 9.66 us -> 10.5 us
where the time goes in v3:
time: 361 us; the launch traced here: 358 us
  Pallas kernels  127 us (35%)
  waiting for transfers between devices  102 us (28%)
  starting transfers between devices  85.7 us (24%)
  matrix products  18.2 us (5%)
  local copies, waits for them, and re-layouts  12.2 us (3%)
  between operations  8.04 us (2%)
  other arithmetic  4.75 us (1%)
    pallas_call x42, Pallas kernels, plain_call(): pl.pallas_call(kernel, grid_spec=pltpu.PrefetchScalarGridSpec(num_scalar_...  127 us
    ppermute x46, waiting for transfers between devices, send(): lax.ppermute(value, axis, [(i, (i + step) % size) for i in range(size)])  80.2 us
    ppermute x46, starting transfers between devices, send(): lax.ppermute(value, axis, [(i, (i + step) % size) for i in range(size)])  72.9 us
    dot_general x7, matrix products, dot(): lax.dot_general(left, right, (((left_dim,), (right_dim,)), ((), ())), pre...  18.2 us
    ppermute x5, waiting for transfers between devices, local(): sums = sums + lax.ppermute(sums, axis, pairs)  14.4 us
    unnamed x178, local copies, waits for them, and re-layouts  10.5 us
  transfers between devices with their start and end apart: 60, of which 28 were waited for; matrix products, arithmetic and copies ran while one was open for 6% of the time, Pallas kernels for 28%

profile of v3, /device:TPU:0, one launch (start us, length us, event | category | flops | bytes accessed | tf_op | source)
XLA Modules:
  0.0 357.6 jit_solution(10581634564418504931)
XLA Ops:
  0.7 2.4 pack.1
  3.0 3.0 collective-permute-start
  6.1 2.6 collective-permute-start.1
  12.5 3.1 collective-permute-done.refs_1_
  15.6 10.4 %collective-permute-done.1.refs_2_ = bf16[128,1024]{1,0:T(8,128)(2,1)S(1)} collective-permute-done((bf16[128,1024]{1,0:T(8,128)(2,1)}, bf16[128,1024]{1,0:T(8,128)(2,1)S(1)}, u32[]{:S(2)}, u32[]{:S(2)}) %collective-permute-start.1) | collective-permute-done | bytes 262176 | tf_op jit(solution)/shard_map/ppermute | solution.py:881
  32.2 6.1 %collective-permute-start.4 = (bf16[144,1024]{1,0:T(8,128)(2,1)S(1)}, bf16[144,1024]{1,0:T(8,128)(2,1)S(1)}, u32[]{:S(2)}, u32[]{:S(2)}) collective-permute-start(bf16[144,1024]{1,0:T(8,128)(2,1)S(1)} %copy-done.71), channel_id=1, source_target_pairs={{0,8},{8,16},{16,24},{24,0},{1,9},{9,17},{17,25},{25,1},{2,10},{10... | collective-permute-start | bytes 884744 | tf_op jit(solution)/shard_map/ppermute | solution.py:881
  38.3 1.6 collective-permute-start.5
  40.6 6.7 %collective-permute-done.4.refs_1_ = bf16[144,1024]{1,0:T(8,128)(2,1)S(1)} collective-permute-done((bf16[144,1024]{1,0:T(8,128)(2,1)S(1)}, bf16[144,1024]{1,0:T(8,128)(2,1)S(1)}, u32[]{:S(2)}, u32[]{:S(2)}) %collective-permute-start.4) | collective-permute-done | bytes 294944 | tf_op jit(solution)/shard_map/ppermute | solution.py:881
  47.4 10.3 %collective-permute-done.5.refs_2_ = bf16[144,1024]{1,0:T(8,128)(2,1)S(1)} collective-permute-done((bf16[144,1024]{1,0:T(8,128)(2,1)S(1)}, bf16[144,1024]{1,0:T(8,128)(2,1)S(1)}, u32[]{:S(2)}, u32[]{:S(2)}) %collective-permute-start.5) | collective-permute-done | bytes 294944 | tf_op jit(solution)/shard_map/ppermute | solution.py:881
  60.2 6.8 %collective-permute-start.11 = (bf16[128,1024]{1,0:T(8,128)(2,1)S(1)}, bf16[128,1024]{1,0:T(8,128)(2,1)S(1)}, u32[]{:S(2)}, u32[]{:S(2)}) collective-permute-start(bf16[128,1024]{1,0:T(8,128)(2,1)S(1)} %copy-done.73), channel_id=1, source_target_pairs={{0,8},{8,16},{16,24},{24,0},{1,9},{9,17},{17,25},{25,1},{2,10},{10... | collective-permute-start | bytes 786440 | tf_op jit(solution)/shard_map/ppermute | solution.py:881
  67.0 2.4 collective-permute-start.12
  71.9 3.6 %convolution_convert_fusion.refs_0_.refs_1_.refs_2_.refs_3_.refs_4_.refs_5_ = bf16[2048,768]{1,0:T(8,128)(2,1)S(1)} fusion(bf16[2048,1024]{1,0:T(8,128)(2,1)S(1)} %place_blocks.1, bf16[1024,768]{1,0:T(8,128)(2,1)S(1)} %get-tuple-element.310.part_ref), kind=kOutput, calls=%fused_computation.2 | convolution fusion | flops 3222798336 | bytes 8912896 | tf_op jit(solution)/shard_map/dot_general | solution.py:66
  75.6 12.3 %attention_forward.1 = (bf16[512,256]{1,0:T(8,128)(2,1)S(1)}, bf16[512,256]{1,0:T(8,128)(2,1)S(1)}, bf16[512,256]{1,0:T(8,128)(2,1)S(1)}, bf16[512,256]{1,0:T(8,128)(2,1)S(1)}, f32[3,8,640]{2,1,0:T(8,128)S(1)}) custom-call(s32[3]{0:T(128)S(1)} %select_reduce_fusion.begin, s32[4]{0:T(128)S(1)} %get-tuple-element.292.spots, ...), custom_call_target="tpu_custom_call" | custom-call | flops 1024 | bytes 1024 | tf_op jit(solution)/shard_map/attention_forward/pallas_call | solution.py:295
  98.5 4.2 %collective-permute-done.17.refs_3_ = bf16[512,256]{1,0:T(8,128)(2,1)S(1)} collective-permute-done((bf16[512,256]{1,0:T(8,128)(2,1)S(1)}, bf16[512,256]{1,0:T(8,128)(2,1)S(1)}, u32[]{:S(2)}, u32[]{:S(2)}) %collective-permute-start.17) | collective-permute-done | bytes 262176 | tf_op jit(solution)/shard_map/ppermute | solution.py:889
  104.9 2.1 proj.1
  109.0 8.9 %up.3 = (bf16[1024,1024]{1,0:T(8,128)(2,1)S(1)}, bf16[1024,1024]{1,0:T(8,128)(2,1)S(1)}, bf16[1024,1024]{1,0:T(8,128)(2,1)S(1)}, bf16[1024,1024]{1,0:T(8,128)(2,1)S(1)}) custom-call(bf16[512,1024]{1,0:T(8,128)(2,1)S(1)} %get-tuple-element.365.low_ref, bf16[1024,1024]{1,0:T(8,128)(2,1)S(1)} %weave.4.refs_0_.refs_2_, ...), custom_call_target="tpu_custom_call" | custom-call | flops 1024 | bytes 1024 | tf_op jit(solution)/shard_map/up/pallas_call | solution.py:295
  117.9 3.6 %collective-permute-done.21.low_ref = bf16[256,1024]{1,0:T(8,128)(2,1)S(1)} collective-permute-done((bf16[256,1024]{1,0:T(8,128)(2,1)S(1)}, bf16[256,1024]{1,0:T(8,128)(2,1)S(1)}, u32[]{:S(2)}, u32[]{:S(2)}) %collective-permute-start.21) | collective-permute-done | bytes 524320 | tf_op jit(solution)/shard_map/ppermute | solution.py:881
  123.9 5.1 %up.4 = (bf16[1024,1024]{1,0:T(8,128)(2,1)S(1)}, bf16[1024,1024]{1,0:T(8,128)(2,1)S(1)}, bf16[1024,1024]{1,0:T(8,128)(2,1)S(1)}, bf16[1024,1024]{1,0:T(8,128)(2,1)S(1)}) custom-call(bf16[256,1024]{1,0:T(8,128)(2,1)S(1)} %collective-permute-done.21.low_ref, ...), custom_call_target="tpu_custom_call", output_to_operand_aliasing={{0}: (3, {}), {1}: (4, {}), {2}: (5, {}), {3}: (6, {})} | custom-call | flops 1024 | bytes 1024 | tf_op jit(solution)/shard_map/up/pallas_call | solution.py:295
  129.0 2.9 wide.6
  132.0 4.7 %collective-permute-done.24.low_ref = bf16[256,1024]{1,0:T(8,128)(2,1)S(1)} collective-permute-done((bf16[256,1024]{1,0:T(8,128)(2,1)S(1)}, bf16[256,1024]{1,0:T(8,128)(2,1)S(1)}, u32[]{:S(2)}, u32[]{:S(2)}) %collective-permute-start.24) | collective-permute-done | bytes 524320 | tf_op jit(solution)/shard_map/ppermute | solution.py:881
  138.2 5.5 %up.5 = (bf16[1024,1024]{1,0:T(8,128)(2,1)S(1)}, bf16[1024,1024]{1,0:T(8,128)(2,1)S(1)}, bf16[1024,1024]{1,0:T(8,128)(2,1)S(1)}, bf16[1024,1024]{1,0:T(8,128)(2,1)S(1)}) custom-call(bf16[256,1024]{1,0:T(8,128)(2,1)S(1)} %collective-permute-done.24.low_ref, ...), custom_call_target="tpu_custom_call", output_to_operand_aliasing={{0}: (3, {}), {1}: (4, {}), {2}: (5, {}), {3}: (6, {})} | custom-call | flops 1024 | bytes 1024 | tf_op jit(solution)/shard_map/up/pallas_call | solution.py:295
  143.8 3.4 wide.7
  149.5 1.6 copy-done.9
  151.1 1.6 copy-done.12
  152.7 1.6 copy-done.15
  154.3 3.1 wide.8.refs_2_
  157.4 4.4 %collective-permute-done.26.refs_4_ = bf16[256,1024]{1,0:T(8,128)(2,1)} collective-permute-done((bf16[256,1024]{1,0:T(8,128)(2,1)}, bf16[256,1024]{1,0:T(8,128)(2,1)}, u32[]{:S(2)}, u32[]{:S(2)}) %collective-permute-start.26) | collective-permute-done | bytes 524320 | tf_op jit(solution)/shard_map/ppermute | solution.py:881
  161.8 2.5 loss.1
  166.0 4.0 %hidden.3 = (bf16[1024,1024]{1,0:T(8,128)(2,1)S(1)}, bf16[1024,1024]{1,0:T(8,128)(2,1)S(1)}) custom-call(bf16[512,1024]{1,0:T(8,128)(2,1)S(1)} %get-tuple-element.396.low_ref, bf16[1024,1024]{1,0:T(8,128)(2,1)S(1)} %copy-done.18, bf16[1024,1024]{1,0:T(8,128)(2,1)S(1)} %copy-done.20, bf16[1024,1024]{1,0:T(8,128)(2,1)S(1)} %copy-done.5, ...), custom_call_target="tpu_custom_call" | custom-call | flops 1024 | bytes 1024 | tf_op jit(solution)/shard_map/hidden/pallas_call | solution.py:295
  170.0 3.1 wide.9.refs_0_
  173.1 4.3 %collective-permute-done.27.low_ref = bf16[256,1024]{1,0:T(8,128)(2,1)S(1)} collective-permute-done((bf16[256,1024]{1,0:T(8,128)(2,1)S(1)}, bf16[256,1024]{1,0:T(8,128)(2,1)S(1)}, u32[]{:S(2)}, u32[]{:S(2)}) %collective-permute-start.27) | collective-permute-done | bytes 524320 | tf_op jit(solution)/shard_map/ppermute | solution.py:881
  178.8 2.6 hidden.4
  181.5 2.0 wide.10
  183.6 6.1 %collective-permute-done.28.low_ref = bf16[256,1024]{1,0:T(8,128)(2,1)S(1)} collective-permute-done((bf16[256,1024]{1,0:T(8,128)(2,1)S(1)}, bf16[256,1024]{1,0:T(8,128)(2,1)S(1)}, u32[]{:S(2)}, u32[]{:S(2)}) %collective-permute-start.28) | collective-permute-done | bytes 524320 | tf_op jit(solution)/shard_map/ppermute | solution.py:881
  190.8 2.6 hidden.5
  193.5 2.0 wide.11
  195.5 2.5 convolution_convert_fusion.2
  198.0 3.0 collective-permute-done.29.refs_1_
  201.0 2.4 convolution_convert_fusion.1
  205.1 2.5 add_convert_fusion.1.refs_0_
  208.1 2.5 add_convert_fusion.refs_0_
  211.3 1.6 split_x.4
  213.9 4.0 %collective-permute-done.30.refs_2_ = bf16[256,1024]{1,0:T(8,128)(2,1)S(1)} collective-permute-done((bf16[256,1024]{1,0:T(8,128)(2,1)S(1)}, bf16[256,1024]{1,0:T(8,128)(2,1)S(1)}, u32[]{:S(2)}, u32[]{:S(2)}) %collective-permute-start.30) | collective-permute-done | bytes 524320 | tf_op jit(solution)/shard_map/ppermute | solution.py:881
  217.9 2.1 middle.1
  231.5 12.6 %attention_backward.2.refs_7_ = bf16[2048,768]{1,0:T(8,128)(2,1)S(1)} custom-call(s32[3]{0:T(128)S(1)} %copy-done.79, s32[4]{0:T(128)S(1)} %copy-done.81, f32[3,8,640]{2,1,0:T(8,128)S(1)} %get-tuple-element.311.bias_ref, bf16[2048,768]{1,0:T(8,128)(2,1)S(1)} %convolution_convert_fusion.refs_0_.refs_1_.refs_2_.refs_3_.refs_4_.refs_5_, ...), custom_call_target="tpu_custom_call" | custom-call | flops 1024 | bytes 1024 | tf_op jit(solution)/shard_map/attention_backward/pallas_call | solution.py:295
  244.1 2.4 fusion.7.refs_0_
  246.6 3.5 collective-permute-done.40.refs_1_
  256.3 4.4 %collective-permute-start.42 = (bf16[128,1024]{1,0:T(8,128)(2,1)}, bf16[128,1024]{1,0:T(8,128)(2,1)}, u32[]{:S(2)}, u32[]{:S(2)}) collective-permute-start(bf16[128,1024]{1,0:T(8,128)(2,1)} %get-tuple-element.473), channel_id=1, source_target_pairs={{0,8},{8,16},{16,24},{24,0},{1,9},{9,17},{17,25},{25,1},{2,10},{10... | collective-permute-start | bytes 786440 | tf_op jit(solution)/shard_map/ppermute | solution.py:881
  260.7 2.1 collective-permute-start.43
  263.1 16.0 %attention_backward.3.grad_ref = bf16[2048,768]{1,0:T(8,128)(2,1)} custom-call(s32[3]{0:T(128)} %copy-done.78, s32[4]{0:T(128)} %copy-done.80, f32[3,8,640]{2,1,0:T(8,128)} %copy-done.74, bf16[2048,768]{1,0:T(8,128)(2,1)} %copy-done, bf16[2048,768]{1,0:T(8,128)(2,1)} %copy-done, bf16[2048,768]{1,0:T(8,128)(2,1)} %copy-done, ...), custom_call_target="tpu_custom_call", output_to_operand_aliasing={{}: (10, {})} | custom-call | flops 1024 | bytes 1024 | tf_op jit(solution)/shard_map/attention_backward/pallas_call | solution.py:295
  279.2 6.3 %unproject.1 = (bf16[1024,1024]{1,0:T(8,128)(2,1)S(1)}, bf16[1024,1024]{1,0:T(8,128)(2,1)S(1)}) custom-call(s32[4]{0:T(128)S(1)} %pad_add_fusion.3.spots, bf16[2048,768]{1,0:T(8,128)(2,1)} %attention_backward.3.grad_ref, bf16[1024,768]{1,0:T(8,128)(2,1)S(1)} %copy-done.47), custom_call_target="tpu_custom_call" | custom-call | flops 1024 | bytes 1024 | tf_op jit(solution)/shard_map/unproject/pallas_call | solution.py:295
  286.5 2.4 fusion.4.refs_1_
  288.9 1.8 split_x.5
  293.9 5.1 %collective-permute-start.49 = (bf16[128,1024]{1,0:T(8,128)(2,1)S(1)}, bf16[128,1024]{1,0:T(8,128)(2,1)S(1)}, u32[]{:S(2)}, u32[]{:S(2)}) collective-permute-start(bf16[128,1024]{1,0:T(8,128)(2,1)S(1)} %get-tuple-element.505), channel_id=1, source_target_pairs={{0,8},{8,16},{16,24},{24,0},{1,9},{9,17},{17,25},{25,1},{2,10},{10... | collective-permute-start | bytes 786440 | tf_op jit(solution)/shard_map/ppermute | solution.py:881
  299.1 1.7 collective-permute-start.50
  301.4 2.7 adam.3
  304.2 3.3 collective-permute-done.49.refs_1_
  307.4 10.5 %collective-permute-done.50.refs_2_ = bf16[128,1024]{1,0:T(8,128)(2,1)S(1)} collective-permute-done((bf16[128,1024]{1,0:T(8,128)(2,1)S(1)}, bf16[128,1024]{1,0:T(8,128)(2,1)S(1)}, u32[]{:S(2)}, u32[]{:S(2)}) %collective-permute-start.50) | collective-permute-done | bytes 262176 | tf_op jit(solution)/shard_map/ppermute | solution.py:881
  319.3 3.1 leave.1
  322.5 5.6 %collective-permute-start.57 = (bf16[128,1024]{1,0:T(8,128)(2,1)S(1)}, bf16[128,1024]{1,0:T(8,128)(2,1)S(1)}, u32[]{:S(2)}, u32[]{:S(2)}) collective-permute-start(bf16[128,1024]{1,0:T(8,128)(2,1)S(1)} %get-tuple-element.529), channel_id=1, source_target_pairs={{0,8},{8,16},{16,24},{24,0},{1,9},{9,17},{17,25},{25,1},{2,10},{10... | collective-permute-start | bytes 786440 | tf_op jit(solution)/shard_map/ppermute | solution.py:881
  333.1 2.6 collective-permute-done.53
  336.7 2.9 collective-permute-done.54
  340.4 6.1 %collective-permute-done.55 = f32[8,1024]{1,0:T(8,128)S(1)} collective-permute-done((f32[8,1024]{1,0:T(8,128)S(1)}, f32[8,1024]{1,0:T(8,128)S(1)}, u32[]{:S(2)}, u32[]{:S(2)}) %collective-permute-start.55) | collective-permute-done | bytes 32800 | tf_op jit(solution)/shard_map/ppermute | solution.py:1214
  346.6 3.1 collective-permute-start.56
  (307 shorter events, 77.7 us)
Async XLA Ops:
  3.0 12.5 %collective-permute-start = (bf16[128,1024]{1,0:T(8,128)(2,1)}, bf16[128,1024]{1,0:T(8,128)(2,1)S(1)}, u32[]{:S(2)}, u32[]{:S(2)}) collective-permute-start(bf16[128,1024]{1,0:T(8,128)(2,1)} %get-tuple-element.288.refs_0_), channel_id=1, source_target_pairs={{0,8},{8,16},{16,24},{24,0},{1,9},{9,17},{17,25},{25,1},{2,10},{10... | collective-permute-start | bytes 786440 | tf_op jit(solution)/shard_map/ppermute | solution.py:881
  6.1 19.9 %collective-permute-start.1 = (bf16[128,1024]{1,0:T(8,128)(2,1)}, bf16[128,1024]{1,0:T(8,128)(2,1)S(1)}, u32[]{:S(2)}, u32[]{:S(2)}) collective-permute-start(bf16[128,1024]{1,0:T(8,128)(2,1)} %get-tuple-element.288.refs_0_), channel_id=1, source_target_pairs={{0,16},{8,24},{16,0},{24,8},{1,17},{9,25},{17,1},{25,9},{2,18},{10... | collective-permute-start | bytes 786440 | tf_op jit(solution)/shard_map/ppermute | solution.py:881
  8.7 17.3 %collective-permute-start.2 = (bf16[128,1024]{1,0:T(8,128)(2,1)}, bf16[128,1024]{1,0:T(8,128)(2,1)S(1)}, u32[]{:S(2)}, u32[]{:S(2)}) collective-permute-start(bf16[128,1024]{1,0:T(8,128)(2,1)} %get-tuple-element.288.refs_0_), channel_id=1, source_target_pairs={{0,24},{8,0},{16,8},{24,16},{1,25},{9,1},{17,9},{25,17},{2,26},{10... | collective-permute-start | bytes 786440 | tf_op jit(solution)/shard_map/ppermute | solution.py:881
  10.8 64.7 %copy-start.78 = (s32[3]{0:T(128)}, s32[3]{0:T(128)S(1)}, u32[]{:S(2)}) copy-start(s32[3]{0:T(128)S(1)} %select_reduce_fusion.begin) | copy-start | bytes 40
  11.7 63.8 %copy-start.80 = (s32[4]{0:T(128)}, s32[4]{0:T(128)S(1)}, u32[]{:S(2)}) copy-start(s32[4]{0:T(128)S(1)} %get-tuple-element.292.spots) | copy-start | bytes 52
  28.0 29.7 %collective-permute-start.3 = (bf16[512,1024]{1,0:T(8,128)(2,1)S(1)}, bf16[512,1024]{1,0:T(8,128)(2,1)S(1)}, u32[]{:S(2)}, u32[]{:S(2)}) collective-permute-start(bf16[512,1024]{1,0:T(8,128)(2,1)S(1)} %stack_z.3.refs_0_), channel_id=1, source_target_pairs={{0,4},{4,0},{1,5},{5,1},{2,6},{6,2},{3,7},{7,3},{8,12},{12,8},{9,1... | collective-permute-start | bytes 3145736 | tf_op jit(solution)/shard_map/ppermute | solution.py:881
  30.6 27.1 %collective-permute-start.7 = (bf16[512,1024]{1,0:T(8,128)(2,1)S(1)}, bf16[512,1024]{1,0:T(8,128)(2,1)S(1)}, u32[]{:S(2)}, u32[]{:S(2)}) collective-permute-start(bf16[512,1024]{1,0:T(8,128)(2,1)S(1)} %first.1.refs_0_), channel_id=1, source_target_pairs={{0,2},{2,0},{1,3},{3,1},{4,6},{6,4},{5,7},{7,5},{8,10},{10,8},{9,1... | collective-permute-start | bytes 3145736 | tf_op jit(solution)/shard_map/ppermute | solution.py:881
  32.2 15.2 %collective-permute-start.4 = (bf16[144,1024]{1,0:T(8,128)(2,1)S(1)}, bf16[144,1024]{1,0:T(8,128)(2,1)S(1)}, u32[]{:S(2)}, u32[]{:S(2)}) collective-permute-start(bf16[144,1024]{1,0:T(8,128)(2,1)S(1)} %copy-done.71), channel_id=1, source_target_pairs={{0,8},{8,16},{16,24},{24,0},{1,9},{9,17},{17,25},{25,1},{2,10},{10... | collective-permute-start | bytes 884744 | tf_op jit(solution)/shard_map/ppermute | solution.py:881
  38.3 19.4 %collective-permute-start.5 = (bf16[144,1024]{1,0:T(8,128)(2,1)S(1)}, bf16[144,1024]{1,0:T(8,128)(2,1)S(1)}, u32[]{:S(2)}, u32[]{:S(2)}) collective-permute-start(bf16[144,1024]{1,0:T(8,128)(2,1)S(1)} %copy-done.71), channel_id=1, source_target_pairs={{0,16},{8,24},{16,0},{24,8},{1,17},{9,25},{17,1},{25,9},{2,18},{10... | collective-permute-start | bytes 884744 | tf_op jit(solution)/shard_map/ppermute | solution.py:881
  39.9 17.8 %collective-permute-start.6 = (bf16[144,1024]{1,0:T(8,128)(2,1)S(1)}, bf16[144,1024]{1,0:T(8,128)(2,1)S(1)}, u32[]{:S(2)}, u32[]{:S(2)}) collective-permute-start(bf16[144,1024]{1,0:T(8,128)(2,1)S(1)} %copy-done.71), channel_id=1, source_target_pairs={{0,24},{8,0},{16,8},{24,16},{1,25},{9,1},{17,9},{25,17},{2,26},{10... | collective-permute-start | bytes 884744 | tf_op jit(solution)/shard_map/ppermute | solution.py:881
  59.1 10.3 %collective-permute-start.8 = (bf16[512,1024]{1,0:T(8,128)(2,1)S(1)}, bf16[512,1024]{1,0:T(8,128)(2,1)S(1)}, u32[]{:S(2)}, u32[]{:S(2)}) collective-permute-start(bf16[512,1024]{1,0:T(8,128)(2,1)S(1)} %first.1.refs_0_), channel_id=1, source_target_pairs={{0,1},{1,0},{2,3},{3,2},{4,5},{5,4},{6,7},{7,6},{8,9},{9,8},{10,11... | collective-permute-start | bytes 3145736 | tf_op jit(solution)/shard_map/ppermute | solution.py:881
  59.2 11.4 %collective-permute-start.9 = (bf16[512,1024]{1,0:T(8,128)(2,1)S(1)}, bf16[512,1024]{1,0:T(8,128)(2,1)S(1)}, u32[]{:S(2)}, u32[]{:S(2)}) collective-permute-start(bf16[512,1024]{1,0:T(8,128)(2,1)S(1)} %collective-permute-done.7.refs_1_), channel_id=1, source_target_pairs={{0,1},{1,0},{2,3},{3,2},{4,5},{5,4},{6,7},{7,6},{8,9},{9,8},{10,11... | collective-permute-start | bytes 3145736 | tf_op jit(solution)/shard_map/ppermute | solution.py:881
  59.7 28.3 %collective-permute-start.10 = (bf16[528,1024]{1,0:T(8,128)(2,1)S(1)}, bf16[528,1024]{1,0:T(8,128)(2,1)S(1)}, u32[]{:S(2)}, u32[]{:S(2)}) collective-permute-start(bf16[528,1024]{1,0:T(8,128)(2,1)S(1)} %stack_z.4.refs_0_), channel_id=1, source_target_pairs={{0,4},{4,0},{1,5},{5,1},{2,6},{6,2},{3,7},{7,3},{8,12},{12,8},{9,1... | collective-permute-start | bytes 3244040 | tf_op jit(solution)/shard_map/ppermute | solution.py:881
  60.2 27.7 %collective-permute-start.11 = (bf16[128,1024]{1,0:T(8,128)(2,1)S(1)}, bf16[128,1024]{1,0:T(8,128)(2,1)S(1)}, u32[]{:S(2)}, u32[]{:S(2)}) collective-permute-start(bf16[128,1024]{1,0:T(8,128)(2,1)S(1)} %copy-done.73), channel_id=1, source_target_pairs={{0,8},{8,16},{16,24},{24,0},{1,9},{9,17},{17,25},{25,1},{2,10},{10... | collective-permute-start | bytes 786440 | tf_op jit(solution)/shard_map/ppermute | solution.py:881
  67.0 20.9 %collective-permute-start.12 = (bf16[128,1024]{1,0:T(8,128)(2,1)S(1)}, bf16[128,1024]{1,0:T(8,128)(2,1)S(1)}, u32[]{:S(2)}, u32[]{:S(2)}) collective-permute-start(bf16[128,1024]{1,0:T(8,128)(2,1)S(1)} %copy-done.73), channel_id=1, source_target_pairs={{0,16},{8,24},{16,0},{24,8},{1,17},{9,25},{17,1},{25,9},{2,18},{10... | collective-permute-start | bytes 786440 | tf_op jit(solution)/shard_map/ppermute | solution.py:881
  69.3 18.6 %collective-permute-start.13 = (bf16[128,1024]{1,0:T(8,128)(2,1)S(1)}, bf16[128,1024]{1,0:T(8,128)(2,1)S(1)}, u32[]{:S(2)}, u32[]{:S(2)}) collective-permute-start(bf16[128,1024]{1,0:T(8,128)(2,1)S(1)} %copy-done.73), channel_id=1, source_target_pairs={{0,24},{8,0},{16,8},{24,16},{1,25},{9,1},{17,9},{25,17},{2,26},{10... | collective-permute-start | bytes 786440 | tf_op jit(solution)/shard_map/ppermute | solution.py:881
  70.5 17.4 %collective-permute-start.14 = (bf16[1024,256]{1,0:T(8,128)(2,1)S(1)}, bf16[1024,256]{1,0:T(8,128)(2,1)S(1)}, u32[]{:S(2)}, u32[]{:S(2)}) collective-permute-start(bf16[1024,256]{1,0:T(8,128)(2,1)S(1)} %get-tuple-element.323.refs_0_), channel_id=1, source_target_pairs={{0,2},{2,0},{1,3},{3,1},{4,6},{6,4},{5,7},{7,5},{8,10},{10,8},{9,1... | collective-permute-start | bytes 1572872 | tf_op jit(solution)/shard_map/ppermute | solution.py:881
  75.5 155.9 %copy-start = (bf16[2048,768]{1,0:T(8,128)(2,1)}, bf16[2048,768]{1,0:T(8,128)(2,1)S(1)}, u32[]{:S(2)}) copy-start(bf16[2048,768]{1,0:T(8,128)(2,1)S(1)} %convolution_convert_fusion.refs_0_.refs_1_.refs_2_.refs_3_.refs_4_.refs_5_) | copy-start | bytes 9437188
  87.9 143.6 %copy-start.74 = (f32[3,8,640]{2,1,0:T(8,128)}, f32[3,8,640]{2,1,0:T(8,128)S(1)}, u32[]{:S(2)}) copy-start(f32[3,8,640]{2,1,0:T(8,128)S(1)} %get-tuple-element.311.bias_ref) | copy-start | bytes 184324
  88.0 15.2 %collective-permute-start.18 = (bf16[1024,512]{1,0:T(8,128)(2,1)S(1)}, bf16[1024,512]{1,0:T(8,128)(2,1)S(1)}, u32[]{:S(2)}, u32[]{:S(2)}) collective-permute-start(bf16[1024,512]{1,0:T(8,128)(2,1)S(1)} %beside.1.refs_4_.refs_0_), channel_id=1, source_target_pairs={{0,1},{1,0},{2,3},{3,2},{4,5},{5,4},{6,7},{7,6},{8,9},{9,8},{10,11... | collective-permute-start | bytes 3145736 | tf_op jit(solution)/shard_map/ppermute | solution.py:881
  88.8 14.4 %collective-permute-start.19 = (bf16[256,1024]{1,0:T(8,128)(2,1)S(1)}, bf16[256,1024]{1,0:T(8,128)(2,1)S(1)}, u32[]{:S(2)}, u32[]{:S(2)}) collective-permute-start(bf16[256,1024]{1,0:T(8,128)(2,1)S(1)} %get-tuple-element.359.refs_0_), channel_id=1, source_target_pairs={{0,4},{4,0},{1,5},{5,1},{2,6},{6,2},{3,7},{7,3},{8,12},{12,8},{9,1... | collective-permute-start | bytes 1572872 | tf_op jit(solution)/shard_map/ppermute | solution.py:881
  89.4 9.1 %collective-permute-start.15 = (bf16[512,256]{1,0:T(8,128)(2,1)S(1)}, bf16[512,256]{1,0:T(8,128)(2,1)S(1)}, u32[]{:S(2)}, u32[]{:S(2)}) collective-permute-start(bf16[512,256]{1,0:T(8,128)(2,1)S(1)} %get-tuple-element.320), channel_id=1, source_target_pairs={{0,2},{1,3},{2,0},{3,1},{4,6},{5,7},{6,4},{7,5},{8,10},{9,11},{10,... | collective-permute-start | bytes 786440 | tf_op jit(solution)/shard_map/ppermute | solution.py:889
  90.9 7.6 %collective-permute-start.16 = (bf16[512,256]{1,0:T(8,128)(2,1)S(1)}, bf16[512,256]{1,0:T(8,128)(2,1)S(1)}, u32[]{:S(2)}, u32[]{:S(2)}) collective-permute-start(bf16[512,256]{1,0:T(8,128)(2,1)S(1)} %get-tuple-element.321), channel_id=1, source_target_pairs={{0,1},{1,0},{2,3},{3,2},{4,5},{5,4},{6,7},{7,6},{8,9},{9,8},{10,11... | collective-permute-start | bytes 786440 | tf_op jit(solution)/shard_map/ppermute | solution.py:889
  90.9 11.8 %collective-permute-start.17 = (bf16[512,256]{1,0:T(8,128)(2,1)S(1)}, bf16[512,256]{1,0:T(8,128)(2,1)S(1)}, u32[]{:S(2)}, u32[]{:S(2)}) collective-permute-start(bf16[512,256]{1,0:T(8,128)(2,1)S(1)} %get-tuple-element.322), channel_id=1, source_target_pairs={{0,3},{1,2},{2,1},{3,0},{4,7},{5,6},{6,5},{7,4},{8,11},{9,10},{10,... | collective-permute-start | bytes 786440 | tf_op jit(solution)/shard_map/ppermute | solution.py:889
  103.2 4.2 %collective-permute-start.20 = (bf16[1024,1024]{1,0:T(8,128)(2,1)S(1)}, bf16[1024,1024]{1,0:T(8,128)(2,1)S(1)}, u32[]{:S(2)}, u32[]{:S(2)}) collective-permute-start(bf16[1024,1024]{1,0:T(8,128)(2,1)S(1)} %weave.4.refs_0_.refs_2_), channel_id=1, source_target_pairs={{0,1},{1,0},{2,3},{3,2},{4,5},{5,4},{6,7},{7,6},{8,9},{9,8},{10,11... | collective-permute-start | bytes 6291464 | tf_op jit(solution)/shard_map/ppermute | solution.py:881
  103.4 14.5 %collective-permute-start.22 = (bf16[256,1024]{1,0:T(8,128)(2,1)S(1)}, bf16[256,1024]{1,0:T(8,128)(2,1)S(1)}, u32[]{:S(2)}, u32[]{:S(2)}) collective-permute-start(bf16[256,1024]{1,0:T(8,128)(2,1)S(1)} %get-tuple-element.360.refs_1_), channel_id=1, source_target_pairs={{0,4},{4,0},{1,5},{5,1},{2,6},{6,2},{3,7},{7,3},{8,12},{12,8},{9,1... | collective-permute-start | bytes 1572872 | tf_op jit(solution)/shard_map/ppermute | solution.py:881
  107.4 14.1 %collective-permute-start.21 = (bf16[256,1024]{1,0:T(8,128)(2,1)S(1)}, bf16[256,1024]{1,0:T(8,128)(2,1)S(1)}, u32[]{:S(2)}, u32[]{:S(2)}) collective-permute-start(bf16[256,1024]{1,0:T(8,128)(2,1)S(1)} %slice.60), channel_id=1, source_target_pairs={{0,2},{2,0},{1,3},{3,1},{4,6},{6,4},{5,7},{7,5},{8,10},{10,8},{9,1... | collective-permute-start | bytes 1572872 | tf_op jit(solution)/shard_map/ppermute | solution.py:881
  122.2 6.8 %collective-permute-start.23 = (bf16[1024,1024]{1,0:T(8,128)(2,1)S(1)}, bf16[1024,1024]{1,0:T(8,128)(2,1)S(1)}, u32[]{:S(2)}, u32[]{:S(2)}) collective-permute-start(bf16[1024,1024]{1,0:T(8,128)(2,1)S(1)} %weave.5.refs_2_), channel_id=1, source_target_pairs={{0,1},{1,0},{2,3},{3,2},{4,5},{5,4},{6,7},{7,6},{8,9},{9,8},{10,11... | collective-permute-start | bytes 6291464 | tf_op jit(solution)/shard_map/ppermute | solution.py:881
  122.3 14.4 %collective-permute-start.24 = (bf16[256,1024]{1,0:T(8,128)(2,1)S(1)}, bf16[256,1024]{1,0:T(8,128)(2,1)S(1)}, u32[]{:S(2)}, u32[]{:S(2)}) collective-permute-start(bf16[256,1024]{1,0:T(8,128)(2,1)S(1)} %slice.61), channel_id=1, source_target_pairs={{0,2},{2,0},{1,3},{3,1},{4,6},{6,4},{5,7},{7,5},{8,10},{10,8},{9,1... | collective-permute-start | bytes 1572872 | tf_op jit(solution)/shard_map/ppermute | solution.py:881
  136.7 20.7 %collective-permute-start.25 = (bf16[256,1024]{1,0:T(8,128)(2,1)}, bf16[256,1024]{1,0:T(8,128)(2,1)}, u32[]{:S(2)}, u32[]{:S(2)}) collective-permute-start(bf16[256,1024]{1,0:T(8,128)(2,1)} %wide.6), channel_id=1, source_target_pairs={{0,2},{2,0},{1,3},{3,1},{4,6},{6,4},{5,7},{7,5},{8,10},{10,8},{9,1... | collective-permute-start | bytes 1572872 | tf_op jit(solution)/shard_map/ppermute | solution.py:881
  147.2 14.6 %collective-permute-start.26 = (bf16[256,1024]{1,0:T(8,128)(2,1)}, bf16[256,1024]{1,0:T(8,128)(2,1)}, u32[]{:S(2)}, u32[]{:S(2)}) collective-permute-start(bf16[256,1024]{1,0:T(8,128)(2,1)} %wide.7), channel_id=1, source_target_pairs={{0,2},{2,0},{1,3},{3,1},{4,6},{6,4},{5,7},{7,5},{8,10},{10,8},{9,1... | collective-permute-start | bytes 1572872 | tf_op jit(solution)/shard_map/ppermute | solution.py:881
  164.4 13.1 %collective-permute-start.27 = (bf16[256,1024]{1,0:T(8,128)(2,1)S(1)}, bf16[256,1024]{1,0:T(8,128)(2,1)S(1)}, u32[]{:S(2)}, u32[]{:S(2)}) collective-permute-start(bf16[256,1024]{1,0:T(8,128)(2,1)S(1)} %slice.62), channel_id=1, source_target_pairs={{0,2},{2,0},{1,3},{3,1},{4,6},{6,4},{5,7},{7,5},{8,10},{10,8},{9,1... | collective-permute-start | bytes 1572872 | tf_op jit(solution)/shard_map/ppermute | solution.py:881
  177.5 12.2 %collective-permute-start.28 = (bf16[256,1024]{1,0:T(8,128)(2,1)S(1)}, bf16[256,1024]{1,0:T(8,128)(2,1)S(1)}, u32[]{:S(2)}, u32[]{:S(2)}) collective-permute-start(bf16[256,1024]{1,0:T(8,128)(2,1)S(1)} %slice.63), channel_id=1, source_target_pairs={{0,2},{2,0},{1,3},{3,1},{4,6},{6,4},{5,7},{7,5},{8,10},{10,8},{9,1... | collective-permute-start | bytes 1572872 | tf_op jit(solution)/shard_map/ppermute | solution.py:881
  189.7 11.2 %collective-permute-start.29 = (bf16[256,1024]{1,0:T(8,128)(2,1)S(1)}, bf16[256,1024]{1,0:T(8,128)(2,1)S(1)}, u32[]{:S(2)}, u32[]{:S(2)}) collective-permute-start(bf16[256,1024]{1,0:T(8,128)(2,1)S(1)} %wide.10), channel_id=1, source_target_pairs={{0,2},{2,0},{1,3},{3,1},{4,6},{6,4},{5,7},{7,5},{8,10},{10,8},{9,1... | collective-permute-start | bytes 1572872 | tf_op jit(solution)/shard_map/ppermute | solution.py:881
  200.9 4.2 %collective-permute-start.31 = (bf16[1024,1024]{1,0:T(8,128)(2,1)S(1)}, bf16[1024,1024]{1,0:T(8,128)(2,1)S(1)}, u32[]{:S(2)}, u32[]{:S(2)}) collective-permute-start(bf16[1024,1024]{1,0:T(8,128)(2,1)S(1)} %convolution_convert_fusion.2), channel_id=1, source_target_pairs={{0,1},{1,0},{2,3},{3,2},{4,5},{5,4},{6,7},{7,6},{8,9},{9,8},{10,11... | collective-permute-start | bytes 6291464 | tf_op jit(solution)/shard_map/ppermute | solution.py:881
  203.4 4.7 %collective-permute-start.32 = (bf16[1024,1024]{1,0:T(8,128)(2,1)S(1)}, bf16[1024,1024]{1,0:T(8,128)(2,1)S(1)}, u32[]{:S(2)}, u32[]{:S(2)}) collective-permute-start(bf16[1024,1024]{1,0:T(8,128)(2,1)S(1)} %convolution_convert_fusion.1), channel_id=1, source_target_pairs={{0,1},{1,0},{2,3},{3,2},{4,5},{5,4},{6,7},{7,6},{8,9},{9,8},{10,11... | collective-permute-start | bytes 6291464 | tf_op jit(solution)/shard_map/ppermute | solution.py:881
  204.0 13.9 %collective-permute-start.30 = (bf16[256,1024]{1,0:T(8,128)(2,1)S(1)}, bf16[256,1024]{1,0:T(8,128)(2,1)S(1)}, u32[]{:S(2)}, u32[]{:S(2)}) collective-permute-start(bf16[256,1024]{1,0:T(8,128)(2,1)S(1)} %wide.11), channel_id=1, source_target_pairs={{0,2},{2,0},{1,3},{3,1},{4,6},{6,4},{5,7},{7,5},{8,10},{10,8},{9,1... | collective-permute-start | bytes 1572872 | tf_op jit(solution)/shard_map/ppermute | solution.py:881
  221.4 6.3 %collective-permute-start.33 = (bf16[512,128]{1,0:T(8,128)(2,1)S(1)}, bf16[512,128]{1,0:T(8,128)(2,1)S(1)}, u32[]{:S(2)}, u32[]{:S(2)}) collective-permute-start(bf16[512,128]{1,0:T(8,128)(2,1)S(1)} %get-tuple-element.430), channel_id=1, source_target_pairs={{0,2},{1,3},{2,0},{3,1},{4,6},{5,7},{6,4},{7,5},{8,10},{9,11},{10,... | collective-permute-start | bytes 393224 | tf_op jit(solution)/shard_map/ppermute | solution.py:889
  222.1 5.5 %collective-permute-start.34 = (bf16[512,128]{1,0:T(8,128)(2,1)S(1)}, bf16[512,128]{1,0:T(8,128)(2,1)S(1)}, u32[]{:S(2)}, u32[]{:S(2)}) collective-permute-start(bf16[512,128]{1,0:T(8,128)(2,1)S(1)} %get-tuple-element.431), channel_id=1, source_target_pairs={{0,1},{1,0},{2,3},{3,2},{4,5},{5,4},{6,7},{7,6},{8,9},{9,8},{10,11... | collective-permute-start | bytes 393224 | tf_op jit(solution)/shard_map/ppermute | solution.py:889
  222.1 5.8 %collective-permute-start.35 = (bf16[512,128]{1,0:T(8,128)(2,1)S(1)}, bf16[512,128]{1,0:T(8,128)(2,1)S(1)}, u32[]{:S(2)}, u32[]{:S(2)}) collective-permute-start(bf16[512,128]{1,0:T(8,128)(2,1)S(1)} %get-tuple-element.432), channel_id=1, source_target_pairs={{0,3},{1,2},{2,1},{3,0},{4,7},{5,6},{6,5},{7,4},{8,11},{9,10},{10,... | collective-permute-start | bytes 393224 | tf_op jit(solution)/shard_map/ppermute | solution.py:889
  224.9 25.1 %collective-permute-start.40 = (bf16[512,1024]{1,0:T(8,128)(2,1)S(1)}, bf16[512,1024]{1,0:T(8,128)(2,1)S(1)}, u32[]{:S(2)}, u32[]{:S(2)}) collective-permute-start(bf16[512,1024]{1,0:T(8,128)(2,1)S(1)} %get-tuple-element.447), channel_id=1, source_target_pairs={{0,4},{4,0},{1,5},{5,1},{2,6},{6,2},{3,7},{7,3},{8,12},{12,8},{9,1... | collective-permute-start | bytes 3145736 | tf_op jit(solution)/shard_map/ppermute | solution.py:881
  227.9 22.1 %collective-permute-start.39 = (bf16[1024,512]{1,0:T(8,128)(2,1)S(1)}, bf16[1024,512]{1,0:T(8,128)(2,1)S(1)}, u32[]{:S(2)}, u32[]{:S(2)}) collective-permute-start(bf16[1024,512]{1,0:T(8,128)(2,1)S(1)} %get-tuple-element.445), channel_id=1, source_target_pairs={{0,1},{1,0},{2,3},{3,2},{4,5},{5,4},{6,7},{7,6},{8,9},{9,8},{10,11... | collective-permute-start | bytes 3145736 | tf_op jit(solution)/shard_map/ppermute | solution.py:881
  229.3 17.2 %collective-permute-start.36 = (bf16[512,128]{1,0:T(8,128)(2,1)S(1)}, bf16[512,128]{1,0:T(8,128)(2,1)S(1)}, u32[]{:S(2)}, u32[]{:S(2)}) collective-permute-start(bf16[512,128]{1,0:T(8,128)(2,1)S(1)} %get-tuple-element.442), channel_id=1, source_target_pairs={{0,2},{1,3},{2,0},{3,1},{4,6},{5,7},{6,4},{7,5},{8,10},{9,11},{10,... | collective-permute-start | bytes 393224 | tf_op jit(solution)/shard_map/ppermute | solution.py:889
  230.0 16.5 %collective-permute-start.37 = (bf16[512,128]{1,0:T(8,128)(2,1)S(1)}, bf16[512,128]{1,0:T(8,128)(2,1)S(1)}, u32[]{:S(2)}, u32[]{:S(2)}) collective-permute-start(bf16[512,128]{1,0:T(8,128)(2,1)S(1)} %get-tuple-element.443), channel_id=1, source_target_pairs={{0,1},{1,0},{2,3},{3,2},{4,5},{5,4},{6,7},{7,6},{8,9},{9,8},{10,11... | collective-permute-start | bytes 393224 | tf_op jit(solution)/shard_map/ppermute | solution.py:889
  230.0 16.5 %collective-permute-start.38 = (bf16[512,128]{1,0:T(8,128)(2,1)S(1)}, bf16[512,128]{1,0:T(8,128)(2,1)S(1)}, u32[]{:S(2)}, u32[]{:S(2)}) collective-permute-start(bf16[512,128]{1,0:T(8,128)(2,1)S(1)} %get-tuple-element.444), channel_id=1, source_target_pairs={{0,3},{1,2},{2,1},{3,0},{4,7},{5,6},{6,5},{7,4},{8,11},{9,10},{10,... | collective-permute-start | bytes 393224 | tf_op jit(solution)/shard_map/ppermute | solution.py:889
  254.1 25.0 %collective-permute-start.41 = (bf16[512,1024]{1,0:T(8,128)(2,1)}, bf16[512,1024]{1,0:T(8,128)(2,1)S(1)}, u32[]{:S(2)}, u32[]{:S(2)}) collective-permute-start(bf16[512,1024]{1,0:T(8,128)(2,1)} %get-tuple-element.471), channel_id=1, source_target_pairs={{0,4},{4,0},{1,5},{5,1},{2,6},{6,2},{3,7},{7,3},{8,12},{12,8},{9,1... | collective-permute-start | bytes 3145736 | tf_op jit(solution)/shard_map/ppermute | solution.py:881
  255.6 23.6 %collective-permute-start.45 = (bf16[1024,256]{1,0:T(8,128)(2,1)}, bf16[1024,256]{1,0:T(8,128)(2,1)}, u32[]{:S(2)}, u32[]{:S(2)}) collective-permute-start(bf16[1024,256]{1,0:T(8,128)(2,1)} %get-tuple-element.477), channel_id=1, source_target_pairs={{0,2},{2,0},{1,3},{3,1},{4,6},{6,4},{5,7},{7,5},{8,10},{10,8},{9,1... | collective-permute-start | bytes 1572872 | tf_op jit(solution)/shard_map/ppermute | solution.py:881
  256.3 22.8 %collective-permute-start.42 = (bf16[128,1024]{1,0:T(8,128)(2,1)}, bf16[128,1024]{1,0:T(8,128)(2,1)}, u32[]{:S(2)}, u32[]{:S(2)}) collective-permute-start(bf16[128,1024]{1,0:T(8,128)(2,1)} %get-tuple-element.473), channel_id=1, source_target_pairs={{0,8},{8,16},{16,24},{24,0},{1,9},{9,17},{17,25},{25,1},{2,10},{10... | collective-permute-start | bytes 786440 | tf_op jit(solution)/shard_map/ppermute | solution.py:881
  260.7 18.4 %collective-permute-start.43 = (bf16[128,1024]{1,0:T(8,128)(2,1)}, bf16[128,1024]{1,0:T(8,128)(2,1)}, u32[]{:S(2)}, u32[]{:S(2)}) collective-permute-start(bf16[128,1024]{1,0:T(8,128)(2,1)} %get-tuple-element.474), channel_id=1, source_target_pairs={{0,16},{8,24},{16,0},{24,8},{1,17},{9,25},{17,1},{25,9},{2,18},{10... | collective-permute-start | bytes 786440 | tf_op jit(solution)/shard_map/ppermute | solution.py:881
  262.8 16.4 %collective-permute-start.44 = (bf16[128,1024]{1,0:T(8,128)(2,1)}, bf16[128,1024]{1,0:T(8,128)(2,1)}, u32[]{:S(2)}, u32[]{:S(2)}) collective-permute-start(bf16[128,1024]{1,0:T(8,128)(2,1)} %get-tuple-element.475), channel_id=1, source_target_pairs={{0,24},{8,0},{16,8},{24,16},{1,25},{9,1},{17,9},{25,17},{2,26},{10... | collective-permute-start | bytes 786440 | tf_op jit(solution)/shard_map/ppermute | solution.py:881
  285.6 5.1 %collective-permute-start.46 = (bf16[1024,1024]{1,0:T(8,128)(2,1)S(1)}, bf16[1024,1024]{1,0:T(8,128)(2,1)S(1)}, u32[]{:S(2)}, u32[]{:S(2)}) collective-permute-start(bf16[1024,1024]{1,0:T(8,128)(2,1)S(1)} %get-tuple-element.485), channel_id=1, source_target_pairs={{0,1},{1,0},{2,3},{3,2},{4,5},{5,4},{6,7},{7,6},{8,9},{9,8},{10,11... | collective-permute-start | bytes 6291464 | tf_op jit(solution)/shard_map/ppermute | solution.py:881
  291.7 26.3 %collective-permute-start.47 = (bf16[512,1024]{1,0:T(8,128)(2,1)S(1)}, bf16[512,1024]{1,0:T(8,128)(2,1)S(1)}, u32[]{:S(2)}, u32[]{:S(2)}) collective-permute-start(bf16[512,1024]{1,0:T(8,128)(2,1)S(1)} %get-tuple-element.502), channel_id=1, source_target_pairs={{0,4},{4,0},{1,5},{5,1},{2,6},{6,2},{3,7},{7,3},{8,12},{12,8},{9,1... | collective-permute-start | bytes 3145736 | tf_op jit(solution)/shard_map/ppermute | solution.py:881
  293.2 25.3 %collective-permute-start.48 = (bf16[512,1024]{1,0:T(8,128)(2,1)S(1)}, bf16[512,1024]{1,0:T(8,128)(2,1)S(1)}, u32[]{:S(2)}, u32[]{:S(2)}) collective-permute-start(bf16[512,1024]{1,0:T(8,128)(2,1)S(1)} %get-tuple-element.503), channel_id=1, source_target_pairs={{0,2},{2,0},{1,3},{3,1},{4,6},{6,4},{5,7},{7,5},{8,10},{10,8},{9,1... | collective-permute-start | bytes 3145736 | tf_op jit(solution)/shard_map/ppermute | solution.py:881
  293.9 13.5 %collective-permute-start.49 = (bf16[128,1024]{1,0:T(8,128)(2,1)S(1)}, bf16[128,1024]{1,0:T(8,128)(2,1)S(1)}, u32[]{:S(2)}, u32[]{:S(2)}) collective-permute-start(bf16[128,1024]{1,0:T(8,128)(2,1)S(1)} %get-tuple-element.505), channel_id=1, source_target_pairs={{0,8},{8,16},{16,24},{24,0},{1,9},{9,17},{17,25},{25,1},{2,10},{10... | collective-permute-start | bytes 786440 | tf_op jit(solution)/shard_map/ppermute | solution.py:881
  299.1 18.9 %collective-permute-start.50 = (bf16[128,1024]{1,0:T(8,128)(2,1)S(1)}, bf16[128,1024]{1,0:T(8,128)(2,1)S(1)}, u32[]{:S(2)}, u32[]{:S(2)}) collective-permute-start(bf16[128,1024]{1,0:T(8,128)(2,1)S(1)} %get-tuple-element.506), channel_id=1, source_target_pairs={{0,16},{8,24},{16,0},{24,8},{1,17},{9,25},{17,1},{25,9},{2,18},{10... | collective-permute-start | bytes 786440 | tf_op jit(solution)/shard_map/ppermute | solution.py:881
  300.7 17.2 %collective-permute-start.51 = (bf16[128,1024]{1,0:T(8,128)(2,1)S(1)}, bf16[128,1024]{1,0:T(8,128)(2,1)S(1)}, u32[]{:S(2)}, u32[]{:S(2)}) collective-permute-start(bf16[128,1024]{1,0:T(8,128)(2,1)S(1)} %get-tuple-element.507), channel_id=1, source_target_pairs={{0,24},{8,0},{16,8},{24,16},{1,25},{9,1},{17,9},{25,17},{2,26},{10... | collective-permute-start | bytes 786440 | tf_op jit(solution)/shard_map/ppermute | solution.py:881
  322.5 30.2 %collective-permute-start.57 = (bf16[128,1024]{1,0:T(8,128)(2,1)S(1)}, bf16[128,1024]{1,0:T(8,128)(2,1)S(1)}, u32[]{:S(2)}, u32[]{:S(2)}) collective-permute-start(bf16[128,1024]{1,0:T(8,128)(2,1)S(1)} %get-tuple-element.529), channel_id=1, source_target_pairs={{0,8},{8,16},{16,24},{24,0},{1,9},{9,17},{17,25},{25,1},{2,10},{10... | collective-permute-start | bytes 786440 | tf_op jit(solution)/shard_map/ppermute | solution.py:881
  328.1 24.5 %collective-permute-start.58 = (bf16[128,1024]{1,0:T(8,128)(2,1)S(1)}, bf16[128,1024]{1,0:T(8,128)(2,1)S(1)}, u32[]{:S(2)}, u32[]{:S(2)}) collective-permute-start(bf16[128,1024]{1,0:T(8,128)(2,1)S(1)} %get-tuple-element.530), channel_id=1, source_target_pairs={{0,16},{8,24},{16,0},{24,8},{1,17},{9,25},{17,1},{25,9},{2,18},{10... | collective-permute-start | bytes 786440 | tf_op jit(solution)/shard_map/ppermute | solution.py:881
  329.3 23.3 %collective-permute-start.59 = (bf16[128,1024]{1,0:T(8,128)(2,1)S(1)}, bf16[128,1024]{1,0:T(8,128)(2,1)S(1)}, u32[]{:S(2)}, u32[]{:S(2)}) collective-permute-start(bf16[128,1024]{1,0:T(8,128)(2,1)S(1)} %get-tuple-element.531), channel_id=1, source_target_pairs={{0,24},{8,0},{16,8},{24,16},{1,25},{9,1},{17,9},{25,17},{2,26},{10... | collective-permute-start | bytes 786440 | tf_op jit(solution)/shard_map/ppermute | solution.py:881
  330.5 1.2 collective-permute-start.52
  331.7 3.9 %collective-permute-start.53 = (f32[8,1024]{1,0:T(8,128)S(1)}, f32[8,1024]{1,0:T(8,128)S(1)}, u32[]{:S(2)}, u32[]{:S(2)}) collective-permute-start(f32[8,1024]{1,0:T(8,128)S(1)} %add.188), channel_id=1, source_target_pairs={{0,2},{2,0},{1,3},{3,1},{4,6},{6,4},{5,7},{7,5},{8,10},{10,8},{9,1... | collective-permute-start | bytes 98312 | tf_op jit(solution)/shard_map/ppermute | solution.py:1214
  335.7 3.9 %collective-permute-start.54 = (f32[8,1024]{1,0:T(8,128)S(1)}, f32[8,1024]{1,0:T(8,128)S(1)}, u32[]{:S(2)}, u32[]{:S(2)}) collective-permute-start(f32[8,1024]{1,0:T(8,128)S(1)} %add.189), channel_id=1, source_target_pairs={{0,4},{4,0},{1,5},{5,1},{2,6},{6,2},{3,7},{7,3},{8,12},{12,8},{9,1... | collective-permute-start | bytes 98312 | tf_op jit(solution)/shard_map/ppermute | solution.py:1214
  339.6 7.0 %collective-permute-start.55 = (f32[8,1024]{1,0:T(8,128)S(1)}, f32[8,1024]{1,0:T(8,128)S(1)}, u32[]{:S(2)}, u32[]{:S(2)}) collective-permute-start(f32[8,1024]{1,0:T(8,128)S(1)} %add.190), channel_id=1, source_target_pairs={{0,8},{8,0},{16,24},{24,16},{1,9},{9,1},{17,25},{25,17},{2,10},{10... | collective-permute-start | bytes 98312 | tf_op jit(solution)/shard_map/ppermute | solution.py:1214
  346.6 6.0 %collective-permute-start.56 = (f32[8,1024]{1,0:T(8,128)S(1)}, f32[8,1024]{1,0:T(8,128)S(1)}, u32[]{:S(2)}, u32[]{:S(2)}) collective-permute-start(f32[8,1024]{1,0:T(8,128)S(1)} %add.191), channel_id=1, source_target_pairs={{0,16},{8,24},{16,0},{24,8},{1,17},{9,25},{17,1},{25,9},{2,18},{10... | collective-permute-start | bytes 98312 | tf_op jit(solution)/shard_map/ppermute | solution.py:1214
  (83 other events, 947.4 us)
